TPU v7x, 128 devices: a whole 4x4x4 slice. The times are simulated.
128 devices in a mesh: dp: 4 (over x), ctx: 32 (over z, y, core).
Axes of the slice: x: 4, y: 4, z: 4, core: 2. Of those that a mesh axis runs over, the one named last changes fastest.
Arguments:
- mixer_input: bfloat16 [4, 4096, 10240], P('dp', 'ctx'), may hold values from -6 to 6
- step_raw: bfloat16 [4, 4096, 128], P('dp', 'ctx'), as said below
- out_grad: bfloat16 [4, 4096, 8192], P('dp', 'ctx'), may hold values from -0.59765625 to 0.59765625
- conv_weight: float32 [4, 10240], replicated, may hold values from -3 to 3
- conv_bias: float32 [10240], replicated, may hold values from -3 to 3
- step_bias: float32 [128], replicated, may hold values from -4 to -3
- decay_log: float32 [128], replicated, as said below
- skip_gain: float32 [128], replicated, may hold values from 0.5 to 1.5
Outputs:
- input_grad: bfloat16 [4, 4096, 10240], P('dp', 'ctx')
- step_grad: float32 [4, 4096, 128], P('dp', 'ctx')
- conv_grads: float32 [5, 10240], P(None, 'dp')
- head_grads: float32 [2, 128], P(None, 'dp')
- gain_grad: float32 [128], P('dp')
Inputs may be any that keep to these rules, and one draw needn't show every extreme that they name: `step_raw`: raw step sizes of one device's positions share a per-head offset. `decay_log`: log magnitudes of the decay rates.
All inputs are finite; a program needn't handle non-finite values.
Results may differ from a plain program's by a relative error of at most 0.018.
Values may be sent and summed in bfloat16 or wider, within the bound.
A program may use at most 448 MiB of HBM per device.

v0:
```python
import math

import jax
import jax.numpy as jnp
from jax import lax
from jax.sharding import PartitionSpec as P

HEAD_DIM = 64
STATE = 128
GROUPS = 8
KERNEL = 4
BLOCK = 128


FULL_PRECISION = lax.Precision.HIGHEST


def passed_along(value, axis, steps):
    count = lax.axis_size(axis)
    initial, last = (max(0, -steps), min(count, count - steps))
    return lax.ppermute(value, axis, [(source, source + steps) for source in range(initial, last)])


def causal_conv(padded, conv_weight, conv_bias):
    kernel_len = conv_weight.shape[0]
    seq_len = padded.shape[0] - kernel_len + 1
    summed = jnp.broadcast_to(conv_bias[None, :], (seq_len, padded.shape[1]))
    for offset in range(kernel_len):
        summed = summed + conv_weight[offset][None, :] * padded[offset : offset + seq_len]
    return jax.nn.silu(summed)


def ssd_core(x_rows, b_rows, c_rows, spread, rates, block_len):
    seq_len, block_count, block_heads, head_dim = x_rows.shape
    state_dim = b_rows.shape[2]
    part_count = seq_len // block_len
    x_parts = x_rows.reshape(part_count, block_len, block_count, block_heads, head_dim)
    b_parts = b_rows.reshape(part_count, block_len, block_count, state_dim)
    c_parts = c_rows.reshape(part_count, block_len, block_count, state_dim)
    step_parts = spread.reshape(part_count, block_len, block_count, block_heads)
    running = jnp.cumsum(step_parts * rates, axis=1)
    causal = jnp.arange(block_len)[:, None] >= jnp.arange(block_len)[None, :]
    gaps = running[:, :, None] - running[:, None, :]
    decays = jnp.exp(jnp.where(causal[None, :, :, None, None], gaps, -1e30))
    scores = jnp.einsum("ctgn,csgn->ctsg", c_parts, b_parts, precision=FULL_PRECISION)
    weights = decays * scores[..., None] * step_parts[:, None]
    result = jnp.einsum("ctsgk,csgkp->ctgkp", weights, x_parts, precision=FULL_PRECISION)
    closing = running[:, -1]
    to_close = jnp.exp(closing[:, None] - running) * step_parts
    states = jnp.einsum(
        "csgn,csgkp->cgknp", b_parts, x_parts * to_close[..., None], precision=FULL_PRECISION
    )
    after = jnp.cumsum(closing, axis=0)
    before = after - closing
    strict = jnp.arange(part_count)[:, None] > jnp.arange(part_count)[None, :]
    spans = before[:, None] - after[None, :]
    passing = jnp.exp(jnp.where(strict[:, :, None, None], spans, -1e30))
    entering = jnp.einsum("cdgk,dgknp->cgknp", passing, states, precision=FULL_PRECISION)
    result = (
        result
        + jnp.einsum("ctgn,cgknp->ctgkp", c_parts, entering, precision=FULL_PRECISION)
        * jnp.exp(running)[..., None]
    )
    final_state = entering[-1] * jnp.exp(closing[-1])[..., None, None] + states[-1]
    return (result.reshape(seq_len, block_count, block_heads, head_dim), final_state, after[-1])


def head_block(pieces):
    x_block, b_block, c_block, spread_block, rate_block, gain_block, grad_block = pieces

    def one_head(items):
        x_head, spread_head, rate_head, grad_head = items

        def forward(x_vals, b_vals, c_vals, spread_vals, rate_vals):
            outputs = ssd_core(
                x_vals[:, None, None],
                b_vals[:, None],
                c_vals[:, None],
                spread_vals[:, None, None],
                rate_vals[None, None],
                BLOCK,
            )
            return outputs[0][:, 0, 0]

        _, backward = jax.vjp(forward, x_head, b_block, c_block, spread_head, rate_head)
        return backward(grad_head)

    head_x, head_b, head_c, head_spread, head_rate = lax.map(
        one_head,
        (
            jnp.moveaxis(x_block, 1, 0),
            jnp.moveaxis(spread_block, 1, 0),
            rate_block,
            jnp.moveaxis(grad_block, 1, 0),
        ),
    )
    grad_x = jnp.moveaxis(head_x, 0, 1) + gain_block[None, :, None] * grad_block
    grad_b = jnp.sum(head_b, axis=0)
    grad_c = jnp.sum(head_c, axis=0)
    grad_spread = jnp.moveaxis(head_spread, 0, 1)
    grad_gain = jnp.sum(grad_block * x_block, axis=(0, 2))
    return (grad_x, grad_b, grad_c, grad_spread, head_rate, grad_gain)


def local(mixer_input, step_raw, out_grad, conv_weight, conv_bias, step_bias, decay_log, skip_gain):
    local_input = mixer_input[0]
    local_raw = step_raw[0]
    local_grad = out_grad[0]
    row_count = local_input.shape[0]
    head_count = local_raw.shape[1]
    inner_width = local_grad.shape[1]
    span_ctx = lax.axis_size("ctx")
    per_device = head_count // span_ctx
    group_copies = span_ctx // GROUPS
    group_width = GROUPS * STATE
    halo_rows = KERNEL - 1
    previous = passed_along(local_input[row_count - halo_rows :], "ctx", 1)
    padded = jnp.concatenate([previous, local_input], axis=0).astype(jnp.float32)
    activated, conv_back = jax.vjp(causal_conv, padded, conv_weight, conv_bias)
    mixed_low = activated.astype(jnp.bfloat16)
    rates = -jnp.exp(decay_log)
    gate_in = local_raw.astype(jnp.float32) + step_bias[None, :]
    x_send = mixed_low[:, :inner_width].reshape(row_count, span_ctx, per_device * HEAD_DIM)
    b_low = mixed_low[:, inner_width : inner_width + group_width].reshape(
        row_count, GROUPS, 1, STATE
    )
    c_low = mixed_low[:, inner_width + group_width :].reshape(row_count, GROUPS, 1, STATE)
    paired = jnp.concatenate([b_low, c_low], axis=3)
    bc_send = jnp.broadcast_to(paired, (row_count, GROUPS, group_copies, 2 * STATE)).reshape(
        row_count, span_ctx, 2 * STATE
    )
    grad_send = local_grad.reshape(row_count, span_ctx, per_device * HEAD_DIM)
    raw_send = local_raw.reshape(row_count, span_ctx, per_device)
    x_recv, bc_recv, grad_recv, raw_recv = (
        lax.all_to_all(x_send, "ctx", split_axis=1, concat_axis=0, tiled=True),
        lax.all_to_all(bc_send, "ctx", split_axis=1, concat_axis=0, tiled=True),
        lax.all_to_all(grad_send, "ctx", split_axis=1, concat_axis=0, tiled=True),
        lax.all_to_all(raw_send, "ctx", split_axis=1, concat_axis=0, tiled=True),
    )
    seq_len = row_count * span_ctx
    first_head = lax.axis_index("ctx") * per_device
    rate_block = lax.dynamic_slice_in_dim(rates, first_head, per_device)
    bias_block = lax.dynamic_slice_in_dim(step_bias, first_head, per_device)
    gain_block = lax.dynamic_slice_in_dim(skip_gain, first_head, per_device)
    x_block = x_recv.reshape(seq_len, per_device, HEAD_DIM).astype(jnp.float32)
    b_block = bc_recv[:, 0, :STATE].astype(jnp.float32)
    c_block = bc_recv[:, 0, STATE:].astype(jnp.float32)
    spread_block = jax.nn.softplus(
        raw_recv.reshape(seq_len, per_device).astype(jnp.float32) + bias_block[None, :]
    )
    grad_block = grad_recv.reshape(seq_len, per_device, HEAD_DIM).astype(jnp.float32)
    grad_x, grad_b, grad_c, grad_spread, grad_rate, grad_gain = head_block(
        (x_block, b_block, c_block, spread_block, rate_block, gain_block, grad_block)
    )
    x_back = grad_x.astype(jnp.bfloat16).reshape(seq_len, 1, per_device * HEAD_DIM)
    bc_back = (
        jnp.concatenate([grad_b, grad_c], axis=1)
        .astype(jnp.bfloat16)
        .reshape(seq_len, 1, 2 * STATE)
    )
    spread_back = grad_spread.astype(jnp.bfloat16).reshape(seq_len, 1, per_device)
    x_home, bc_home, spread_home = (
        lax.all_to_all(x_back, "ctx", split_axis=0, concat_axis=1, tiled=True),
        lax.all_to_all(bc_back, "ctx", split_axis=0, concat_axis=1, tiled=True),
        lax.all_to_all(spread_back, "ctx", split_axis=0, concat_axis=1, tiled=True),
    )
    grad_inner = x_home.reshape(row_count, inner_width).astype(jnp.float32)
    bc_sum = jnp.sum(
        bc_home.astype(jnp.float32).reshape(row_count, GROUPS, group_copies, 2 * STATE), axis=2
    )
    grad_bgroups = bc_sum[:, :, :STATE].reshape(row_count, group_width)
    grad_cgroups = bc_sum[:, :, STATE:].reshape(row_count, group_width)
    grad_steps = spread_home.reshape(row_count, head_count).astype(jnp.float32)
    zero_heads = jnp.zeros((head_count,), jnp.float32)
    rate_part = lax.dynamic_update_slice_in_dim(zero_heads, grad_rate * rate_block, first_head, 0)
    gain_part = lax.dynamic_update_slice_in_dim(zero_heads, grad_gain, first_head, 0)
    local_step_grad = grad_steps * jax.nn.sigmoid(gate_in)
    grad_mixed = jnp.concatenate([grad_inner, grad_bgroups, grad_cgroups], axis=1)
    grad_pad, grad_weight, grad_bias = conv_back(grad_mixed)
    spilled = passed_along(grad_pad[:halo_rows].astype(jnp.bfloat16), "ctx", -1).astype(jnp.float32)
    own_rows = grad_pad[halo_rows:]
    own_rows = jnp.concatenate(
        [own_rows[: row_count - halo_rows], own_rows[row_count - halo_rows :] + spilled], axis=0
    )
    local_input_grad = own_rows.astype(jnp.bfloat16)[None]
    conv_part = jnp.concatenate([grad_weight, grad_bias[None, :]], axis=0)
    head_part = jnp.stack([rate_part, jnp.sum(local_step_grad, axis=0), gain_part])
    conv_total, head_total = (
        lax.psum(conv_part.astype(jnp.bfloat16), "ctx").astype(jnp.float32),
        lax.psum(head_part.astype(jnp.bfloat16), "ctx").astype(jnp.float32),
    )
    conv_share, head_share = (
        lax.psum_scatter(
            conv_total.astype(jnp.bfloat16), "dp", scatter_dimension=1, tiled=True
        ).astype(jnp.float32),
        lax.psum_scatter(
            head_total.astype(jnp.bfloat16), "dp", scatter_dimension=1, tiled=True
        ).astype(jnp.float32),
    )
    factor = 1.0 / math.sqrt(lax.axis_size("dp") * row_count * span_ctx)
    return (
        local_input_grad,
        local_step_grad[None],
        conv_share * factor,
        head_share[:2] * factor,
        head_share[2] * factor,
    )


def solution(mesh):
    in_specs = (
        P("dp", "ctx", None),
        P("dp", "ctx", None),
        P("dp", "ctx", None),
        P(),
        P(),
        P(),
        P(),
        P(),
    )
    out_specs = (P("dp", "ctx", None), P("dp", "ctx", None), P(None, "dp"), P(None, "dp"), P("dp"))
    return jax.shard_map(local, mesh=mesh, in_specs=in_specs, out_specs=out_specs, check_vma=False)
```

profile of v0, /device:TPU:1, one launch (start us, length us, event | category | flops | bytes accessed | tf_op | source)
XLA Modules:
  0.0 910.4 jit_solution(12505088579396042225)
XLA Ops:
  8.6 9.6 %all-to-all-start.1 = ((bf16[128,32,4]{0,2,1:T(4,128)(2,1)}), bf16[128,32,4]{0,2,1:T(4,128)(2,1)S(1)}, u32[]{:S(2)}, u32[]{:S(2)}) async-start(bf16[128,32,4]{0,2,1:T(4,128)(2,1)} %bitcast.81), calls=%async_computation.1 | async-start | bytes 65536 | tf_op jit(solution)/shard_map/all_to_all | solution.py:138
  27.4 4.1 copy.465
  33.6 6.3 maximum_convert_fusion
  39.8 6.8 all-to-all-start
  46.7 18.2 %multiply_convert_fusion = (bf16[128,10240]{0,1:T(8,128)(2,1)S(1)}, f32[128,10240]{0,1:T(8,128)}) fusion(f32[131,10240]{0,1:T(8,128)} %maximum_convert_fusion, f32[10240]{0:T(1024)S(1)} %bitcast.469, f32[10240]{0:T(1024)S(1)} %bitcast.471, f32[10240]{0:T(1024)S(1)} %bitcast.473, f32[10240]{0:T(1024)S(1)} %bitcast.467, f32[10240]{0:T(1024)S(1)} %copy-done.30), kind=kLoop, calls=%fused_computation.120 | loop fusion | flops 17039360 | bytes 29040640 | tf_op jit(solution)/shard_map/convert_element_type | solution.py:120
  67.9 6.6 all-to-all-done
  74.5 6.7 all-to-all-start.3
  82.6 26.6 %all-to-all-done.3 = bf16[128,32,256]{0,2,1:T(8,128)(2,1)} async-done(((bf16[128,32,256]{0,2,1:T(8,128)(2,1)}), bf16[128,32,256]{0,2,1:T(8,128)(2,1)}, u32[]{:S(2)}, u32[]{:S(2)}) %all-to-all-start.3) | async-done | bytes 2097184 | tf_op jit(solution)/shard_map/all_to_all | solution.py:135
  110.8 7.6 all-to-all-start.2
  119.8 4.4 copy.466
  124.3 4.9 reshape.904
  131.3 4.4 copy.471
  135.7 5.0 reshape.912
  140.7 5.5 all-to-all-done.2
  151.8 418.0 %while.19 = (s32[]{:T(128)}, f32[4,4096,64]{1,2,0:T(8,128)}, f32[4,4096,128]{2,1,0:T(8,128)}, f32[4,4096,128]{2,1,0:T(8,128)}, bf16[4,4096]{1,0:T(4,128)(2,1)}, ...) while((s32[]{:T(128)}, f32[4,4096,64]{1,2,0:T(8,128)}, ...), condition=%wide.region_14.15_spmd, body=%wide.region_0.14_spmd.sunk | while | flops 5150182400 | bytes 184448304 | solution.py:88
  178.7 4.6 fusion.185
  197.6 6.1 fusion.187
  203.9 5.7 fusion.193
  209.7 5.6 fusion.189
  215.4 7.8 fusion.188
  223.2 4.0 fusion.190
  227.2 5.7 bitcast_add_fusion.7
  235.5 7.3 fusion.194
  281.1 4.6 fusion.185
  300.0 5.9 fusion.187
  306.2 5.7 fusion.193
  311.9 5.6 fusion.189
  317.7 8.0 fusion.188
  325.7 4.0 fusion.190
  329.7 5.6 bitcast_add_fusion.7
  337.9 7.3 fusion.194
  383.5 4.8 fusion.185
  402.6 5.9 fusion.187
  408.7 5.7 fusion.193
  414.5 5.6 fusion.189
  420.2 7.8 fusion.188
  428.0 4.0 fusion.190
  432.0 5.8 bitcast_add_fusion.7
  440.5 7.3 fusion.194
  486.0 4.6 fusion.185
  504.9 6.1 fusion.187
  511.3 5.7 fusion.193
  517.0 5.6 fusion.189
  522.7 7.8 fusion.188
  530.5 4.0 fusion.190
  534.5 5.7 bitcast_add_fusion.7
  542.8 7.3 fusion.194
  574.9 5.9 all-to-all-start.6
  580.8 5.6 fusion.82
  596.7 7.5 all-to-all-start.4
  604.2 4.1 reduce_sum.215
  608.4 5.1 reduce_sum.219
  621.9 10.2 %all-to-all-done.4 = bf16[32,2,16384]{2,1,0:T(2,128)(2,1)} async-done(((bf16[32,2,16384]{2,1,0:T(2,128)(2,1)}), bf16[32,2,16384]{2,1,0:T(2,128)(2,1)}, u32[]{:S(2)}, u32[]{:S(2)}) %all-to-all-start.4) | async-done | bytes 2097184 | tf_op jit(solution)/shard_map/all_to_all | solution.py:163
  632.1 6.7 all-to-all-start.5
  650.6 18.5 %reduce-scatter.7.cloned.1.call-done = bf16[32,3]{1,0:T(8,128)(2,1)} async-done(((bf16[128,3]{1,0:T(8,128)(2,1)}), bf16[32,3]{1,0:T(8,128)(2,1)}) %reduce-scatter.7.cloned.1.call-update) | async-done | bytes 208
  669.8 10.6 %reshape.931 = bf16[4096,1,256]{2,1,0:T(2,128)(2,1)} reshape(bf16[32,2,16384]{2,1,0:T(2,128)(2,1)} %all-to-all-done.4) | data formatting | bytes 4194304
  685.5 5.6 copy.478
  691.1 10.5 %reshape.929 = bf16[4096,1,256]{2,1,0:T(2,128)(2,1)} reshape(bf16[32,2,16384]{2,1,0:T(2,128)(2,1)} %all-to-all-done.5) | data formatting | bytes 4194304
  701.5 6.5 convert_bitcast_fusion.2
  709.4 22.6 %multiply_reduce_fusion.6 = (f32[10240]{0:T(1024)S(1)}, f32[10240]{0:T(1024)S(1)}, f32[10240]{0:T(1024)S(1)}, f32[10240]{0:T(1024)S(1)}, bf16[10240]{0:T(1024)(128)(2,1)S(1)}, /*index=5*/f32[128,10240]{0,1:T(8,128)S(1)}) fusion(f32[131,10240]{0,1:T(8,128)} %maximum_convert_fusion, f32[128,10240]{0,1:T(8,128)} %get-tuple-element.331, ...), kind=kLoop, calls=%fused_computation.119 | loop fusion | flops 26163200 | bytes 36884480 | tf_op jit(solution)/shard_map/transpose(jvp())/reduce_sum | solution.py:29
  732.0 8.6 broadcast_multiply_fusion.5
  740.6 11.9 %fusion.99 = (bf16[131,10240]{0,1:T(8,128)(2,1)S(1)}, f32[131,10240]{0,1:T(8,128)}) fusion(f32[128,10240]{0,1:T(8,128)S(1)} %get-tuple-element.340, f32[128,10240]{0,1:T(8,128)S(1)} %get-tuple-element.341, f32[128,10240]{0,1:T(8,128)} %get-tuple-element.342, f32[128,10240]{0,1:T(8,128)S(1)} %get-tuple-element.339), kind=kLoop, calls=%fused_computation.172 | loop fusion | flops 5365760 | bytes 29020160 | tf_op jit(solution)/shard_map/convert.37
  765.7 4.5 fusion.83
  778.2 123.4 %all-reduce.9 = (bf16[5,2560]{1,0:T(8,128)(2,1)S(1)}, bf16[3,32]{1,0:T(4,128)(2,1)S(1)}) all-reduce(bf16[5,2560]{1,0:T(8,128)(2,1)} %reduce-scatter.5.cloned.1.call-done, bf16[3,32]{1,0:T(4,128)(2,1)S(1)} %copy.498), channel_id=1, replica_groups=mesh['dp'=4,'ctx'=32] {'ctx'}, use_global_device_ids=true, to_apply=%region_23.24 | all-reduce | flops 12896 | bytes 51584 | tf_op jit(solution)/shard_map/psum | solution.py:189
  (482 shorter events, 313.1 us)
Async XLA Ops:
  8.6 31.2 %all-to-all-start.1 = ((bf16[128,32,4]{0,2,1:T(4,128)(2,1)}), bf16[128,32,4]{0,2,1:T(4,128)(2,1)S(1)}, u32[]{:S(2)}, u32[]{:S(2)}) async-start(bf16[128,32,4]{0,2,1:T(4,128)(2,1)} %bitcast.81), calls=%async_computation.1 | async-start | bytes 65536 | tf_op jit(solution)/shard_map/all_to_all | solution.py:138
  19.2 12.3 %collective-permute-start = (bf16[3,10240]{1,0:T(4,128)(2,1)S(1)}, bf16[3,10240]{1,0:T(4,128)(2,1)S(1)}, u32[]{:S(2)}, u32[]{:S(2)}) collective-permute-start(bf16[3,10240]{1,0:T(4,128)(2,1)S(1)} %slice_bitcast_fusion.1), channel_id=1, source_target_pairs={{0,1},{1,2},{2,3},{3,4},{4,5},{5,6},{6,7},{7,8},{8,9},{9,10},{10,1... | collective-permute-start | bytes 184328 | tf_op jit(solution)/shard_map/ppermute | solution.py:21
  24.1 22.5 %copy-start.22 = (f32[1,10240]{1,0:T(1,128)}, f32[1,10240]{1,0:T(1,128)S(1)}, u32[]{:S(2)}) copy-start(f32[1,10240]{1,0:T(1,128)S(1)} %get-tuple-element.351) | copy-start | bytes 122884
  24.1 22.5 %copy-start.24 = (f32[1,10240]{1,0:T(1,128)}, f32[1,10240]{1,0:T(1,128)S(1)}, u32[]{:S(2)}) copy-start(f32[1,10240]{1,0:T(1,128)S(1)} %get-tuple-element.352) | copy-start | bytes 122884
  24.1 22.5 %copy-start.26 = (f32[1,10240]{1,0:T(1,128)}, f32[1,10240]{1,0:T(1,128)S(1)}, u32[]{:S(2)}) copy-start(f32[1,10240]{1,0:T(1,128)S(1)} %get-tuple-element.353) | copy-start | bytes 122884
  24.1 22.5 %copy-start.28 = (f32[1,10240]{1,0:T(1,128)}, f32[1,10240]{1,0:T(1,128)S(1)}, u32[]{:S(2)}) copy-start(f32[1,10240]{1,0:T(1,128)S(1)} %get-tuple-element.354) | copy-start | bytes 122884
  39.8 6.8 copy-start.30
  39.8 34.6 %all-to-all-start = ((bf16[128,32,256]{0,2,1:T(8,128)(2,1)}), bf16[128,32,256]{0,2,1:T(8,128)(2,1)S(1)}, u32[]{:S(2)}, u32[]{:S(2)}) async-start(bf16[128,32,256]{0,2,1:T(8,128)(2,1)} %bitcast.446), calls=%async_computation | async-start | bytes 4194304 | tf_op jit(solution)/shard_map/all_to_all | solution.py:137
  74.5 44.9 %copy-start.16 = (bf16[128,32,256]{0,2,1:T(8,128)(2,1)}, bf16[128,32,256]{0,2,1:T(8,128)(2,1)S(1)}, u32[]{:S(2)}) copy-start(bf16[128,32,256]{0,2,1:T(8,128)(2,1)S(1)} %all-to-all-done) | copy-start | bytes 6291460
  74.5 34.7 %all-to-all-start.3 = ((bf16[128,32,256]{0,2,1:T(8,128)(2,1)}), bf16[128,32,256]{0,2,1:T(8,128)(2,1)}, u32[]{:S(2)}, u32[]{:S(2)}) async-start(bf16[128,32,256]{0,2,1:T(8,128)(2,1)} %bitcast.447), calls=%async_computation.3 | async-start | bytes 4194304 | tf_op jit(solution)/shard_map/all_to_all | solution.py:135
  110.8 7.7 copy-start.38
  110.8 7.8 copy-start.39
  110.8 8.3 copy-start.33
  110.8 35.4 %all-to-all-start.2 = ((bf16[128,32,256]{2,0,1:T(8,128)(2,1)}), bf16[128,32,256]{2,0,1:T(8,128)(2,1)}, u32[]{:S(2)}, u32[]{:S(2)}) async-start(bf16[128,32,256]{2,0,1:T(8,128)(2,1)} %bitcast.445), calls=%async_computation.2 | async-start | bytes 4194304 | tf_op jit(solution)/shard_map/all_to_all | solution.py:136
  151.8 429.0 %copy-start.37 = (f32[4]{0:T(128)S(1)}, f32[4]{0:T(128)}, u32[]{:S(2)}) copy-start(f32[4]{0:T(128)} %dynamic_slice.30) | copy-start | bytes 52
  173.3 5.4 copy-start
  173.3 5.4 copy-start.3
  203.9 5.7 copy-start.9
  203.9 5.7 copy-start.10
  215.4 7.8 copy-start.2
  215.4 7.8 copy-start.12
  235.4 13.0 %copy-start.31 = (bf16[4,4096]{1,0:T(4,128)(2,1)S(1)}, bf16[4,4096]{1,0:T(4,128)(2,1)}, u32[]{:S(2)}) copy-start(bf16[4,4096]{1,0:T(4,128)(2,1)} %get-tuple-element.482) | copy-start | bytes 98308 | tf_op jit(solution)/shard_map/while
  235.4 13.1 %copy-start.14 = (f32[32,128,1,1,64]{1,0,2,4,3:T(8,128)S(1)}, f32[32,128,1,1,64]{1,0,2,4,3:T(8,128)}, u32[]{:S(2)}) copy-start(f32[32,128,1,1,64]{1,0,2,4,3:T(8,128)} %copy.648) | copy-start | bytes 3145732 | tf_op jit(solution)/shard_map/while
  248.6 5.5 copy-start.32
  275.7 5.4 copy-start
  275.7 5.4 copy-start.3
  306.2 5.7 copy-start.9
  306.2 5.7 copy-start.10
  317.6 8.0 copy-start.2
  317.7 8.0 copy-start.12
  337.9 13.0 %copy-start.31 = (bf16[4,4096]{1,0:T(4,128)(2,1)S(1)}, bf16[4,4096]{1,0:T(4,128)(2,1)}, u32[]{:S(2)}) copy-start(bf16[4,4096]{1,0:T(4,128)(2,1)} %get-tuple-element.482) | copy-start | bytes 98308 | tf_op jit(solution)/shard_map/while
  337.9 13.1 %copy-start.14 = (f32[32,128,1,1,64]{1,0,2,4,3:T(8,128)S(1)}, f32[32,128,1,1,64]{1,0,2,4,3:T(8,128)}, u32[]{:S(2)}) copy-start(f32[32,128,1,1,64]{1,0,2,4,3:T(8,128)} %copy.648) | copy-start | bytes 3145732 | tf_op jit(solution)/shard_map/while
  351.0 5.6 copy-start.32
  378.1 5.4 copy-start
  378.1 5.4 copy-start.3
  383.5 5.0 copy-start.15
  408.7 5.7 copy-start.9
  408.7 5.7 copy-start.10
  420.2 7.8 copy-start.2
  420.2 7.8 copy-start.12
  440.5 13.0 %copy-start.31 = (bf16[4,4096]{1,0:T(4,128)(2,1)S(1)}, bf16[4,4096]{1,0:T(4,128)(2,1)}, u32[]{:S(2)}) copy-start(bf16[4,4096]{1,0:T(4,128)(2,1)} %get-tuple-element.482) | copy-start | bytes 98308 | tf_op jit(solution)/shard_map/while
  440.5 13.1 %copy-start.14 = (f32[32,128,1,1,64]{1,0,2,4,3:T(8,128)S(1)}, f32[32,128,1,1,64]{1,0,2,4,3:T(8,128)}, u32[]{:S(2)}) copy-start(f32[32,128,1,1,64]{1,0,2,4,3:T(8,128)} %copy.648) | copy-start | bytes 3145732 | tf_op jit(solution)/shard_map/while
  453.6 5.5 copy-start.32
  480.6 5.4 copy-start
  480.6 5.4 copy-start.3
  511.3 5.7 copy-start.9
  511.3 5.7 copy-start.10
  522.7 7.8 copy-start.2
  522.7 7.8 copy-start.12
  542.8 13.0 %copy-start.31 = (bf16[4,4096]{1,0:T(4,128)(2,1)S(1)}, bf16[4,4096]{1,0:T(4,128)(2,1)}, u32[]{:S(2)}) copy-start(bf16[4,4096]{1,0:T(4,128)(2,1)} %get-tuple-element.482) | copy-start | bytes 98308 | tf_op jit(solution)/shard_map/while
  542.8 13.1 %copy-start.14 = (f32[32,128,1,1,64]{1,0,2,4,3:T(8,128)S(1)}, f32[32,128,1,1,64]{1,0,2,4,3:T(8,128)}, u32[]{:S(2)}) copy-start(f32[32,128,1,1,64]{1,0,2,4,3:T(8,128)} %copy.648) | copy-start | bytes 3145732 | tf_op jit(solution)/shard_map/while
  555.9 5.5 copy-start.32
  574.9 21.8 %all-to-all-start.6 = ((bf16[32,2,256]{2,1,0:T(2,128)(2,1)}), bf16[32,2,256]{2,1,0:T(2,128)(2,1)S(1)}, u32[]{:S(2)}, u32[]{:S(2)}) async-start(bf16[32,2,256]{2,1,0:T(2,128)(2,1)} %reshape.932), calls=%async_computation.6 | async-start | bytes 65536 | tf_op jit(solution)/shard_map/all_to_all | solution.py:165
  596.7 35.4 %all-to-all-start.4 = ((bf16[32,2,16384]{2,1,0:T(2,128)(2,1)}), bf16[32,2,16384]{2,1,0:T(2,128)(2,1)}, u32[]{:S(2)}, u32[]{:S(2)}) async-start(bf16[32,2,16384]{2,1,0:T(2,128)(2,1)} %reshape.930), calls=%async_computation.4 | async-start | bytes 4194304 | tf_op jit(solution)/shard_map/all_to_all | solution.py:163
  621.9 17.0 %copy-start.34 = (f32[128]{0:T(128)S(1)}, f32[128]{0:T(128)}, u32[]{:S(2)}) copy-start(f32[128]{0:T(128)} %param.15) | copy-start | bytes 1540
  621.9 18.0 %copy-start.17 = (bf16[128,32,256]{0,2,1:T(8,128)(2,1)S(1)}, bf16[128,32,256]{0,2,1:T(8,128)(2,1)}, u32[]{:S(2)}) copy-start(bf16[128,32,256]{0,2,1:T(8,128)(2,1)} %copy-done.16) | copy-start | bytes 6291460
  632.1 59.0 %all-to-all-start.5 = ((bf16[32,2,16384]{2,1,0:T(2,128)(2,1)}), bf16[32,2,16384]{2,1,0:T(2,128)(2,1)}, u32[]{:S(2)}, u32[]{:S(2)}) async-start(bf16[32,2,16384]{2,1,0:T(2,128)(2,1)} %reshape.928), calls=%async_computation.5 | async-start | bytes 4194304 | tf_op jit(solution)/shard_map/all_to_all | solution.py:164
  638.9 30.2 %reduce-scatter.7.cloned.1.call-start = ((), (), s32[]{:S(2)}) async-start(), calls=%async_computation.10 | async-start | bytes 40960
  648.9 129.3 %reduce-scatter.5.cloned.1.call-start = ((), (), s32[]{:S(2)}) async-start(), calls=%async_computation.9 | async-start | bytes 204800 | tf_op jit(solution)/shard_map/reduce_scatter | solution.py:193
  709.3 22.6 %copy-start.23 = (f32[1,10240]{1,0:T(1,128)S(1)}, f32[1,10240]{1,0:T(1,128)}, u32[]{:S(2)}) copy-start(f32[1,10240]{1,0:T(1,128)} %copy-done.22) | copy-start | bytes 122884
  709.3 22.6 %copy-start.25 = (f32[1,10240]{1,0:T(1,128)S(1)}, f32[1,10240]{1,0:T(1,128)}, u32[]{:S(2)}) copy-start(f32[1,10240]{1,0:T(1,128)} %copy-done.24) | copy-start | bytes 122884
  709.4 22.6 %copy-start.27 = (f32[1,10240]{1,0:T(1,128)S(1)}, f32[1,10240]{1,0:T(1,128)}, u32[]{:S(2)}) copy-start(f32[1,10240]{1,0:T(1,128)} %copy-done.26) | copy-start | bytes 122884
  709.4 22.6 %copy-start.29 = (f32[1,10240]{1,0:T(1,128)S(1)}, f32[1,10240]{1,0:T(1,128)}, u32[]{:S(2)}) copy-start(f32[1,10240]{1,0:T(1,128)} %copy-done.28) | copy-start | bytes 122884
  755.7 7.1 collective-permute-start.1
  (47 other events, 147.1 us)
Sparse Core Ops, SparseCore 0:
  649.0 19.9 reduce-scatter.6
  760.7 17.4 reduce-scatter.4
where the time goes:
time: 924 us; the launch traced here: 910 us
  local copies, waits for them, and re-layouts  224 us (24%)
  matrix products  219 us (24%)
  other arithmetic  187 us (20%)
  blocking collectives  123 us (13%)
  waiting for transfers between devices  73.3 us (8%)
  starting transfers between devices  58.4 us (6%)
  between operations  14.9 us (2%)
  loops' own time  10.5 us (1%)
    psum x1, blocking collectives, local(): lax.psum(conv_part.astype(jnp.bfloat16), 'ctx').astype(jnp.float32)  123 us
    dot_general x12, matrix products, ssd_core(): jnp.einsum('ctgn,cgknp->ctgkp', c_parts, entering, precision=FULL_PRECISION)  55.7 us
    unnamed x57, local copies, waits for them, and re-layouts  53.3 us
    dot_general x12, matrix products, ssd_core(): jnp.einsum('csgn,csgkp->cgknp', b_parts, x_parts * to_close[..., None], p...  52.9 us
    dot_general x8, matrix products, ssd_core(): jnp.einsum('ctsgk,csgkp->ctgkp', weights, x_parts, precision=FULL_PRECISION)  42.8 us
    another operation x8, other arithmetic, ssd_core(): running = jnp.cumsum(step_parts * rates, axis=1)  41.9 us
    dot_general x9, matrix products, ssd_core(): jnp.einsum('ctgn,csgn->ctsg', c_parts, b_parts, precision=FULL_PRECISION)  41 us
    another operation x12, local copies, waits for them, and re-layouts, ssd_core(): running = jnp.cumsum(step_parts * rates, axis=1)  30.8 us
  transfers between devices with their start and end apart: 11, of which 7 were waited for; matrix products, arithmetic and copies ran while one was open for 15% of the time, Pallas kernels for 0%

commit v1 on v0

v1 whole, which is shorter than its diff:
```python
import functools
import math

import jax
import jax.numpy as jnp
from jax import lax
from jax.experimental import pallas as pl
from jax.experimental.pallas import tpu as pltpu
from jax.sharding import PartitionSpec as P

HEADS = 128
HEAD_DIM = 64
STATE = 128
GROUPS = 8
KERNEL = 4
ROWS = 128
INNER = 8192
CONV = 10240
GROUP_HEADS = HEADS // GROUPS
GROUP_PAIRS = GROUP_HEADS // 2
GROUP_LANES = GROUP_HEADS * HEAD_DIM
PAIRS = HEADS // 2
HALF = PAIRS // 2
MESH = pl.DeviceIdType.MESH
F32 = jnp.float32
BF16 = jnp.bfloat16
EXACT = lax.Precision.HIGHEST


def dot(a, b, precision=None):
    return jnp.dot(a, b, precision=precision, preferred_element_type=F32)


def dot_nt(a, b):
    return lax.dot_general(a, b, (((1,), (1,)), ((), ())), preferred_element_type=F32)


def sigmoid(v):
    return 0.5 + 0.5 * jnp.tanh(0.5 * v)


def softplus(v):
    return jnp.maximum(v, 0.0) + jnp.log1p(jnp.exp(-jnp.abs(v)))


def iota(shape, dim):
    return lax.broadcasted_iota(jnp.int32, shape, dim)


def low_half(shape):
    return iota(shape, len(shape) - 1) < HEAD_DIM


def pair_of(columns, j):
    shape = (columns.shape[0], 2 * HEAD_DIM)
    first = jnp.broadcast_to(columns[:, 2 * j : 2 * j + 1], shape)
    second = jnp.broadcast_to(columns[:, 2 * j + 1 : 2 * j + 2], shape)
    return jnp.where(low_half(shape), first, second)


def conv_pre(pad, tile_ref, halo_ref, taps_ref, lanes):
    pad[0:8, :] = halo_ref[:, lanes]
    pad[8:, :] = tile_ref[:, lanes].astype(F32)
    pre = jnp.broadcast_to(taps_ref[4:5, lanes], (ROWS, 128))
    for k in range(KERNEL):
        pre = pre + taps_ref[k : k + 1, lanes] * pad[5 + k : 5 + k + ROWS, :]
    return pre


def states_kernel(
    x_ref, b_ref, c_ref, hx_ref, hb_ref, hc_ref, tx_ref, tb_ref, tc_ref, raw_ref, bias_ref, rate_ref, dy_ref,
    xm_ref, bm_ref, cm_ref, s_ref, g_ref, a_ref, run_ref, run_t_ref, sp_ref,
    pad,
):
    g = pl.program_id(0)

    @pl.when(g == 0)
    def _():
        spread = softplus(raw_ref[...].astype(F32) + bias_ref[...])
        shape = (ROWS, ROWS)
        lower = jnp.where(iota(shape, 0) >= iota(shape, 1), 1.0, 0.0).astype(F32)
        running = dot(lower, spread * rate_ref[...], EXACT)
        sp_ref[...] = spread
        run_ref[...] = running
        run_t_ref[...] = running.T

    def mixed(slot, tile_ref, halo_ref, taps_ref, lanes):
        pre = conv_pre(pad.at[slot], tile_ref, halo_ref, taps_ref, lanes)
        return (pre * sigmoid(pre)).astype(BF16)

    whole = pl.ds(0, 128)
    b16 = mixed(GROUP_PAIRS, b_ref, hb_ref, tb_ref, whole)
    c16 = mixed(GROUP_PAIRS + 1, c_ref, hc_ref, tc_ref, whole)
    bm_ref[0] = b16
    cm_ref[0] = c16
    b_t = b16.astype(F32).T.astype(BF16)
    c_t = c16.astype(F32).T.astype(BF16)
    back = lax.rem(HEADS - GROUP_HEADS * g, HEADS)
    run = pltpu.roll(run_ref[...], back, 1)
    spread = pltpu.roll(sp_ref[...], back, 1)
    closing = run[ROWS - 1 : ROWS, :]
    grown = jnp.exp(run)
    to_close = jnp.exp(closing - run) * spread
    whole_decay = jnp.exp(closing)
    for j in range(GROUP_PAIRS):
        lanes = pl.ds(128 * j, 128)
        x16 = mixed(j, x_ref, hx_ref, tx_ref, lanes)
        xm_ref[:, lanes] = x16
        s_ref[j] = dot(b_t, (x16.astype(F32) * pair_of(to_close, j)).astype(BF16)).astype(BF16)
        g_ref[j] = dot(c_t, (dy_ref[:, lanes].astype(F32) * pair_of(grown, j)).astype(BF16)).astype(BF16)
        a_ref[j] = pair_of(whole_decay, j)


def full(shape):
    return pl.BlockSpec(shape, lambda g: (0,) * len(shape))


def channel_specs(rows):
    return [
        pl.BlockSpec((rows, GROUP_LANES), lambda g: (0, g)),
        pl.BlockSpec((rows, STATE), lambda g: (0, INNER // STATE + g)),
        pl.BlockSpec((rows, STATE), lambda g: (0, INNER // STATE + GROUPS + g)),
    ]


def states(mixer, halo, taps, raw, bias, rate, dy):
    square = jax.ShapeDtypeStruct((ROWS, HEADS), F32)
    group = jax.ShapeDtypeStruct((GROUPS, ROWS, STATE), BF16)
    state = jax.ShapeDtypeStruct((PAIRS, STATE, 128), BF16)
    group_spec = pl.BlockSpec((1, ROWS, STATE), lambda g: (g, 0, 0))
    state_spec = pl.BlockSpec((GROUP_PAIRS, STATE, 128), lambda g: (g, 0, 0))
    x_spec = pl.BlockSpec((ROWS, GROUP_LANES), lambda g: (0, g))
    return pl.pallas_call(
        states_kernel,
        grid=(GROUPS,),
        in_specs=channel_specs(ROWS) + channel_specs(8) + channel_specs(8)
        + [full((ROWS, HEADS)), full((1, HEADS)), full((1, HEADS)), x_spec],
        out_specs=[
            x_spec, group_spec, group_spec, state_spec, state_spec,
            pl.BlockSpec((GROUP_PAIRS, 1, 128), lambda g: (g, 0, 0)),
            full((ROWS, HEADS)), full((HEADS, ROWS)), full((ROWS, HEADS)),
        ],
        out_shape=[
            jax.ShapeDtypeStruct((ROWS, INNER), BF16), group, group, state, state,
            jax.ShapeDtypeStruct((PAIRS, 1, 128), F32), square, square, square,
        ],
        scratch_shapes=[pltpu.VMEM((GROUP_PAIRS + 2, ROWS + 8, 128), F32)],
        compiler_params=pltpu.CompilerParams(vmem_limit_bytes=40 << 20),
        name="states",
    )(mixer, mixer, mixer, halo, halo, halo, taps, taps, taps, raw, bias, rate, dy)


def pass_kernel(
    s_ref, g_ref, a_ref, h_ref, l_ref,
    s_oth, g_oth, a_oth, s_out, g_out, a_out, s_in, g_in, a_in, h_out, l_out, h_in, l_in, h_oth, l_oth,
    x_send, x_recv, s_send, s_recv, g_send, g_recv, a_send, a_recv, h_send, h_recv, l_send, l_recv, o_send, o_recv,
):
    dp = lax.axis_index("dp")
    ctx = lax.axis_index("ctx")
    core = lax.rem(ctx, 2)
    chip = ctx // 2
    z, y = chip // 4, lax.rem(chip, 4)
    chips = lax.axis_size("ctx") // 2
    own = HALF // chips
    other = ctx + 1 - 2 * core
    mine = core * HALF
    theirs = HALF - mine

    def chip_at(r):
        return lax.rem(z + r // 4, 4) * 4 + lax.rem(y + r, 4)

    def device_at(r):
        return chip_at(r) * 2 + core

    barrier = pltpu.get_barrier_semaphore()
    pl.semaphore_signal(barrier, inc=1, device_id=(dp, other), device_id_type=MESH)

    def greet(r, _):
        pl.semaphore_signal(barrier, inc=1, device_id=(dp, device_at(r)), device_id_type=MESH)
        return 0

    lax.fori_loop(1, chips, greet, 0)
    pl.semaphore_wait(barrier, chips)

    def remote(src, dst, send, recv, device):
        return pltpu.make_async_remote_copy(
            src_ref=src, dst_ref=dst, send_sem=send, recv_sem=recv, device_id=(dp, device), device_id_type=MESH
        )

    swaps = [
        remote(src.at[pl.ds(theirs, HALF)], dst, x_send.at[i], x_recv.at[i], other)
        for i, (src, dst) in enumerate(((a_ref, a_oth), (s_ref, s_oth), (g_ref, g_oth)))
    ]
    for copy in swaps:
        copy.start()
    for copy in swaps:
        copy.wait()

    first = core == 0

    def ordered(held, sent):
        return jnp.where(first, held, sent), jnp.where(first, sent, held)

    def decays(at):
        return ordered(a_ref[pl.ds(mine + at, own)], a_oth[pl.ds(at, own)])

    def values(ref, oth, at):
        return ordered(ref[pl.ds(mine + at, own)].astype(F32), oth[pl.ds(at, own)].astype(F32))

    def out_copies(r):
        chosen = chip_at(r)
        at = pl.ds(chosen * own, own)
        device = device_at(r)
        return (
            remote(a_out.at[at], a_in.at[chip], a_send.at[r], a_recv.at[r], device),
            remote(s_out.at[at], s_in.at[chip], s_send.at[r], s_recv.at[r], device),
            remote(g_out.at[at], g_in.at[chip], g_send.at[r], g_recv.at[r], device),
        )

    def combine(r, _):
        at = chip_at(r) * own
        a0, a1 = decays(at)
        s0, s1 = values(s_ref, s_oth, at)
        g0, g1 = values(g_ref, g_oth, at)
        a_out[pl.ds(at, own)] = a0 * a1
        s_out[pl.ds(at, own)] = (a1 * s0 + s1).astype(BF16)
        g_out[pl.ds(at, own)] = (a0 * g1 + g0).astype(BF16)

        @pl.when(r > 0)
        def _():
            for copy in out_copies(r):
                copy.start()

        return 0

    lax.fori_loop(0, chips, combine, 0)
    at_own = pl.ds(chip * own, own)
    a_in[chip] = a_out[at_own]
    s_in[chip] = s_out[at_own]
    g_in[chip] = g_out[at_own]

    def arrived(r, _):
        for copy in out_copies(r):
            copy.wait_recv()
        return 0

    lax.fori_loop(1, chips, arrived, 0)

    def forth(c, state):
        h_out[c] = state.astype(BF16)
        return a_in[c] * state + s_in[c].astype(F32)

    def back(i, state):
        c = chips - 1 - i
        l_out[c] = state.astype(BF16)
        return a_in[c] * state + g_in[c].astype(F32)

    zero = jnp.zeros((own, STATE, 128), F32)
    lax.fori_loop(0, chips, forth, zero)
    lax.fori_loop(0, chips, back, zero)

    def home_copies(r):
        chosen = chip_at(r)
        device = device_at(r)
        return (
            remote(h_out.at[chosen], h_in.at[pl.ds(chip * own, own)], h_send.at[r], h_recv.at[r], device),
            remote(l_out.at[chosen], l_in.at[pl.ds(chip * own, own)], l_send.at[r], l_recv.at[r], device),
        )

    def send_home(r, _):
        for copy in home_copies(r):
            copy.start()
        return 0

    lax.fori_loop(1, chips, send_home, 0)
    h_in[at_own] = h_out[chip]
    l_in[at_own] = l_out[chip]

    def finish(r, _):
        source = lax.rem(z + 4 - r // 4, 4) * 4 + lax.rem(y + 4 - lax.rem(r, 4), 4)

        @pl.when(r > 0)
        def _():
            for copy in home_copies(r):
                copy.wait_recv()

        at = source * own
        here = pl.ds(at, own)
        held = pl.ds(mine + at, own)
        a0, a1 = decays(at)
        s0, _ = values(s_ref, s_oth, at)
        _, g1 = values(g_ref, g_oth, at)
        h0 = h_in[here]
        h1 = (a0 * h0.astype(F32) + s0).astype(BF16)
        l1 = l_in[here]
        l0 = (a1 * l1.astype(F32) + g1).astype(BF16)
        h_ref[held] = jnp.where(first, h0, h1)
        h_oth[here] = jnp.where(first, h1, h0)
        l_ref[held] = jnp.where(first, l0, l1)
        l_oth[here] = jnp.where(first, l1, l0)
        return 0

    lax.fori_loop(0, chips, finish, 0)
    lasts = [
        remote(src, dst.at[pl.ds(mine, HALF)], o_send.at[i], o_recv.at[i], other)
        for i, (src, dst) in enumerate(((h_oth, h_ref), (l_oth, l_ref)))
    ]
    for copy in lasts:
        copy.start()

    def sent(r, _):
        for copy in out_copies(r) + home_copies(r):
            copy.wait_send()
        return 0

    lax.fori_loop(1, chips, sent, 0)
    for copy in lasts:
        copy.wait()


def pass_states(s, g, a):
    chips = lax.axis_size("ctx") // 2
    own = HALF // chips
    wide = pltpu.VMEM((HALF, STATE, 128), BF16)
    split = pltpu.VMEM((chips, own, STATE, 128), BF16)
    row = pltpu.VMEM((HALF, 1, 128), F32)
    many = pltpu.SemaphoreType.DMA((chips,))
    memory = pl.BlockSpec(memory_space=pltpu.VMEM)
    return pl.pallas_call(
        pass_kernel,
        out_shape=[jax.ShapeDtypeStruct((PAIRS, STATE, 128), BF16)] * 2,
        in_specs=[memory] * 3,
        out_specs=[memory] * 2,
        scratch_shapes=[
            wide, wide, row, wide, wide, row, split, split, pltpu.VMEM((chips, own, 1, 128), F32),
            split, split, wide, wide, wide, wide,
            pltpu.SemaphoreType.DMA((3,)), pltpu.SemaphoreType.DMA((3,)),
        ] + [many] * 10 + [pltpu.SemaphoreType.DMA((2,)), pltpu.SemaphoreType.DMA((2,))],
        compiler_params=pltpu.CompilerParams(
            collective_id=0, has_side_effects=True, vmem_limit_bytes=48 << 20
        ),
        name="pass_states",
    )(s, g, a)


def grads_kernel(
    x_ref, b_ref, c_ref, hx_ref, hb_ref, hc_ref, tx_ref, tb_ref, tc_ref, raw_ref, bias_ref, rate_ref, dy_ref,
    gain_ref, xm_ref, bm_ref, cm_ref, h_ref, l_ref, run_ref, run_t_ref, sp_ref,
    ig_ref, last_ref, spill_ref, taps_out, step_ref, rows_ref,
    pad, dpad, dsc, acc_b, acc_c, col_u, col_q, col_s, row_g, full_u, full_q, full_s, full_r, full_g,
):
    g = pl.program_id(0)
    back = lax.rem(HEADS - GROUP_HEADS * g, HEADS)
    shape = (ROWS, ROWS)

    @pl.when(g == 0)
    def _():
        dpad[:, ROWS:, :] = jnp.zeros((GROUP_PAIRS + 2, 8, 128), F32)
        for ref in (full_u, full_q, full_s, full_g, col_u, col_q, col_s, row_g):
            ref[...] = jnp.zeros(ref.shape, F32)

    b16, c16 = bm_ref[0], cm_ref[0]
    scores = jnp.where(iota(shape, 1) >= iota(shape, 0), dot_nt(b16, c16), 0.0)
    run = pltpu.roll(run_ref[...], back, 1)
    spread = pltpu.roll(sp_ref[...], back, 1)
    grown = jnp.exp(run)
    to_close = jnp.exp(run[ROWS - 1 : ROWS, :] - run) * spread
    low = low_half(shape)
    low_row = low_half((1, 128))
    dsc[...] = jnp.zeros(shape, F32)
    acc_b[...] = jnp.zeros(shape, F32)
    acc_c[...] = jnp.zeros(shape, F32)

    def conv_back(slot, grad, tile_ref, halo_ref, taps_ref, lanes, out):
        here = pad.at[slot]
        there = dpad.at[slot]
        pre = conv_pre(here, tile_ref, halo_ref, taps_ref, lanes)
        gate = sigmoid(pre)
        dpre = grad * (gate * (1.0 + pre * (1.0 - gate)))
        there[0:ROWS, :] = dpre
        whole = jnp.zeros(shape, F32)
        for k in range(KERNEL):
            whole = whole + taps_ref[k : k + 1, lanes] * there[3 - k : 3 - k + ROWS, :]
            taps_out[k : k + 1, out] = jnp.sum(dpre * here[5 + k : 5 + k + ROWS, :], axis=0, keepdims=True)
        taps_out[4:5, out] = jnp.sum(dpre, axis=0, keepdims=True)
        taps_out[5:8, out] = jnp.zeros((3, 128), F32)
        ig_ref[:, out] = whole.astype(BF16)
        last_ref[:, out] = whole[ROWS - 8 :, :]
        head = dpre[0:8, :]
        row = iota((8, 128), 0)
        spilled = jnp.zeros((8, 128), F32)
        for k in range(KERNEL - 1):
            moved = pltpu.roll(head, 5 + k, 0)
            spilled = spilled + jnp.where(row >= 5 + k, taps_ref[k : k + 1, lanes] * moved, 0.0)
        spill_ref[:, out] = spilled

    for j in range(GROUP_PAIRS):
        lanes = pl.ds(128 * j, 128)
        x16 = xm_ref[:, lanes]
        x = x16.astype(F32)
        dy = dy_ref[:, lanes].astype(F32)
        split = jnp.concatenate([jnp.where(low, dy, 0.0), jnp.where(low, 0.0, dy)], axis=0).astype(BF16)
        d_weights = dot_nt(x16, split)
        weights = []
        for i in range(2):
            head = 2 * j + i
            at = GROUP_HEADS * g + head
            step = spread[:, head : head + 1]
            d_weight = d_weights[:, 128 * i : 128 * i + 128]
            decay = jnp.exp(jnp.minimum(run_t_ref[pl.ds(at, 1), :] - run[:, head : head + 1], 0.0))
            plain = decay * scores
            weights.append((plain * step).astype(BF16))
            product = d_weight * plain
            col_s[:, head : head + 1] = jnp.sum(product, axis=1, keepdims=True)
            full_r[pl.ds(at, 1), :] = jnp.sum(product * step, axis=0, keepdims=True)
            dsc[...] += d_weight * decay * step
        h16, l16 = h_ref[j], l_ref[j]
        grown_2 = pair_of(grown, j)
        close_2 = pair_of(to_close, j)
        entered = dy * dot(c16, h16)
        left = dot(b16, l16)
        used = x * left
        for i in range(2):
            head = 2 * j + i
            mask = low if i == 0 else jnp.logical_not(low)
            mask_row = low_row if i == 0 else jnp.logical_not(low_row)
            col_u[:, head : head + 1] = jnp.sum(jnp.where(mask, entered, 0.0), axis=1, keepdims=True)
            col_q[:, head : head + 1] = jnp.sum(jnp.where(mask, used, 0.0), axis=1, keepdims=True)
            crossed = jnp.sum(h16.astype(F32) * l16.astype(F32), axis=0, keepdims=True)
            gained = jnp.sum(dy * x, axis=0, keepdims=True)
            row_g[0:1, head : head + 1] = jnp.sum(jnp.where(mask_row, crossed, 0.0), axis=1, keepdims=True)
            row_g[1:2, head : head + 1] = jnp.sum(jnp.where(mask_row, gained, 0.0), axis=1, keepdims=True)
        acc_c[...] += dot_nt((dy * grown_2).astype(BF16), h16)
        acc_b[...] += dot_nt((x * close_2).astype(BF16), l16)
        grad_x = dot(jnp.concatenate(weights, axis=1), split) + close_2 * left + gain_ref[0, :, lanes] * dy
        conv_back(j, grad_x, x_ref, hx_ref, tx_ref, lanes, pl.ds(pl.multiple_of(g * GROUP_LANES + 128 * j, 128), 128))

    d_scores = jnp.where(iota(shape, 1) >= iota(shape, 0), dsc[...], 0.0)
    grad_b = acc_b[...] + dot(d_scores.astype(BF16), c16)
    grad_c = acc_c[...] + dot(d_scores.T.astype(BF16), b16)
    every = pl.ds(0, 128)
    conv_back(GROUP_PAIRS, grad_b, b_ref, hb_ref, tb_ref, every, pl.ds(pl.multiple_of(INNER + 128 * g, 128), 128))
    conv_back(
        GROUP_PAIRS + 1, grad_c, c_ref, hc_ref, tc_ref, every,
        pl.ds(pl.multiple_of(INNER + GROUPS * STATE + 128 * g, 128), 128),
    )

    forward = lax.rem(GROUP_HEADS * g, HEADS)
    for whole_ref, part_ref in ((full_u, col_u), (full_q, col_q), (full_s, col_s), (full_g, row_g)):
        lane = iota(part_ref.shape, 1)
        whole_ref[...] += pltpu.roll(jnp.where(lane < GROUP_HEADS, part_ref[...], 0.0), forward, 1)

    @pl.when(g == GROUPS - 1)
    def _():
        running, steps = run_ref[...], sp_ref[...]
        rate = rate_ref[...]
        closing = running[ROWS - 1 : ROWS, :]
        from_close = jnp.exp(closing - running)
        direct_q = from_close * full_q[...]
        used_q = direct_q * steps
        summed = full_r[...].T + jnp.exp(running) * full_u[...] - full_s[...] * steps - used_q
        upper = jnp.where(iota(shape, 1) >= iota(shape, 0), 1.0, 0.0).astype(F32)
        constant = jnp.sum(used_q, axis=0, keepdims=True) + jnp.exp(closing) * full_g[0:1, :]
        d_logs = dot(upper, summed, EXACT) + constant
        d_spread = (d_logs * rate + full_s[...] + direct_q).astype(BF16).astype(F32)
        step_grad = d_spread * sigmoid(raw_ref[...].astype(F32) + bias_ref[...])
        step_ref[...] = step_grad
        rows_ref[...] = jnp.zeros((8, HEADS), F32)
        rows_ref[0:1, :] = rate * jnp.sum(d_logs * steps, axis=0, keepdims=True)
        rows_ref[1:2, :] = jnp.sum(step_grad, axis=0, keepdims=True)
        rows_ref[2:3, :] = full_g[1:2, :]


def grads(mixer, halo, taps, raw, bias, rate, dy, gain, xm, bm, cm, h, l, run, run_t, sp):
    x_spec = pl.BlockSpec((ROWS, GROUP_LANES), lambda g: (0, g))
    group_spec = pl.BlockSpec((1, ROWS, STATE), lambda g: (g, 0, 0))
    state_spec = pl.BlockSpec((GROUP_PAIRS, STATE, 128), lambda g: (g, 0, 0))
    square = full((ROWS, HEADS))
    plane = pltpu.VMEM((ROWS, 128), F32)
    tall = pltpu.VMEM((GROUP_PAIRS + 2, ROWS + 8, 128), F32)
    rows = pltpu.VMEM((8, 128), F32)
    edge = jax.ShapeDtypeStruct((8, CONV), F32)
    return pl.pallas_call(
        grads_kernel,
        grid=(GROUPS,),
        in_specs=channel_specs(ROWS) + channel_specs(8) + channel_specs(8)
        + [square, full((1, HEADS)), full((1, HEADS)), x_spec]
        + [pl.BlockSpec((1, 1, GROUP_LANES), lambda g: (g, 0, 0)), x_spec, group_spec, group_spec]
        + [state_spec, state_spec, square, square, square],
        out_specs=[full((ROWS, CONV))] + [full((8, CONV))] * 3 + [square, full((8, HEADS))],
        out_shape=[
            jax.ShapeDtypeStruct((ROWS, CONV), BF16), edge, edge, edge,
            jax.ShapeDtypeStruct((ROWS, HEADS), F32), jax.ShapeDtypeStruct((8, HEADS), F32),
        ],
        scratch_shapes=[tall, tall] + [plane] * 6 + [rows] + [plane] * 4 + [rows],
        compiler_params=pltpu.CompilerParams(vmem_limit_bytes=48 << 20),
        name="grads",
    )(
        mixer, mixer, mixer, halo, halo, halo, taps, taps, taps, raw, bias, rate, dy,
        gain, xm, bm, cm, h, l, run, run_t, sp,
    )


def passed_along(value, axis, steps):
    count = lax.axis_size(axis)
    initial, last = (max(0, -steps), min(count, count - steps))
    return lax.ppermute(value, axis, [(source, source + steps) for source in range(initial, last)])


def local(mixer_input, step_raw, out_grad, conv_weight, conv_bias, step_bias, decay_log, skip_gain):
    mixer, raw, dy = mixer_input[0], step_raw[0], out_grad[0]
    halo = passed_along(mixer[ROWS - 8 :], "ctx", 1).astype(F32)
    taps = jnp.concatenate([conv_weight, conv_bias[None], jnp.zeros((3, CONV), F32)], axis=0)
    bias = step_bias[None]
    rate = -jnp.exp(decay_log)[None]
    gain = jnp.repeat(skip_gain, HEAD_DIM).reshape(GROUPS, 1, GROUP_LANES)
    xm, bm, cm, s, g, a, run, run_t, sp = states(mixer, halo, taps, raw, bias, rate, dy)
    h, l = pass_states(s, g, a)
    input_grad, last, spill, taps_grad, step_grad, rows = grads(
        mixer, halo, taps, raw, bias, rate, dy, gain, xm, bm, cm, h, l, run, run_t, sp
    )
    spilled = passed_along(spill.astype(BF16), "ctx", -1).astype(F32)
    input_grad = lax.dynamic_update_slice(input_grad, (last + spilled).astype(BF16), (ROWS - 8, 0))
    factor = 1.0 / math.sqrt(lax.axis_size("dp") * ROWS * lax.axis_size("ctx"))
    conv_share = lax.psum_scatter(taps_grad[: KERNEL + 1], "dp", scatter_dimension=1, tiled=True)
    head_share = lax.psum_scatter(rows[:3], "dp", scatter_dimension=1, tiled=True)
    conv_total, head_total = lax.psum((conv_share, head_share), "ctx")
    return (
        input_grad[None],
        step_grad[None],
        conv_total * factor,
        head_total[:2] * factor,
        head_total[2] * factor,
    )


def solution(mesh):
    spread = P("dp", "ctx", None)
    in_specs = (spread, spread, spread, P(), P(), P(), P(), P())
    out_specs = (spread, spread, P(None, "dp"), P(None, "dp"), P("dp"))
    return jax.shard_map(local, mesh=mesh, in_specs=in_specs, out_specs=out_specs, check_vma=False)
```

time: 924 us -> 346 us (0.37)
  matrix products: 219 us -> 0 us
  local copies, waits for them, and re-layouts: 224 us -> 14.8 us
  other arithmetic: 187 us -> 4.16 us
  Pallas kernels: 0 us -> 135 us
  starting transfers between devices: 58.4 us -> 6.72 us
  waiting for transfers between devices: 73.3 us -> 42.7 us
  loops' own time: 10.5 us -> 0 us
    dot_general x53 -> x0, matrix products: 219 us -> none  [the longest x12 55.7 us: ssd_core(): jnp.einsum('ctgn,cgknp->ctgkp', c_parts, entering, precision=FULL_PRECISION)]
    pallas_call x0 -> x3, Pallas kernels: none -> 135 us  [the longest x1 82.7 us: pass_states(): pl.pallas_call(pass_kernel, out_shape=[jax.ShapeDtypeStruct((PAIRS, STATE...]
    another operation x31 -> x0, other arithmetic: 56.2 us -> none  [the longest x8 41.9 us: ssd_core(): running = jnp.cumsum(step_parts * rates, axis=1)]
    all_to_all x7 -> x0, starting transfers between devices: 50.8 us -> none  [the longest x1 9.6 us: local(): lax.all_to_all(raw_send, 'ctx', split_axis=1, concat_axis=0, tiled=True)]
    all_to_all x7 -> x0, waiting for transfers between devices: 48.9 us -> none  [the longest x1 26.6 us: local(): lax.all_to_all(x_send, 'ctx', split_axis=1, concat_axis=0, tiled=True)]
    reduce_sum x15 -> x0, other arithmetic: 41.5 us -> none  [the longest x1 22.6 us: causal_conv(): conv_weight[offset][None, :] * padded[offset:offset + seq_len]]
    unnamed x57 -> x26, local copies, waits for them, and re-layouts: 53.3 us -> 12.9 us
    convert_element_type x8 -> x2, other arithmetic: 40.3 us -> 0.04 us  [the longest x1 0.02 us: local(): halo = passed_along(mixer[ROWS - 8:], 'ctx', 1).astype(F32)]
  transfers between devices with their start and end apart: 11 -> 4, of which waited for: 7 -> 2; matrix products, arithmetic and copies ran while one was open for 15% -> 1% of each run, Pallas kernels for 0% -> 0%
where the time goes in v1:
time: 346 us; the launch traced here: 341 us
  Pallas kernels  135 us (39%)
  blocking collectives  124 us (36%)
  waiting for transfers between devices  42.7 us (12%)
  local copies, waits for them, and re-layouts  14.8 us (4%)
  between operations  14.2 us (4%)
  starting transfers between devices  6.72 us (2%)
  other arithmetic  4.16 us (1%)
    psum x1, blocking collectives, local(): conv_total, head_total = lax.psum((conv_share, head_share), 'ctx')  124 us
    pallas_call x1, Pallas kernels, pass_states(): pl.pallas_call(pass_kernel, out_shape=[jax.ShapeDtypeStruct((PAIRS, STATE...  82.7 us
    pallas_call x1, Pallas kernels, grads(): pl.pallas_call(grads_kernel, grid=(GROUPS,), in_specs=channel_specs(ROWS)...  41.6 us
    reduce_scatter x1, waiting for transfers between devices, local(): lax.psum_scatter(taps_grad[:KERNEL + 1], 'dp', scatter_dimension=1, tiled...  21.5 us
    unnamed x3, waiting for transfers between devices  21.2 us
    unnamed x26, local copies, waits for them, and re-layouts  12.9 us
    pallas_call x1, Pallas kernels, states(): pl.pallas_call(states_kernel, grid=(GROUPS,), in_specs=channel_specs(ROWS...  10.3 us
  transfers between devices with their start and end apart: 4, of which 2 were waited for; matrix products, arithmetic and copies ran while one was open for 1% of the time, Pallas kernels for 0%

profile of v1, /device:TPU:1, one launch (start us, length us, event | category | flops | bytes accessed | tf_op | source)
XLA Modules:
  0.0 341.1 jit_solution(12788693755117994265)
XLA Ops:
  7.2 0.0 reduce-scatter.7.cloned.1.call-start
  7.2 0.9 slice_bitcast_fusion
  8.1 4.6 %collective-permute-start = (bf16[8,10240]{1,0:T(8,128)(2,1)S(1)}, bf16[8,10240]{1,0:T(8,128)(2,1)S(1)}, u32[]{:S(2)}, u32[]{:S(2)}) collective-permute-start(bf16[8,10240]{1,0:T(8,128)(2,1)S(1)} %slice_bitcast_fusion), channel_id=1, source_target_pairs={{0,1},{1,2},{2,3},{3,4},{4,5},{5,6},{6,7},{7,8},{8,9},{9,10},{10,1... | collective-permute-start | bytes 491528 | tf_op jit(solution)/shard_map/ppermute | solution.py:507
  12.7 0.7 broadcast_in_dim.28
  13.5 0.1 broadcast_in_dim.29
  13.6 0.1 broadcast_in_dim.30.gain_ref
  13.7 0.1 pad.2.clone
  13.8 1.0 maximum_maximum_fusion.tx_ref.tb_ref.tc_ref
  14.8 0.7 negate_bitcast_fusion.rate_ref
  15.5 0.0 collective-permute-done
  15.5 0.0 copy-start
  15.5 1.7 copy-done
  17.2 0.0 copy-start.1
  17.2 1.6 copy-done.1
  18.8 0.0 copy-start.8
  18.8 0.8 copy-done.8
  19.6 0.0 copy-start.10
  19.6 0.7 copy-done.10
  20.2 10.3 %states.1 = (bf16[128,8192]{1,0:T(8,128)(2,1)S(1)}, bf16[8,128,128]{2,1,0:T(8,128)(2,1)S(1)}, bf16[8,128,128]{2,1,0:T(8,128)(2,1)S(1)}, bf16[64,128,128]{2,1,0:T...) custom-call(bf16[128,10240]{1,0:T(8,128)(2,1)S(1)} %bitcast.23, ...), custom_call_target="tpu_custom_call" | custom-call | tf_op jit(solution)/shard_map/states/pallas_call | solution.py:133
  30.5 0.0 copy-start.3
  30.5 1.3 copy-done.3
  31.9 0.0 copy-start.6
  31.9 1.3 copy-done.6
  33.2 0.0 copy-start.7
  33.2 1.3 copy-done.7
  34.5 0.0 copy-start.2
  34.5 0.0 copy-start.9
  34.5 0.0 copy-start.11
  34.5 82.7 %pass_states.1 = (bf16[64,128,128]{2,1,0:T(8,128)(2,1)S(1)}, bf16[64,128,128]{2,1,0:T(8,128)(2,1)S(1)}) custom-call(bf16[64,128,128]{2,1,0:T(8,128)(2,1)} %copy-done.6, bf16[64,128,128]{2,1,0:T(8,128)(2,1)} %copy-done.7, f32[64,1,128]{2,1,0:T(1,128)S(1)} %get-tuple-element.27.a_ref), custom_call_target="tpu_custom_call" | custom-call | tf_op jit(solution)/shard_map/pass_states/pallas_call | solution.py:329
  117.2 0.0 copy-start.4
  117.3 1.3 copy-done.4
  118.6 0.0 copy-start.5
  118.6 1.3 copy-done.5
  119.9 0.0 copy-done.2
  119.9 0.0 copy-done.9
  119.9 0.0 copy-done.11
  119.9 41.6 %grads.1 = (bf16[128,10240]{1,0:T(8,128)(2,1)}, f32[8,10240]{1,0:T(8,128)S(1)}, f32[8,10240]{1,0:T(8,128)S(1)}, f32[8,10240]{1,0:T(8,128)}, f32[128,128]{1,0:T(8,128)}, /*index=5*/f32[8,128]{1,0:T(8,128)S(1)}) custom-call(bf16[128,10240]{1,0:T(8,128)(2,1)} %bitcast.20, bf16[128,10240]{1,0:T(8,128)(2,1)} %bitcast.21, bf16[128,10240]{1,0:T(8,128)(2,1)} %bitcast.22, ...), custom_call_target="tpu_custom_call" | custom-call | tf_op jit(solution)/shard_map/grads/pallas_call | solution.py:483
  161.6 2.0 collective-permute-start.1
  163.6 0.7 copy.13
  164.4 0.0 reduce-scatter.7.cloned.1.call-update
  164.4 0.0 reduce-scatter.5.cloned.1.call-start
  164.5 0.7 reduce-scatter.5.cloned.1.call-update
  165.2 20.5 %reduce-scatter.7.cloned.1.call-done = f32[32,3]{1,0:T(8,128)} async-done(((f32[128,3]{1,0:T(8,128)}), f32[32,3]{1,0:T(8,128)}) %reduce-scatter.7.cloned.1.call-update) | async-done | bytes 400
  185.6 0.8 copy.14
  186.4 0.0 collective-permute-done.1
  186.4 0.7 fusion.1
  187.1 21.5 %reduce-scatter.5.cloned.1.call-done = f32[5,2560]{1,0:T(8,128)} async-done(((f32[5,10240]{1,0:T(8,128)}), f32[5,2560]{1,0:T(8,128)}) %reduce-scatter.5.cloned.1.call-update) | async-done | bytes 51216 | tf_op jit(solution)/shard_map/reduce_scatter | solution.py:525
  208.6 123.9 %all-reduce = (f32[5,2560]{1,0:T(8,128)S(1)}, f32[3,32]{1,0:T(4,128)S(1)}) all-reduce(f32[5,2560]{1,0:T(8,128)} %reduce-scatter.5.cloned.1.call-done, f32[3,32]{1,0:T(4,128)S(1)} %copy.14), channel_id=1, replica_groups=mesh['dp'=4,'ctx'=32] {'ctx'}, use_global_device_ids=true, to_apply=%region_1.0 | all-reduce | flops 12896 | bytes 103168 | tf_op jit(solution)/shard_map/psum | solution.py:527
  332.6 0.6 slice_multiply_fusion
  333.1 0.5 multiply_bitcast_fusion
  333.7 0.6 broadcast_multiply_fusion
  (4 shorter events, 0.0 us)
Async XLA Ops:
  7.2 178.5 %reduce-scatter.7.cloned.1.call-start = ((), (), s32[]{:S(2)}) async-start(), calls=%async_computation.3 | async-start | bytes 81920
  8.1 7.3 %collective-permute-start = (bf16[8,10240]{1,0:T(8,128)(2,1)S(1)}, bf16[8,10240]{1,0:T(8,128)(2,1)S(1)}, u32[]{:S(2)}, u32[]{:S(2)}) collective-permute-start(bf16[8,10240]{1,0:T(8,128)(2,1)S(1)} %slice_bitcast_fusion), channel_id=1, source_target_pairs={{0,1},{1,2},{2,3},{3,4},{4,5},{5,6},{6,7},{7,8},{8,9},{9,10},{10,1... | collective-permute-start | bytes 491528 | tf_op jit(solution)/shard_map/ppermute | solution.py:507
  15.5 1.7 copy-start
  17.2 1.6 copy-start.1
  18.8 0.8 copy-start.8
  19.6 0.7 copy-start.10
  30.5 1.3 copy-start.3
  31.9 1.3 copy-start.6
  33.2 1.3 copy-start.7
  34.5 85.4 %copy-start.2 = (bf16[1,128,8192]{2,1,0:T(8,128)(2,1)S(1)}, bf16[1,128,8192]{2,1,0:T(8,128)(2,1)}, u32[]{:S(2)}) copy-start(bf16[1,128,8192]{2,1,0:T(8,128)(2,1)} %param.10) | copy-start | bytes 6291460
  34.5 85.4 %copy-start.9 = (bf16[1,128,128]{2,1,0:T(8,128)(2,1)S(1)}, bf16[1,128,128]{2,1,0:T(8,128)(2,1)}, u32[]{:S(2)}) copy-start(bf16[1,128,128]{2,1,0:T(8,128)(2,1)} %param.9) | copy-start | bytes 98308
  34.5 85.4 %copy-start.11 = (f32[128]{0:T(128)S(1)}, f32[128]{0:T(128)}, u32[]{:S(2)}) copy-start(f32[128]{0:T(128)} %param.13) | copy-start | bytes 1540
  117.2 1.3 copy-start.4
  118.6 1.3 copy-start.5
  161.6 24.8 %collective-permute-start.1 = (bf16[8,10240]{1,0:T(8,128)(2,1)S(1)}, bf16[8,10240]{1,0:T(8,128)(2,1)S(1)}, u32[]{:S(2)}, u32[]{:S(2)}) collective-permute-start(bf16[8,10240]{1,0:T(8,128)(2,1)S(1)} %convert_element_type.13), channel_id=1, source_target_pairs={{1,0},{2,1},{3,2},{4,3},{5,4},{6,5},{7,6},{8,7},{9,8},{10,9},{11,1... | collective-permute-start | bytes 491528 | tf_op jit(solution)/shard_map/ppermute | solution.py:507
  164.4 44.2 %reduce-scatter.5.cloned.1.call-start = ((), (), s32[]{:S(2)}) async-start(), calls=%async_computation.2 | async-start | bytes 409600 | tf_op jit(solution)/shard_map/reduce_scatter | solution.py:525
Sparse Core Ops, SparseCore 0:
  164.5 21.0 reduce-scatter.6
  188.1 20.4 reduce-scatter.4

commit v2 on v1

v2 whole, which is shorter than its diff:
```python
import functools
import math

import jax
import jax.numpy as jnp
from jax import lax
from jax.experimental import pallas as pl
from jax.experimental.pallas import tpu as pltpu
from jax.sharding import PartitionSpec as P

HEADS = 128
HEAD_DIM = 64
STATE = 128
GROUPS = 8
KERNEL = 4
ROWS = 128
INNER = 8192
CONV = 10240
GROUP_HEADS = HEADS // GROUPS
GROUP_PAIRS = GROUP_HEADS // 2
GROUP_LANES = GROUP_HEADS * HEAD_DIM
PAIRS = HEADS // 2
HALF = PAIRS // 2
MESH = pl.DeviceIdType.MESH
F32 = jnp.float32
BF16 = jnp.bfloat16
VMEM = 60 << 20
EARLY, MIDDLE, LATE = 12, 32, 44
EXACT = lax.Precision.HIGHEST


def dot(a, b, precision=None):
    return jnp.dot(a, b, precision=precision, preferred_element_type=F32)


def dot_nt(a, b):
    return lax.dot_general(a, b, (((1,), (1,)), ((), ())), preferred_element_type=F32)


def sigmoid(v):
    return 0.5 + 0.5 * jnp.tanh(0.5 * v)


def softplus(v):
    return jnp.maximum(v, 0.0) + jnp.log1p(jnp.exp(-jnp.abs(v)))


def iota(shape, dim):
    return lax.broadcasted_iota(jnp.int32, shape, dim)


def low_half(shape):
    return iota(shape, len(shape) - 1) < HEAD_DIM


def pair_of(columns, j):
    shape = (columns.shape[0], 2 * HEAD_DIM)
    first = jnp.broadcast_to(columns[:, 2 * j : 2 * j + 1], shape)
    second = jnp.broadcast_to(columns[:, 2 * j + 1 : 2 * j + 2], shape)
    return jnp.where(low_half(shape), first, second)


def conv_pre(pad, tile_ref, halo_ref, taps_ref, lanes):
    pad[0:8, :] = halo_ref[:, lanes]
    pad[8:, :] = tile_ref[:, lanes].astype(F32)
    pre = jnp.broadcast_to(taps_ref[4:5, lanes], (ROWS, 128))
    for k in range(KERNEL):
        pre = pre + taps_ref[k : k + 1, lanes] * pad[5 + k : 5 + k + ROWS, :]
    return pre


def full(shape):
    return pl.BlockSpec(shape, lambda g: (0,) * len(shape))


def channel_specs(rows):
    return [
        pl.BlockSpec((rows, GROUP_LANES), lambda g: (0, g)),
        pl.BlockSpec((rows, STATE), lambda g: (0, INNER // STATE + g)),
        pl.BlockSpec((rows, STATE), lambda g: (0, INNER // STATE + GROUPS + g)),
    ]


def front_kernel(
    mix_ref, halo_ref, taps_ref, raw_ref, bias_ref, rate_ref, dy_ref,
    bm_ref, cm_ref, dxi_ref, dsc_ref, h_ref, l_ref, run_ref, run_t_ref, sp_ref, sum_s_ref, sum_r_ref,
    pad, xm, scores, s_own, g_own, a_own, s_oth, g_oth, a_oth, s_out, g_out, a_out, s_in, g_in, a_in, g_mid,
    h_out, l_out, h_in, l_in, l_mid, h_oth, l_oth,
    x_send, x_recv, y_send, y_recv, z_send, z_recv, a_send, a_recv, s_send, s_recv, g_send, g_recv,
    gm_send, gm_recv, h_send, h_recv, l_send, l_recv, lm_send, lm_recv, p_send, p_recv, q_send, q_recv,
):
    dp = lax.axis_index("dp")
    ctx = lax.axis_index("ctx")
    core = lax.rem(ctx, 2)
    chip = ctx // 2
    z, y = chip // 4, lax.rem(chip, 4)
    chips = lax.axis_size("ctx") // 2
    own = HALF // chips
    other = ctx + 1 - 2 * core
    mine = core * HALF
    theirs = HALF - mine
    half_groups = GROUPS // 2
    shape = (ROWS, ROWS)
    first = core == 0

    def chip_at(r):
        return lax.rem(z + r // 4, 4) * 4 + lax.rem(y + r, 4)

    def chip_before(r):
        return lax.rem(z + 4 - r // 4, 4) * 4 + lax.rem(y + 4 - lax.rem(r, 4), 4)

    def tied(r):
        return (lax.rem(r, 4) == 2) | (r // 4 == 2)

    def below(r):
        return jnp.where(r // 4 == 2, 1, 0), jnp.where(lax.rem(r, 4) == 2, 1, 0)

    def mid_at(r):
        dz, dy = below(r)
        return lax.rem(z + 4 - dz, 4) * 4 + lax.rem(y + 4 - dy, 4)

    def mid_source(r):
        dz, dy = below(r)
        return lax.rem(z + dz, 4) * 4 + lax.rem(y + dy, 4)

    def mid_target(r):
        dz, dy = below(r)
        return lax.rem(z + dz + r // 4, 4) * 4 + lax.rem(y + dy + r, 4)

    barrier = pltpu.get_barrier_semaphore()
    pl.semaphore_signal(barrier, inc=1, device_id=(dp, other), device_id_type=MESH)

    def greet(r, _):
        pl.semaphore_signal(barrier, inc=1, device_id=(dp, chip_at(r) * 2 + core), device_id_type=MESH)
        return 0

    lax.fori_loop(1, chips, greet, 0)

    def remote(src, dst, send, recv, device):
        return pltpu.make_async_remote_copy(
            src_ref=src, dst_ref=dst, send_sem=send, recv_sem=recv, device_id=(dp, device), device_id_type=MESH
        )

    spread = softplus(raw_ref[...].astype(F32) + bias_ref[...])
    lower = jnp.where(iota(shape, 0) >= iota(shape, 1), 1.0, 0.0).astype(F32)
    running = dot(lower, spread * rate_ref[...], EXACT)
    sp_ref[...] = spread
    run_ref[...] = running
    run_t_ref[...] = running.T
    sum_s_ref[...] = jnp.zeros((ROWS, HEADS), F32)

    def mixed(slot, lanes):
        here = pad.at[slot]
        here[0:8, :] = halo_ref[:, lanes]
        here[8:, :] = mix_ref[:, lanes].astype(F32)
        pre = jnp.broadcast_to(taps_ref[4:5, lanes], (ROWS, 128))
        for k in range(KERNEL):
            pre = pre + taps_ref[k : k + 1, lanes] * here[5 + k : 5 + k + ROWS, :]
        return (pre * sigmoid(pre)).astype(BF16)

    def tile(start):
        return pl.ds(pl.multiple_of(start, 128), 128)

    def group_states(g):
        b16 = mixed(GROUP_PAIRS, tile(INNER + STATE * g))
        c16 = mixed(GROUP_PAIRS + 1, tile(INNER + GROUPS * STATE + STATE * g))
        bm_ref[g] = b16
        cm_ref[g] = c16
        scores[g] = jnp.where(iota(shape, 1) >= iota(shape, 0), dot_nt(b16, c16), 0.0)
        dsc_ref[g] = jnp.zeros(shape, F32)
        b_t = b16.astype(F32).T.astype(BF16)
        c_t = c16.astype(F32).T.astype(BF16)
        back = lax.rem(HEADS - GROUP_HEADS * g, HEADS)
        run = pltpu.roll(run_ref[...], back, 1)
        step = pltpu.roll(sp_ref[...], back, 1)
        closing = run[ROWS - 1 : ROWS, :]
        grown = jnp.exp(run)
        to_close = jnp.exp(closing - run) * step
        whole_decay = jnp.exp(closing)
        for j in range(GROUP_PAIRS):
            at = GROUP_PAIRS * g + j
            lanes = tile(GROUP_LANES * g + 128 * j)
            x16 = mixed(j, lanes)
            xm[:, lanes] = x16
            s_own[at] = dot(b_t, (x16.astype(F32) * pair_of(to_close, j)).astype(BF16)).astype(BF16)
            g_own[at] = dot(c_t, (dy_ref[:, lanes].astype(F32) * pair_of(grown, j)).astype(BF16)).astype(BF16)
            a_own[at] = pair_of(whole_decay, j)

    def swaps(i):
        here = pl.ds(i * GROUP_PAIRS, GROUP_PAIRS)
        there = pl.ds(theirs + i * GROUP_PAIRS, GROUP_PAIRS)
        return (
            remote(a_own.at[there], a_oth.at[here], x_send.at[i], x_recv.at[i], other),
            remote(s_own.at[there], s_oth.at[here], y_send.at[i], y_recv.at[i], other),
            remote(g_own.at[there], g_oth.at[here], z_send.at[i], z_recv.at[i], other),
        )

    def ordered(held, sent):
        return jnp.where(first, held, sent), jnp.where(first, sent, held)

    def decays(at):
        return ordered(a_own[pl.ds(mine + at, own)], a_oth[pl.ds(at, own)])

    def values(ref, oth, at):
        return ordered(ref[pl.ds(mine + at, own)].astype(F32), oth[pl.ds(at, own)].astype(F32))

    def small_copies(r):
        at = pl.ds(chip_at(r) * own, own)
        device = chip_at(r) * 2 + core
        return (
            remote(a_out.at[at], a_in.at[chip], a_send.at[r], a_recv.at[r], device),
            remote(s_out.at[at], s_in.at[chip], s_send.at[r], s_recv.at[r], device),
        )

    def g_copy(r):
        at = pl.ds(chip_at(r) * own, own)
        return remote(g_out.at[at], g_in.at[chip], g_send.at[r], g_recv.at[r], chip_at(r) * 2 + core)

    def g_lift(r):
        at = pl.ds(chip_at(r) * own, own)
        return remote(g_out.at[at], g_mid.at[r], g_send.at[r], gm_recv.at[r], mid_at(r) * 2 + core)

    def g_drop(r):
        return remote(g_mid.at[r], g_in.at[mid_source(r)], gm_send.at[r], g_recv.at[r], mid_target(r) * 2 + core)

    def h_copy(r):
        at = pl.ds(chip * own, own)
        return remote(h_out.at[chip_at(r)], h_in.at[at], h_send.at[r], h_recv.at[r], chip_at(r) * 2 + core)

    def l_copy(r):
        at = pl.ds(chip * own, own)
        return remote(l_out.at[chip_at(r)], l_in.at[at], l_send.at[r], l_recv.at[r], chip_at(r) * 2 + core)

    def l_lift(r):
        return remote(l_out.at[chip_at(r)], l_mid.at[r], l_send.at[r], lm_recv.at[r], mid_at(r) * 2 + core)

    def l_drop(r):
        at = pl.ds(mid_source(r) * own, own)
        return remote(l_mid.at[r], l_in.at[at], lm_send.at[r], l_recv.at[r], mid_target(r) * 2 + core)

    def go(r, direct, lifted):
        @pl.when(tied(r))
        def _():
            lifted(r).start()

        @pl.when(jnp.logical_not(tied(r)))
        def _():
            direct(r).start()

    def relay(lifted, dropped):
        def one(r, _):
            @pl.when(tied(r))
            def _():
                lifted(r).wait_recv()
                dropped(r).start()

            return 0

        lax.fori_loop(1, chips, one, 0)

    def group_theirs(i, _):
        group_states(theirs // GROUP_PAIRS + i)

        @pl.when(i == 0)
        def _():
            pl.semaphore_wait(barrier, chips)

        for copy in swaps(i):
            copy.start()
        return 0

    lax.fori_loop(0, half_groups, group_theirs, 0)

    def group_mine(k, _):
        i = lax.rem(z + k, half_groups)
        group_states(mine // GROUP_PAIRS + i)
        for copy in swaps(i):
            copy.wait_recv()

        def combine(d, _):
            r = k * 4 + d
            at = chip_at(r) * own
            a0, a1 = decays(at)
            s0, s1 = values(s_own, s_oth, at)
            g0, g1 = values(g_own, g_oth, at)
            here = pl.ds(at, own)
            a_out[here] = a0 * a1
            s_out[here] = (a1 * s0 + s1).astype(BF16)
            g_out[here] = (a0 * g1 + g0).astype(BF16)

            @pl.when(r > 0)
            def _():
                for copy in small_copies(r):
                    copy.start()
                go(r, g_copy, g_lift)

            return 0

        lax.fori_loop(0, 4, combine, 0)
        return 0

    lax.fori_loop(0, half_groups, group_mine, 0)
    at_own = pl.ds(chip * own, own)
    a_in[chip] = a_out[at_own]
    s_in[chip] = s_out[at_own]
    g_in[chip] = g_out[at_own]

    low = low_half(shape)

    def inside(jj, _):
        g = jj // GROUP_PAIRS
        lanes = tile(128 * jj)
        x16 = xm[:, lanes]
        dy = dy_ref[:, lanes].astype(F32)
        split = jnp.concatenate([jnp.where(low, dy, 0.0), jnp.where(low, 0.0, dy)], axis=0).astype(BF16)
        d_weights = dot_nt(x16, split)
        back = lax.rem(HEADS - 2 * jj, HEADS)
        run = pltpu.roll(run_ref[...], back, 1)
        steps = pltpu.roll(sp_ref[...], back, 1)
        score = scores[g]
        weights = []
        gathered = dsc_ref[g]
        sums = sum_s_ref[...]
        lane = iota(shape, 1)
        for i in range(2):
            at = 2 * jj + i
            step = steps[:, i : i + 1]
            d_weight = d_weights[:, 128 * i : 128 * i + 128]
            decay = jnp.exp(jnp.minimum(run_t_ref[pl.ds(at, 1), :] - run[:, i : i + 1], 0.0))
            plain = decay * score
            weights.append((plain * step).astype(BF16))
            product = d_weight * plain
            sums = jnp.where(lane == at, jnp.sum(product, axis=1, keepdims=True), sums)
            sum_r_ref[pl.ds(at, 1), :] = jnp.sum(product * step, axis=0, keepdims=True)
            gathered = gathered + d_weight * decay * step
        sum_s_ref[...] = sums
        dsc_ref[g] = gathered
        dxi_ref[:, lanes] = dot(jnp.concatenate(weights, axis=1), split).astype(BF16)
        return 0

    lax.fori_loop(0, EARLY, inside, 0)
    relay(g_lift, g_drop)
    lax.fori_loop(EARLY, MIDDLE, inside, 0)

    def arrived(r, _):
        for copy in small_copies(r):
            copy.wait_recv()
        g_copy(r).wait_recv()
        return 0

    lax.fori_loop(1, chips, arrived, 0)

    def forth(c, state):
        h_out[c] = state.astype(BF16)
        return a_in[c] * state + s_in[c].astype(F32)

    def back_again(i, state):
        c = chips - 1 - i
        l_out[c] = state.astype(BF16)
        return a_in[c] * state + g_in[c].astype(F32)

    zero = jnp.zeros((own, STATE, 128), F32)
    lax.fori_loop(0, chips, back_again, zero)

    def send_l(r, _):
        go(r, l_copy, l_lift)
        return 0

    lax.fori_loop(1, chips, send_l, 0)
    lax.fori_loop(0, chips, forth, zero)

    def send_h(r, _):
        h_copy(r).start()
        return 0

    lax.fori_loop(1, chips, send_h, 0)
    h_in[at_own] = h_out[chip]
    l_in[at_own] = l_out[chip]
    lax.fori_loop(MIDDLE, LATE, inside, 0)
    relay(l_lift, l_drop)
    lax.fori_loop(LATE, PAIRS, inside, 0)

    def swap_back(r):
        here = pl.ds(chip_before(r) * own, own)
        there = pl.ds(mine + chip_before(r) * own, own)
        return (
            remote(h_oth.at[here], h_ref.at[there], p_send.at[r], p_recv.at[r], other),
            remote(l_oth.at[here], l_ref.at[there], q_send.at[r], q_recv.at[r], other),
        )

    def finish(r, _):
        at = chip_before(r) * own

        @pl.when(r > 0)
        def _():
            h_copy(r).wait_recv()
            l_copy(r).wait_recv()

        here = pl.ds(at, own)
        held = pl.ds(mine + at, own)
        a0, a1 = decays(at)
        s0, _ = values(s_own, s_oth, at)
        _, g1 = values(g_own, g_oth, at)
        h0 = h_in[here]
        h1 = (a0 * h0.astype(F32) + s0).astype(BF16)
        l1 = l_in[here]
        l0 = (a1 * l1.astype(F32) + g1).astype(BF16)
        h_ref[held] = jnp.where(first, h0, h1)
        h_oth[here] = jnp.where(first, h1, h0)
        l_ref[held] = jnp.where(first, l0, l1)
        l_oth[here] = jnp.where(first, l1, l0)
        for copy in swap_back(r):
            copy.start()
        return 0

    lax.fori_loop(0, chips, finish, 0)

    def swapped(i, _):
        for copy in swaps(i):
            copy.wait_send()
        return 0

    lax.fori_loop(0, half_groups, swapped, 0)

    def sent(r, _):
        for copy in small_copies(r):
            copy.wait_send()
        g_copy(r).wait_send()
        h_copy(r).wait_send()
        l_copy(r).wait_send()

        @pl.when(tied(r))
        def _():
            g_drop(r).wait_send()
            l_drop(r).wait_send()

        return 0

    lax.fori_loop(1, chips, sent, 0)

    def settled(r, _):
        for copy in swap_back(r):
            copy.wait()
        return 0

    lax.fori_loop(0, chips, settled, 0)


def front(mixer, halo, taps, raw, bias, rate, dy):
    chips = lax.axis_size("ctx") // 2
    own = HALF // chips
    square = jax.ShapeDtypeStruct((ROWS, HEADS), F32)
    group = jax.ShapeDtypeStruct((GROUPS, ROWS, STATE), BF16)
    state = jax.ShapeDtypeStruct((PAIRS, STATE, 128), BF16)
    whole = pltpu.VMEM((PAIRS, STATE, 128), BF16)
    wide = pltpu.VMEM((HALF, STATE, 128), BF16)
    split = pltpu.VMEM((chips, own, STATE, 128), BF16)
    row = pltpu.VMEM((HALF, 1, 128), F32)
    few = pltpu.SemaphoreType.DMA((GROUPS // 2,))
    many = pltpu.SemaphoreType.DMA((chips,))
    memory = pl.BlockSpec(memory_space=pltpu.VMEM)
    return pl.pallas_call(
        front_kernel,
        out_shape=[
            group, group, jax.ShapeDtypeStruct((ROWS, INNER), BF16),
            jax.ShapeDtypeStruct((GROUPS, ROWS, ROWS), F32), state, state, square, square, square, square, square,
        ],
        in_specs=[memory] * 7,
        out_specs=[memory] * 11,
        scratch_shapes=[
            pltpu.VMEM((GROUP_PAIRS + 2, ROWS + 8, 128), F32), pltpu.VMEM((ROWS, INNER), BF16),
            pltpu.VMEM((GROUPS, ROWS, ROWS), F32),
            whole, whole, pltpu.VMEM((PAIRS, 1, 128), F32), wide, wide, row, wide, wide, row,
            split, split, pltpu.VMEM((chips, own, 1, 128), F32), split,
            split, split, wide, wide, split, wide, wide,
        ] + [few] * 6 + [many] * 18,
        compiler_params=pltpu.CompilerParams(
            collective_id=0, has_side_effects=True, vmem_limit_bytes=VMEM
        ),
        name="front",
    )(mixer, halo, taps, raw, bias, rate, dy)


def grads_kernel(
    x_ref, b_ref, c_ref, hx_ref, hb_ref, hc_ref, tx_ref, tb_ref, tc_ref, raw_ref, bias_ref, rate_ref, dy_ref,
    gain_ref, bm_ref, cm_ref, dxi_ref, dsc_ref, h_ref, l_ref, run_ref, sp_ref, sum_s_ref, sum_r_ref,
    ig_ref, last_ref, spill_ref, taps_out, step_ref, rows_ref,
    pad, dpad, acc_b, acc_c, col_u, col_q, row_g, full_u, full_q, full_g,
):
    g = pl.program_id(0)
    back = lax.rem(HEADS - GROUP_HEADS * g, HEADS)
    shape = (ROWS, ROWS)

    @pl.when(g == 0)
    def _():
        dpad[:, ROWS:, :] = jnp.zeros((GROUP_PAIRS + 2, 8, 128), F32)
        for ref in (full_u, full_q, full_g, col_u, col_q, row_g):
            ref[...] = jnp.zeros(ref.shape, F32)

    b16, c16 = bm_ref[0], cm_ref[0]
    run = pltpu.roll(run_ref[...], back, 1)
    spread = pltpu.roll(sp_ref[...], back, 1)
    grown = jnp.exp(run)
    to_close = jnp.exp(run[ROWS - 1 : ROWS, :] - run) * spread
    low = low_half(shape)
    low_row = low_half((1, 128))
    acc_b[...] = jnp.zeros(shape, F32)
    acc_c[...] = jnp.zeros(shape, F32)

    def conv_back(slot, grad, pre, gate, taps_ref, lanes, out):
        here = pad.at[slot]
        there = dpad.at[slot]
        dpre = grad * (gate * (1.0 + pre * (1.0 - gate)))
        there[0:ROWS, :] = dpre
        whole = jnp.zeros(shape, F32)
        for k in range(KERNEL):
            whole = whole + taps_ref[k : k + 1, lanes] * there[3 - k : 3 - k + ROWS, :]
            taps_out[k : k + 1, out] = jnp.sum(dpre * here[5 + k : 5 + k + ROWS, :], axis=0, keepdims=True)
        taps_out[4:5, out] = jnp.sum(dpre, axis=0, keepdims=True)
        taps_out[5:8, out] = jnp.zeros((3, 128), F32)
        ig_ref[:, out] = whole.astype(BF16)
        last_ref[:, out] = whole[ROWS - 8 :, :]
        head = dpre[0:8, :]
        row = iota((8, 128), 0)
        spilled = jnp.zeros((8, 128), F32)
        for k in range(KERNEL - 1):
            moved = pltpu.roll(head, 5 + k, 0)
            spilled = spilled + jnp.where(row >= 5 + k, taps_ref[k : k + 1, lanes] * moved, 0.0)
        spill_ref[:, out] = spilled

    for j in range(GROUP_PAIRS):
        lanes = pl.ds(128 * j, 128)
        pre = conv_pre(pad.at[j], x_ref, hx_ref, tx_ref, lanes)
        gate = sigmoid(pre)
        x = (pre * gate).astype(BF16).astype(F32)
        dy = dy_ref[:, lanes].astype(F32)
        h16, l16 = h_ref[j], l_ref[j]
        grown_2 = pair_of(grown, j)
        close_2 = pair_of(to_close, j)
        entered = dy * dot(c16, h16)
        left = dot(b16, l16)
        used = x * left
        for i in range(2):
            head = 2 * j + i
            mask = low if i == 0 else jnp.logical_not(low)
            mask_row = low_row if i == 0 else jnp.logical_not(low_row)
            col_u[:, head : head + 1] = jnp.sum(jnp.where(mask, entered, 0.0), axis=1, keepdims=True)
            col_q[:, head : head + 1] = jnp.sum(jnp.where(mask, used, 0.0), axis=1, keepdims=True)
            crossed = jnp.sum(h16.astype(F32) * l16.astype(F32), axis=0, keepdims=True)
            gained = jnp.sum(dy * x, axis=0, keepdims=True)
            row_g[0:1, head : head + 1] = jnp.sum(jnp.where(mask_row, crossed, 0.0), axis=1, keepdims=True)
            row_g[1:2, head : head + 1] = jnp.sum(jnp.where(mask_row, gained, 0.0), axis=1, keepdims=True)
        acc_c[...] += dot_nt((dy * grown_2).astype(BF16), h16)
        acc_b[...] += dot_nt((x * close_2).astype(BF16), l16)
        grad_x = dxi_ref[:, lanes].astype(F32) + close_2 * left + gain_ref[0, :, lanes] * dy
        conv_back(j, grad_x, pre, gate, tx_ref, lanes, pl.ds(pl.multiple_of(g * GROUP_LANES + 128 * j, 128), 128))

    d_scores = jnp.where(iota(shape, 1) >= iota(shape, 0), dsc_ref[0], 0.0)
    grad_b = acc_b[...] + dot(d_scores.astype(BF16), c16)
    grad_c = acc_c[...] + dot(d_scores.T.astype(BF16), b16)
    every = pl.ds(0, 128)
    for i, (grad, tile_ref, halo_ref, taps_ref) in enumerate(
        ((grad_b, b_ref, hb_ref, tb_ref), (grad_c, c_ref, hc_ref, tc_ref))
    ):
        pre = conv_pre(pad.at[GROUP_PAIRS + i], tile_ref, halo_ref, taps_ref, every)
        out = pl.ds(pl.multiple_of(INNER + GROUPS * STATE * i + 128 * g, 128), 128)
        conv_back(GROUP_PAIRS + i, grad, pre, sigmoid(pre), taps_ref, every, out)

    forward = lax.rem(GROUP_HEADS * g, HEADS)
    for whole_ref, part_ref in ((full_u, col_u), (full_q, col_q), (full_g, row_g)):
        lane = iota(part_ref.shape, 1)
        whole_ref[...] += pltpu.roll(jnp.where(lane < GROUP_HEADS, part_ref[...], 0.0), forward, 1)

    @pl.when(g == GROUPS - 1)
    def _():
        running, steps = run_ref[...], sp_ref[...]
        rate = rate_ref[...]
        closing = running[ROWS - 1 : ROWS, :]
        from_close = jnp.exp(closing - running)
        direct_q = from_close * full_q[...]
        used_q = direct_q * steps
        summed = sum_r_ref[...].T + jnp.exp(running) * full_u[...] - sum_s_ref[...] * steps - used_q
        upper = jnp.where(iota(shape, 1) >= iota(shape, 0), 1.0, 0.0).astype(F32)
        constant = jnp.sum(used_q, axis=0, keepdims=True) + jnp.exp(closing) * full_g[0:1, :]
        d_logs = dot(upper, summed, EXACT) + constant
        d_spread = (d_logs * rate + sum_s_ref[...] + direct_q).astype(BF16).astype(F32)
        step_grad = d_spread * sigmoid(raw_ref[...].astype(F32) + bias_ref[...])
        step_ref[...] = step_grad
        rows_ref[...] = jnp.zeros((8, HEADS), F32)
        rows_ref[0:1, :] = rate * jnp.sum(d_logs * steps, axis=0, keepdims=True)
        rows_ref[1:2, :] = jnp.sum(step_grad, axis=0, keepdims=True)
        rows_ref[2:3, :] = full_g[1:2, :]


def grads(mixer, halo, taps, raw, bias, rate, dy, gain, bm, cm, dxi, dsc, h, l, run, sp, sum_s, sum_r):
    x_spec = pl.BlockSpec((ROWS, GROUP_LANES), lambda g: (0, g))
    group_spec = pl.BlockSpec((1, ROWS, STATE), lambda g: (g, 0, 0))
    state_spec = pl.BlockSpec((GROUP_PAIRS, STATE, 128), lambda g: (g, 0, 0))
    square = full((ROWS, HEADS))
    plane = pltpu.VMEM((ROWS, 128), F32)
    tall = pltpu.VMEM((GROUP_PAIRS + 2, ROWS + 8, 128), F32)
    rows = pltpu.VMEM((8, 128), F32)
    edge = jax.ShapeDtypeStruct((8, CONV), F32)
    return pl.pallas_call(
        grads_kernel,
        grid=(GROUPS,),
        in_specs=channel_specs(ROWS) + channel_specs(8) + channel_specs(8)
        + [square, full((1, HEADS)), full((1, HEADS)), x_spec]
        + [pl.BlockSpec((1, 1, GROUP_LANES), lambda g: (g, 0, 0)), group_spec, group_spec, x_spec, group_spec]
        + [state_spec, state_spec, square, square, square, square],
        out_specs=[full((ROWS, CONV))] + [full((8, CONV))] * 3 + [square, full((8, HEADS))],
        out_shape=[
            jax.ShapeDtypeStruct((ROWS, CONV), BF16), edge, edge, edge,
            jax.ShapeDtypeStruct((ROWS, HEADS), F32), jax.ShapeDtypeStruct((8, HEADS), F32),
        ],
        scratch_shapes=[tall, tall] + [plane] * 4 + [rows] + [plane] * 2 + [rows],
        compiler_params=pltpu.CompilerParams(vmem_limit_bytes=VMEM),
        name="grads",
    )(
        mixer, mixer, mixer, halo, halo, halo, taps, taps, taps, raw, bias, rate, dy,
        gain, bm, cm, dxi, dsc, h, l, run, sp, sum_s, sum_r,
    )


def reduce_kernel(
    taps_ref, rows_ref, conv_ref, head_ref,
    taps_oth, rows_oth, shards, arrived, flat, packed, packed_in, total, total_oth,
    x_send, x_recv, d_send, d_recv, c_send, c_recv, o_send, o_recv,
):
    dp = lax.axis_index("dp")
    ctx = lax.axis_index("ctx")
    shard_count = lax.axis_size("dp")
    core = lax.rem(ctx, 2)
    chip = ctx // 2
    z, y = chip // 4, lax.rem(chip, 4)
    chips = lax.axis_size("ctx") // 2
    other = ctx + 1 - 2 * core
    width = total.shape[1]
    half = width // 2

    def chip_at(r):
        return lax.rem(z + r // 4, 4) * 4 + lax.rem(y + r, 4)

    def dp_at(r):
        return lax.rem(dp + r, shard_count)

    barrier = pltpu.get_barrier_semaphore()
    pl.semaphore_signal(barrier, inc=1, device_id=(dp, other), device_id_type=MESH)
    for r in range(1, shard_count):
        pl.semaphore_signal(barrier, inc=1, device_id=(dp_at(r), ctx), device_id_type=MESH)

    def greet(r, _):
        pl.semaphore_signal(barrier, inc=1, device_id=(dp, chip_at(r) * 2 + core), device_id_type=MESH)
        return 0

    lax.fori_loop(1, chips, greet, 0)
    pl.semaphore_wait(barrier, chips + shard_count - 1)

    def remote(src, dst, send, recv, d, c):
        return pltpu.make_async_remote_copy(
            src_ref=src, dst_ref=dst, send_sem=send, recv_sem=recv, device_id=(d, c), device_id_type=MESH
        )

    def columns(shard, part):
        return pl.ds(pl.multiple_of(shard * (2 * width) + part * width, 128), width)

    swaps = [
        remote(taps_ref.at[:, columns(i, 1 - core)], taps_oth.at[i], x_send.at[i], x_recv.at[i], dp, other)
        for i in range(shard_count)
    ]
    swaps.append(remote(rows_ref, rows_oth, x_send.at[shard_count], x_recv.at[shard_count], dp, other))
    for copy in swaps:
        copy.start()
    for copy in swaps:
        copy.wait()
    for i in range(shard_count):
        shards[i, :, 0:width] = taps_ref[:, columns(i, core)] + taps_oth[i]
        shards[i, :, width:] = rows_ref[...] + rows_oth[...]

    def shard_copy(r):
        return remote(shards.at[dp_at(r)], arrived.at[r], d_send.at[r], d_recv.at[r], dp_at(r), ctx)

    for r in range(1, shard_count):
        shard_copy(r).start()
    summed = shards[dp]
    for r in range(1, shard_count):
        shard_copy(r).wait()
        summed = summed + arrived[r]
    flat[0:4, 0:half] = summed[0:4, 0:half]
    flat[4:8, 0:half] = summed[0:4, half:width]
    flat[8:9, 0:half] = summed[4:5, 0:half]
    flat[9:10, 0:half] = summed[4:5, half:width]
    flat[10:16, 0:half] = jnp.zeros((6, half), F32)
    flat[0:8, half:] = summed[:, width:]
    flat[8:16, half:] = jnp.zeros((8, 128), F32)
    packed[...] = flat[...].astype(BF16)

    def chip_copy(r):
        return remote(packed, packed_in.at[r], c_send.at[r], c_recv.at[r], dp, chip_at(r) * 2 + core)

    def send(r, _):
        chip_copy(r).start()
        return 0

    def take(r, _):
        chip_copy(r).wait()
        flat[...] += packed_in[r].astype(F32)
        return 0

    lax.fori_loop(1, chips, send, 0)
    lax.fori_loop(1, chips, take, 0)
    total[0:4, 0:half] = flat[0:4, 0:half]
    total[0:4, half:] = flat[4:8, 0:half]
    total[4:5, 0:half] = flat[8:9, 0:half]
    total[4:5, half:] = flat[9:10, 0:half]
    total[5:8, :] = jnp.zeros((3, width), F32)
    last = remote(total, total_oth, o_send.at[0], o_recv.at[0], dp, other)
    last.start()
    head_ref[...] = pltpu.roll(flat[0:8, half:], lax.rem(HEADS - (HEADS // shard_count) * dp, HEADS), 1)
    conv_ref[:, pl.ds(pl.multiple_of(core * width, 128), width)] = total[...]
    last.wait()
    conv_ref[:, pl.ds(pl.multiple_of((1 - core) * width, 128), width)] = total_oth[...]


def reduce_params(taps_grad, rows):
    shards = lax.axis_size("dp")
    chips = lax.axis_size("ctx") // 2
    width = CONV // shards // 2
    memory = pl.BlockSpec(memory_space=pltpu.VMEM)
    dma = pltpu.SemaphoreType.DMA
    return pl.pallas_call(
        reduce_kernel,
        out_shape=[jax.ShapeDtypeStruct((8, 2 * width), F32), jax.ShapeDtypeStruct((8, HEADS), F32)],
        in_specs=[memory] * 2,
        out_specs=[memory] * 2,
        scratch_shapes=[
            pltpu.VMEM((shards, 8, width), F32), pltpu.VMEM((8, HEADS), F32),
            pltpu.VMEM((shards, 8, width + 128), F32), pltpu.VMEM((shards, 8, width + 128), F32),
            pltpu.VMEM((16, width // 2 + 128), F32), pltpu.VMEM((16, width // 2 + 128), BF16),
            pltpu.VMEM((chips, 16, width // 2 + 128), BF16),
            pltpu.VMEM((8, width), F32), pltpu.VMEM((8, width), F32),
            dma((shards + 1,)), dma((shards + 1,)), dma((shards,)), dma((shards,)),
            dma((chips,)), dma((chips,)), dma((1,)), dma((1,)),
        ],
        compiler_params=pltpu.CompilerParams(
            collective_id=1, has_side_effects=True, vmem_limit_bytes=VMEM
        ),
        name="reduce_params",
    )(taps_grad, rows)


def passed_along(value, axis, steps):
    count = lax.axis_size(axis)
    initial, last = (max(0, -steps), min(count, count - steps))
    return lax.ppermute(value, axis, [(source, source + steps) for source in range(initial, last)])


def local(mixer_input, step_raw, out_grad, conv_weight, conv_bias, step_bias, decay_log, skip_gain):
    mixer, raw, dy = mixer_input[0], step_raw[0], out_grad[0]
    halo = passed_along(mixer[ROWS - 8 :], "ctx", 1).astype(F32)
    taps = jnp.concatenate([conv_weight, conv_bias[None], jnp.zeros((3, CONV), F32)], axis=0)
    bias = step_bias[None]
    rate = -jnp.exp(decay_log)[None]
    gain = jnp.repeat(skip_gain, HEAD_DIM).reshape(GROUPS, 1, GROUP_LANES)
    bm, cm, dxi, dsc, h, l, run, _, sp, sum_s, sum_r = front(mixer, halo, taps, raw, bias, rate, dy)
    input_grad, last, spill, taps_grad, step_grad, rows = grads(
        mixer, halo, taps, raw, bias, rate, dy, gain, bm, cm, dxi, dsc, h, l, run, sp, sum_s, sum_r
    )
    spilled = passed_along(spill.astype(BF16), "ctx", -1).astype(F32)
    input_grad = lax.dynamic_update_slice(input_grad, (last + spilled).astype(BF16), (ROWS - 8, 0))
    factor = 1.0 / math.sqrt(lax.axis_size("dp") * ROWS * lax.axis_size("ctx"))
    conv_total, head_total = reduce_params(taps_grad, rows)
    return (
        input_grad[None],
        step_grad[None],
        conv_total[: KERNEL + 1] * factor,
        head_total[:2, : HEADS // lax.axis_size("dp")] * factor,
        head_total[2, : HEADS // lax.axis_size("dp")] * factor,
    )


def solution(mesh):
    spread = P("dp", "ctx", None)
    in_specs = (spread, spread, spread, P(), P(), P(), P(), P())
    out_specs = (spread, spread, P(None, "dp"), P(None, "dp"), P("dp"))
    return jax.shard_map(local, mesh=mesh, in_specs=in_specs, out_specs=out_specs, check_vma=False)
```

time: 346 us -> 153 us (0.44); the launches traced: 341 us -> 152 us
  blocking collectives: 124 us -> 0 us
  waiting for transfers between devices: 42.7 us -> 3.37 us
  between operations: 14.2 us -> 0.68 us
  local copies, waits for them, and re-layouts: 14.8 us -> 2.55 us
  other arithmetic: 4.16 us -> 10.3 us
  Pallas kernels: 135 us -> 129 us
    psum x1 -> x0, blocking collectives: 124 us -> none  [local(): conv_total, head_total = lax.psum((conv_share, head_share), 'ctx')]
    reduce_scatter x1 -> x0, waiting for transfers between devices: 21.5 us -> none  [local(): lax.psum_scatter(taps_grad[:KERNEL + 1], 'dp', scatter_dimension=1, tiled...]
    unnamed x3 -> x0, waiting for transfers between devices: 21.2 us -> none
    pallas_call x1, Pallas kernels: 41.6 us -> 23 us  [grads(): pl.pallas_call(grads_kernel, grid=(GROUPS,), in_specs=channel_specs(ROWS)...]
    pallas_call x2, Pallas kernels: 93 us -> 106 us  [the longest x1 84.9 us: front(): pl.pallas_call(front_kernel, out_shape=[group, group, jax.ShapeDtypeStruc...]
    unnamed x26 -> x0, local copies, waits for them, and re-layouts: 12.9 us -> none
  transfers between devices with their start and end apart: 4 -> 2, of which waited for: 2 -> 1; matrix products, arithmetic and copies ran while one was open for 1% -> 4% of each run, Pallas kernels for 0% -> 0%
where the time goes in v2:
time: 153 us; the launch traced here: 152 us
  Pallas kernels  129 us (84%)
  other arithmetic  10.3 us (7%)
  starting transfers between devices  6.67 us (4%)
  waiting for transfers between devices  3.37 us (2%)
  local copies, waits for them, and re-layouts  2.55 us (2%)
    pallas_call x1, Pallas kernels, front(): pl.pallas_call(front_kernel, out_shape=[group, group, jax.ShapeDtypeStruc...  84.9 us
    pallas_call x1, Pallas kernels, grads(): pl.pallas_call(grads_kernel, grid=(GROUPS,), in_specs=channel_specs(ROWS)...  23 us
    pallas_call x1, Pallas kernels, reduce_params(): pl.pallas_call(reduce_kernel, out_shape=[jax.ShapeDtypeStruct((8, 2 * wid...  21.1 us
    ppermute x2, starting transfers between devices, passed_along(): lax.ppermute(value, axis, [(source, source + steps) for source in range(i...  6.67 us
    ppermute x2, waiting for transfers between devices, passed_along(): lax.ppermute(value, axis, [(source, source + steps) for source in range(i...  3.37 us
  transfers between devices with their start and end apart: 2, of which 1 were waited for; matrix products, arithmetic and copies ran while one was open for 4% of the time, Pallas kernels for 0%

profile of v2, /device:TPU:1, one launch (start us, length us, event | category | flops | bytes accessed | tf_op | source)
XLA Modules:
  0.0 152.5 jit_solution(31372688626633285)
XLA Ops:
  0.6 0.9 slice_bitcast_fusion
  1.6 4.6 %collective-permute-start = (bf16[8,10240]{1,0:T(8,128)(2,1)S(1)}, bf16[8,10240]{1,0:T(8,128)(2,1)S(1)}, u32[]{:S(2)}, u32[]{:S(2)}) collective-permute-start(bf16[8,10240]{1,0:T(8,128)(2,1)S(1)} %slice_bitcast_fusion), channel_id=1, source_target_pairs={{0,1},{1,2},{2,3},{3,4},{4,5},{5,6},{6,7},{7,8},{8,9},{9,10},{10,1... | collective-permute-start | bytes 491528 | tf_op jit(solution)/shard_map/ppermute | solution.py:755
  6.2 0.7 broadcast_in_dim.28
  6.9 0.1 broadcast_in_dim.29
  7.0 0.7 broadcast_in_dim.30.gain_ref
  7.7 0.1 pad.2.clone
  7.8 1.8 %maximum_maximum_fusion.taps_ref.tx_ref.tb_ref.tc_ref = f32[8,10240]{1,0:T(8,128)} fusion(f32[1,10240]{1,0:T(1,128)} %bitcast.25, f32[4,10240]{1,0:T(4,128)} %param.11, f32[8]{0:T(128)S(1)} %pad.2.clone), kind=kLoop, calls=%fused_computation | loop fusion | flops 163840 | bytes 532512 | tf_op jit(solution)/shard_map/concatenate | solution.py:761
  9.6 1.2 negate_bitcast_fusion.rate_ref
  10.7 0.0 collective-permute-done
  10.7 0.7 convert_element_type.12.halo_ref.hx_ref.hb_ref.hc_ref
  11.5 84.9 %front.1 = (bf16[8,128,128]{2,1,0:T(8,128)(2,1)}, bf16[8,128,128]{2,1,0:T(8,128)(2,1)}, bf16[128,8192]{1,0:T(8,128)(2,1)}, f32[8,128,128]{2,1,0:T(8,128)}, bf16[...) custom-call(bf16[128,10240]{1,0:T(8,128)(2,1)} %bitcast.17, ...), custom_call_target="tpu_custom_call" | custom-call | tf_op jit(solution)/shard_map/front/pallas_call | solution.py:462
  96.3 23.0 %grads.1 = (bf16[128,10240]{1,0:T(8,128)(2,1)}, f32[8,10240]{1,0:T(8,128)}, f32[8,10240]{1,0:T(8,128)}, f32[8,10240]{1,0:T(8,128)}, f32[128,128]{1,0:T(8,128)}, /*index=5*/f32[8,128]{1,0:T(8,128)}) custom-call(bf16[128,10240]{1,0:T(8,128)(2,1)} %bitcast.18, bf16[128,10240]{1,0:T(8,128)(2,1)} %bitcast.19, bf16[128,10240]{1,0:T(8,128)(2,1)} %bitcast.20, ...), custom_call_target="tpu_custom_call" | custom-call | tf_op jit(solution)/shard_map/grads/pallas_call | solution.py:604
  119.3 21.1 %reduce_params.1 = (f32[8,2560]{1,0:T(8,128)}, f32[8,128]{1,0:T(8,128)}) custom-call(f32[8,10240]{1,0:T(8,128)} %get-tuple-element.37.taps_ref, f32[8,128]{1,0:T(8,128)} %get-tuple-element.38.rows_ref), custom_call_target="tpu_custom_call" | custom-call | tf_op jit(solution)/shard_map/reduce_params/pallas_call | solution.py:731
  140.4 1.5 %slice_multiply_fusion = f32[5,2560]{1,0:T(8,128)} fusion(f32[8,2560]{1,0:T(8,128)} %get-tuple-element.39), kind=kLoop, calls=%fused_computation.5 | loop fusion | flops 12800 | bytes 102400 | tf_op jit(solution)/shard_map/mul | solution.py:776
  141.9 1.2 slice_multiply_fusion.1
  143.2 1.0 convert_element_type.13
  144.2 2.1 %collective-permute-start.1 = (bf16[8,10240]{1,0:T(8,128)(2,1)S(1)}, bf16[8,10240]{1,0:T(8,128)(2,1)S(1)}, u32[]{:S(2)}, u32[]{:S(2)}) collective-permute-start(bf16[8,10240]{1,0:T(8,128)(2,1)S(1)} %convert_element_type.13), channel_id=1, source_target_pairs={{1,0},{2,1},{3,2},{4,3},{5,4},{6,5},{7,6},{8,7},{9,8},{10,9},{11,1... | collective-permute-start | bytes 491528 | tf_op jit(solution)/shard_map/ppermute | solution.py:755
  146.2 1.2 multiply_bitcast_fusion
  147.4 3.4 %collective-permute-done.1 = bf16[8,10240]{1,0:T(8,128)(2,1)S(1)} collective-permute-done((bf16[8,10240]{1,0:T(8,128)(2,1)S(1)}, bf16[8,10240]{1,0:T(8,128)(2,1)S(1)}, u32[]{:S(2)}, u32[]{:S(2)}) %collective-permute-start.1) | collective-permute-done | bytes 163872 | tf_op jit(solution)/shard_map/ppermute | solution.py:755
  150.8 1.7 %fusion.1 = bf16[1,128,10240]{2,1,0:T(8,128)(2,1)} fusion(bf16[1,128,10240]{2,1,0:T(8,128)(2,1)} %bitcast.28, f32[8,10240]{1,0:T(8,128)} %get-tuple-element.34, bf16[8,10240]{1,0:T(8,128)(2,1)S(1)} %collective-permute-done.1), kind=kLoop, calls=%fused_computation.3 | loop fusion | flops 245760 | bytes 655360 | tf_op jit(solution)/shard_map/dynamic_update_slice | solution.py:770
  (1 shorter events, 0.0 us)
Async XLA Ops:
  1.6 9.2 %collective-permute-start = (bf16[8,10240]{1,0:T(8,128)(2,1)S(1)}, bf16[8,10240]{1,0:T(8,128)(2,1)S(1)}, u32[]{:S(2)}, u32[]{:S(2)}) collective-permute-start(bf16[8,10240]{1,0:T(8,128)(2,1)S(1)} %slice_bitcast_fusion), channel_id=1, source_target_pairs={{0,1},{1,2},{2,3},{3,4},{4,5},{5,6},{6,7},{7,8},{8,9},{9,10},{10,1... | collective-permute-start | bytes 491528 | tf_op jit(solution)/shard_map/ppermute | solution.py:755
  144.2 6.6 %collective-permute-start.1 = (bf16[8,10240]{1,0:T(8,128)(2,1)S(1)}, bf16[8,10240]{1,0:T(8,128)(2,1)S(1)}, u32[]{:S(2)}, u32[]{:S(2)}) collective-permute-start(bf16[8,10240]{1,0:T(8,128)(2,1)S(1)} %convert_element_type.13), channel_id=1, source_target_pairs={{1,0},{2,1},{3,2},{4,3},{5,4},{6,5},{7,6},{8,7},{9,8},{10,9},{11,1... | collective-permute-start | bytes 491528 | tf_op jit(solution)/shard_map/ppermute | solution.py:755

commit v3 on v0

v3 whole, which is shorter than its diff:
```python
import functools
import math

import jax
import jax.numpy as jnp
from jax import lax
from jax.experimental import pallas as pl
from jax.experimental.pallas import tpu as pltpu
from jax.sharding import PartitionSpec as P

HEADS = 128
HEAD_DIM = 64
STATE = 128
GROUPS = 8
KERNEL = 4
ROWS = 128
INNER = 8192
CONV = 10240
GROUP_HEADS = HEADS // GROUPS
GROUP_PAIRS = GROUP_HEADS // 2
GROUP_LANES = GROUP_HEADS * HEAD_DIM
PAIRS = HEADS // 2
HALF = PAIRS // 2
MESH = pl.DeviceIdType.MESH
F32 = jnp.float32
BF16 = jnp.bfloat16
VMEM = 60 << 20
BATCHES = 4
BLOCK_ROWS = 64
FIRST, SLICE = 6, 14
EXACT = lax.Precision.HIGHEST


def dot(a, b, precision=None):
    return jnp.dot(a, b, precision=precision, preferred_element_type=F32)


def dot_nt(a, b):
    return lax.dot_general(a, b, (((1,), (1,)), ((), ())), preferred_element_type=F32)


def sigmoid(v):
    return 0.5 + 0.5 * jnp.tanh(0.5 * v)


def softplus(v):
    return jnp.maximum(v, 0.0) + jnp.log1p(jnp.exp(-jnp.abs(v)))


def iota(shape, dim):
    return lax.broadcasted_iota(jnp.int32, shape, dim)


def low_half(shape):
    return iota(shape, len(shape) - 1) < HEAD_DIM


def pair_of(columns, j):
    shape = (columns.shape[0], 2 * HEAD_DIM)
    first = jnp.broadcast_to(columns[:, 2 * j : 2 * j + 1], shape)
    second = jnp.broadcast_to(columns[:, 2 * j + 1 : 2 * j + 2], shape)
    return jnp.where(low_half(shape), first, second)


def mixer_kernel(
    mix_ref, halo_ref, weight_ref, shift_ref, raw_ref, bias_ref, decay_ref, gain_ref, dy_ref,
    ig_ref, step_ref, conv_ref, head_ref,
    run_ref, run_t_ref, sp_ref, close_own, close_oth, close_out, close_in, decay_own, decay_oth, decay_in, pad, dpad,
    xm, bm, cm, scores, dxi, dsc, sum_s, sum_r, s_own, g_own, s_oth, g_oth, sg_out, sg_in, hl_out, hl_in,
    h_all, l_all, h_oth, l_oth, acc_b, acc_c, col_u, col_q, row_g, full_u, full_q, full_g,
    last, spill, spill_in, taps, rows, taps_oth, rows_oth, shards, arrived, flat, packed, packed_in, total, total_oth,
    e_send, e_recv, k_send, k_recv, x_send, x_recv, y_send, y_recv, sg_send, sg_recv, hl_send, hl_recv,
    p_send, p_recv, q_send, q_recv, sp_send, sp_recv, t_send, t_recv, d_send, d_recv, c_send, c_recv, o_send, o_recv,
):
    dp = lax.axis_index("dp")
    ctx = lax.axis_index("ctx")
    shard_count = lax.axis_size("dp")
    devices = lax.axis_size("ctx")
    core = lax.rem(ctx, 2)
    chip = ctx // 2
    z, y = chip // 4, lax.rem(chip, 4)
    chips = devices // 2
    other = ctx + 1 - 2 * core
    beyond = lax.rem(ctx + devices - 1 + 2 * core, devices)
    half_blocks = HALF * STATE // BLOCK_ROWS
    mine = core * half_blocks
    half_groups = GROUPS // 2
    mine_group = core * half_groups
    theirs_group = half_groups - mine_group
    shape = (ROWS, ROWS)
    first = core == 0
    low = low_half(shape)
    low_row = low_half((1, 128))

    def chip_at(r):
        return lax.rem(z + r // 4, 4) * 4 + lax.rem(y + r, 4)

    def chip_before(r):
        return lax.rem(z + 4 - r // 4, 4) * 4 + lax.rem(y + 4 - lax.rem(r, 4), 4)

    def dp_at(r):
        return lax.rem(dp + r, shard_count)

    barrier = pltpu.get_barrier_semaphore()
    for device in (other, beyond):
        pl.semaphore_signal(barrier, inc=1, device_id=(dp, device), device_id_type=MESH)
    for r in range(1, shard_count):
        pl.semaphore_signal(barrier, inc=1, device_id=(dp_at(r), ctx), device_id_type=MESH)

    def greet(r, _):
        pl.semaphore_signal(barrier, inc=1, device_id=(dp, chip_at(r) * 2 + core), device_id_type=MESH)
        return 0

    lax.fori_loop(1, chips, greet, 0)

    def remote(src, dst, send, recv, device, d=None):
        return pltpu.make_async_remote_copy(
            src_ref=src, dst_ref=dst, send_sem=send, recv_sem=recv,
            device_id=(dp if d is None else d, device), device_id_type=MESH,
        )

    def tile(start):
        return pl.ds(pl.multiple_of(start, 128), 128)

    rate = -jnp.exp(decay_ref[...])
    spread = softplus(raw_ref[...].astype(F32) + bias_ref[...])
    lower = jnp.where(iota(shape, 0) >= iota(shape, 1), 1.0, 0.0).astype(F32)
    running = dot(lower, spread * rate, EXACT)
    sp_ref[...] = spread
    run_ref[...] = running
    run_t_ref[...] = running.T
    close_own[...] = jnp.broadcast_to(running[ROWS - 1 : ROWS, :], (8, HEADS))
    sum_s[...] = jnp.zeros((ROWS, HEADS), F32)

    def conv_pre(slot, lanes):
        here = pad.at[slot]
        here[0:8, :] = halo_ref[:, lanes].astype(F32)
        here[8:, :] = mix_ref[:, lanes].astype(F32)
        pre = jnp.broadcast_to(shift_ref[:, lanes], (ROWS, 128))
        for k in range(KERNEL):
            pre = pre + weight_ref[k : k + 1, lanes] * here[5 + k : 5 + k + ROWS, :]
        return pre

    def mixed(slot, lanes):
        pre = conv_pre(slot, lanes)
        return (pre * sigmoid(pre)).astype(BF16)

    def group_states(g):
        b16 = mixed(GROUP_PAIRS, tile(INNER + STATE * g))
        c16 = mixed(GROUP_PAIRS + 1, tile(INNER + GROUPS * STATE + STATE * g))
        bm[g] = b16
        cm[g] = c16
        scores[g] = jnp.where(iota(shape, 1) >= iota(shape, 0), dot_nt(b16, c16), 0.0)
        dsc[g] = jnp.zeros(shape, F32)
        b_t = b16.astype(F32).T.astype(BF16)
        c_t = c16.astype(F32).T.astype(BF16)
        back = lax.rem(HEADS - GROUP_HEADS * g, HEADS)
        run = pltpu.roll(run_ref[...], back, 1)
        step = pltpu.roll(sp_ref[...], back, 1)
        grown = jnp.exp(run)
        to_close = jnp.exp(run[ROWS - 1 : ROWS, :] - run) * step
        for j in range(GROUP_PAIRS):
            at = pl.ds(2 * (GROUP_PAIRS * g + j), 2)
            lanes = tile(GROUP_LANES * g + 128 * j)
            x16 = mixed(j, lanes)
            xm[:, lanes] = x16
            state = dot(b_t, (x16.astype(F32) * pair_of(to_close, j)).astype(BF16))
            s_own[at] = state.astype(BF16).reshape(2, BLOCK_ROWS, 128)
            state = dot(c_t, (dy_ref[:, lanes].astype(F32) * pair_of(grown, j)).astype(BF16))
            g_own[at] = state.astype(BF16).reshape(2, BLOCK_ROWS, 128)

    def batch(i):
        return pl.ds(i * chips, chips)

    def swaps(i):
        there = pl.ds(half_blocks - mine + i * chips, chips)
        return (
            remote(s_own.at[there], s_oth.at[batch(i)], x_send.at[i], x_recv.at[i], other),
            remote(g_own.at[there], g_oth.at[batch(i)], y_send.at[i], y_recv.at[i], other),
        )

    def swap_back(i):
        there = pl.ds(mine + i * chips, chips)
        return (
            remote(h_oth.at[batch(i)], h_all.at[there], p_send.at[i], p_recv.at[i], other),
            remote(l_oth.at[batch(i)], l_all.at[there], q_send.at[i], q_recv.at[i], other),
        )

    close_swap = remote(close_own, close_oth, e_send.at[0], e_recv.at[0], other)

    def close_copy(r):
        return remote(close_out, close_in.at[chip], k_send.at[r], k_recv.at[r], chip_at(r) * 2 + core)

    def sg_copy(i, r):
        q = chip_at(r)
        return remote(sg_out.at[i, q], sg_in.at[i, chip], sg_send.at[i, r], sg_recv.at[i, r], q * 2 + core)

    def hl_copy(i, r):
        q = chip_at(r)
        return remote(hl_out.at[i, q], hl_in.at[i, chip], hl_send.at[i, r], hl_recv.at[i, r], q * 2 + core)

    def ordered(held, sent):
        return jnp.where(first, held, sent), jnp.where(first, sent, held)

    def spread_pairs(closing, pairs):
        head = iota(closing.shape, 1)
        picked = jnp.where(head // 2 == pairs, closing, 0.0)
        shape = (HEADS, 128)
        lanes = jnp.where(lax.rem(iota(shape, 0), 2) == iota(shape, 1) // HEAD_DIM, 1.0, 0.0).astype(F32)
        return jnp.exp(dot(picked, lanes, EXACT))

    def held_decays(closing_ref):
        pairs = core * HALF + iota((HALF, HEADS), 0)
        return spread_pairs(jnp.broadcast_to(closing_ref[0:1, :], (HALF, HEADS)), pairs)

    def values(ref, oth, b):
        return ordered(ref[mine + b].astype(F32), oth[b].astype(F32))

    def both_decays(b):
        row = pl.ds(b // 2, 1)
        return ordered(decay_own[row, :], decay_oth[row, :])

    def build(u, _):
        i = u // 2
        theirs = lax.rem(u, 2) == 0
        group_states(jnp.where(theirs, theirs_group, mine_group) + i)

        @pl.when(u == 0)
        def _():
            pl.semaphore_wait(barrier, chips + shard_count)
            close_swap.start()

        @pl.when(theirs)
        def _():
            for copy in swaps(i):
                copy.start()

        @pl.when(u == 1)
        def _():
            close_swap.wait_recv()
            close_out[...] = close_own[...] + close_oth[...]
            decay_own[...] = held_decays(close_own)
            decay_oth[...] = held_decays(close_oth)
            close_in[chip] = close_out[...]

            def send(r, _):
                close_copy(r).start()
                return 0

            lax.fori_loop(1, chips, send, 0)

        @pl.when(jnp.logical_not(theirs))
        def _():
            for copy in swaps(i):
                copy.wait_recv()

            def combine(r, _):
                q = chip_at(r)
                b = chips * i + q
                a0, a1 = both_decays(b)
                s0, s1 = values(s_own, s_oth, b)
                g0, g1 = values(g_own, g_oth, b)
                sg_out[i, q, 0] = (a1 * s0 + s1).astype(BF16)
                sg_out[i, q, 1] = (a0 * g1 + g0).astype(BF16)

                @pl.when(r > 0)
                def _():
                    sg_copy(i, r).start()

                return 0

            lax.fori_loop(0, chips, combine, 0)
            sg_in[i, chip] = sg_out[i, chip]

        return 0

    lax.fori_loop(0, 2 * BATCHES, build, 0)

    def inside(jj, _):
        g = jj // GROUP_PAIRS
        lanes = tile(128 * jj)
        x16 = xm[:, lanes]
        dy = dy_ref[:, lanes].astype(F32)
        split = jnp.concatenate([jnp.where(low, dy, 0.0), jnp.where(low, 0.0, dy)], axis=0).astype(BF16)
        d_weights = dot_nt(x16, split)
        back = lax.rem(HEADS - 2 * jj, HEADS)
        run = pltpu.roll(run_ref[...], back, 1)
        steps = pltpu.roll(sp_ref[...], back, 1)
        score = scores[g]
        weights = []
        gathered = dsc[g]
        sums = sum_s[...]
        lane = iota(shape, 1)
        for i in range(2):
            at = 2 * jj + i
            step = steps[:, i : i + 1]
            d_weight = d_weights[:, 128 * i : 128 * i + 128]
            decay = jnp.exp(jnp.minimum(run_t_ref[pl.ds(at, 1), :] - run[:, i : i + 1], 0.0))
            plain = decay * score
            weights.append((plain * step).astype(BF16))
            product = d_weight * plain
            sums = jnp.where(lane == at, jnp.sum(product, axis=1, keepdims=True), sums)
            sum_r[pl.ds(at, 1), :] = jnp.sum(product * step, axis=0, keepdims=True)
            gathered = gathered + d_weight * decay * step
        sum_s[...] = sums
        dsc[g] = gathered
        dxi[:, lanes] = dot(jnp.concatenate(weights, axis=1), split).astype(BF16)
        return 0

    def scan(i):
        def arrive(r, _):
            @pl.when(i == 0)
            def _():
                close_copy(r).wait_recv()

            sg_copy(i, r).wait_recv()
            return 0

        lax.fori_loop(1, chips, arrive, 0)
        decay_in[...] = spread_pairs(close_in[:, 0, :], (mine + chips * i + chip) // 2)

        def both(c, states):
            forth, back = states
            d = chips - 1 - c
            hl_out[i, c, 0] = forth.astype(BF16)
            hl_out[i, d, 1] = back.astype(BF16)
            forth = decay_in[pl.ds(c, 1), :] * forth + sg_in[i, c, 0].astype(F32)
            back = decay_in[pl.ds(d, 1), :] * back + sg_in[i, d, 1].astype(F32)
            return forth, back

        zero = jnp.zeros((BLOCK_ROWS, 128), F32)
        lax.fori_loop(0, chips, both, (zero, zero), unroll=4)

        def send(r, _):
            hl_copy(i, r).start()
            return 0

        lax.fori_loop(1, chips, send, 0)
        hl_in[i, chip] = hl_out[i, chip]

    def middle(i, _):
        lax.fori_loop(jnp.maximum(SLICE * (i - 1) + FIRST, 0), SLICE * i + FIRST, inside, 0)
        scan(i)
        return 0

    lax.fori_loop(0, BATCHES, middle, 0)
    lax.fori_loop(SLICE * (BATCHES - 1) + FIRST, PAIRS, inside, 0)

    dpad[:, ROWS:, :] = jnp.zeros((GROUP_PAIRS + 2, 8, 128), F32)
    taps[...] = jnp.zeros(taps.shape, F32)
    for ref in (full_u, full_q, full_g, col_u, col_q, row_g):
        ref[...] = jnp.zeros(ref.shape, F32)

    def conv_back(slot, grad, pre, gate, lanes):
        here = pad.at[slot]
        there = dpad.at[slot]
        dpre = grad * (gate * (1.0 + pre * (1.0 - gate)))
        there[0:ROWS, :] = dpre
        whole = jnp.zeros(shape, F32)
        for k in range(KERNEL):
            whole = whole + weight_ref[k : k + 1, lanes] * there[3 - k : 3 - k + ROWS, :]
            taps[k : k + 1, lanes] = jnp.sum(dpre * here[5 + k : 5 + k + ROWS, :], axis=0, keepdims=True)
        taps[4:5, lanes] = jnp.sum(dpre, axis=0, keepdims=True)
        ig_ref[:, lanes] = whole.astype(BF16)
        last[:, lanes] = whole[ROWS - 16 :, :]
        edge = dpre[0:8, :]
        row = iota((8, 128), 0)
        spilled = jnp.zeros((8, 128), F32)
        for k in range(KERNEL - 1):
            moved = pltpu.roll(edge, 5 + k, 0)
            spilled = spilled + jnp.where(row >= 5 + k, weight_ref[k : k + 1, lanes] * moved, 0.0)
        spill[:, lanes] = spilled

    before = lax.rem(ctx + devices - 1, devices)

    def spill_copies(g):
        parts = (
            pl.ds(pl.multiple_of(GROUP_LANES * g, 128), GROUP_LANES),
            tile(INNER + STATE * g),
            tile(INNER + GROUPS * STATE + STATE * g),
        )
        return [
            remote(spill.at[:, lanes], spill_in.at[:, lanes], sp_send.at[g, n], sp_recv.at[g, n], before)
            for n, lanes in enumerate(parts)
        ]

    def group_grads(g):
        back = lax.rem(HEADS - GROUP_HEADS * g, HEADS)
        b16, c16 = bm[g], cm[g]
        run = pltpu.roll(run_ref[...], back, 1)
        step = pltpu.roll(sp_ref[...], back, 1)
        gain = pltpu.roll(jnp.broadcast_to(gain_ref[...], (8, HEADS)), back, 1)
        grown = jnp.exp(run)
        to_close = jnp.exp(run[ROWS - 1 : ROWS, :] - run) * step
        acc_b[...] = jnp.zeros(shape, F32)
        acc_c[...] = jnp.zeros(shape, F32)
        for j in range(GROUP_PAIRS):
            lanes = tile(GROUP_LANES * g + 128 * j)
            at = pl.ds(2 * (GROUP_PAIRS * g + j), 2)
            pre = conv_pre(j, lanes)
            gate = sigmoid(pre)
            x = xm[:, lanes].astype(F32)
            dy = dy_ref[:, lanes].astype(F32)
            h16 = h_all[at].reshape(STATE, 128)
            l16 = l_all[at].reshape(STATE, 128)
            close_2 = pair_of(to_close, j)
            entered = dy * dot(c16, h16)
            left = dot(b16, l16)
            used = x * left
            crossed = jnp.sum(h16.astype(F32) * l16.astype(F32), axis=0, keepdims=True)
            gained = jnp.sum(dy * x, axis=0, keepdims=True)
            for i in range(2):
                head = 2 * j + i
                mask = low if i == 0 else jnp.logical_not(low)
                mask_row = low_row if i == 0 else jnp.logical_not(low_row)
                col_u[:, head : head + 1] = jnp.sum(jnp.where(mask, entered, 0.0), axis=1, keepdims=True)
                col_q[:, head : head + 1] = jnp.sum(jnp.where(mask, used, 0.0), axis=1, keepdims=True)
                row_g[0:1, head : head + 1] = jnp.sum(jnp.where(mask_row, crossed, 0.0), axis=1, keepdims=True)
                row_g[1:2, head : head + 1] = jnp.sum(jnp.where(mask_row, gained, 0.0), axis=1, keepdims=True)
            acc_c[...] += dot_nt((dy * pair_of(grown, j)).astype(BF16), h16)
            acc_b[...] += dot_nt((x * close_2).astype(BF16), l16)
            grad_x = dxi[:, lanes].astype(F32) + close_2 * left + pair_of(gain, j)[0:1, :] * dy
            conv_back(j, grad_x, pre, gate, lanes)
        d_scores = jnp.where(iota(shape, 1) >= iota(shape, 0), dsc[g], 0.0)
        grad_b = acc_b[...] + dot(d_scores.astype(BF16), c16)
        grad_c = acc_c[...] + dot(d_scores.T.astype(BF16), b16)
        for i, grad in enumerate((grad_b, grad_c)):
            lanes = tile(INNER + GROUPS * STATE * i + STATE * g)
            pre = conv_pre(GROUP_PAIRS + i, lanes)
            conv_back(GROUP_PAIRS + i, grad, pre, sigmoid(pre), lanes)
        forward = lax.rem(GROUP_HEADS * g, HEADS)
        for whole_ref, part_ref in ((full_u, col_u), (full_q, col_q), (full_g, row_g)):
            lane = iota(part_ref.shape, 1)
            whole_ref[...] += pltpu.roll(jnp.where(lane < GROUP_HEADS, part_ref[...], 0.0), forward, 1)

        @pl.when(ctx > 0)
        def _():
            for copy in spill_copies(g):
                copy.start()

    def gather(i):
        def finish(r, _):
            q = chip_before(r)

            @pl.when(r > 0)
            def _():
                hl_copy(i, r).wait_recv()

            b = chips * i + q
            a0, a1 = both_decays(b)
            s0, _ = values(s_own, s_oth, b)
            _, g1 = values(g_own, g_oth, b)
            h0 = hl_in[i, q, 0]
            h1 = (a0 * h0.astype(F32) + s0).astype(BF16)
            l1 = hl_in[i, q, 1]
            l0 = (a1 * l1.astype(F32) + g1).astype(BF16)
            h_all[mine + b] = jnp.where(first, h0, h1)
            h_oth[b] = jnp.where(first, h1, h0)
            l_all[mine + b] = jnp.where(first, l0, l1)
            l_oth[b] = jnp.where(first, l1, l0)
            return 0

        lax.fori_loop(0, chips, finish, 0)
        for copy in swap_back(i):
            copy.start()

    def outer(u, _):
        i = u // 2
        held = lax.rem(u, 2) == 0

        @pl.when(held)
        def _():
            gather(i)

        @pl.when(jnp.logical_not(held))
        def _():
            for copy in swap_back(i):
                copy.wait_recv()

        group_grads(jnp.where(held, mine_group, theirs_group) + i)
        return 0

    lax.fori_loop(0, 2 * BATCHES, outer, 0)

    closing = run_ref[ROWS - 1 : ROWS, :]
    running = run_ref[...]
    steps = sp_ref[...]
    direct_q = jnp.exp(closing - running) * full_q[...]
    used_q = direct_q * steps
    summed = sum_r[...].T + jnp.exp(running) * full_u[...] - sum_s[...] * steps - used_q
    upper = jnp.where(iota(shape, 1) >= iota(shape, 0), 1.0, 0.0).astype(F32)
    constant = jnp.sum(used_q, axis=0, keepdims=True) + jnp.exp(closing) * full_g[0:1, :]
    d_logs = dot(upper, summed, EXACT) + constant
    d_spread = (d_logs * (-jnp.exp(decay_ref[...])) + sum_s[...] + direct_q).astype(BF16).astype(F32)
    step_grad = d_spread * sigmoid(raw_ref[...].astype(F32) + bias_ref[...])
    step_ref[...] = step_grad
    rows[...] = jnp.zeros((8, HEADS), F32)
    rows[0:1, :] = -jnp.exp(decay_ref[...]) * jnp.sum(d_logs * steps, axis=0, keepdims=True)
    rows[1:2, :] = jnp.sum(step_grad, axis=0, keepdims=True)
    rows[2:3, :] = full_g[1:2, :]

    width = total.shape[1]
    half = width // 2

    def columns(shard, part):
        return pl.ds(pl.multiple_of(shard * (2 * width) + part * width, 128), width)

    sums = [
        remote(taps.at[:, columns(i, 1 - core)], taps_oth.at[i], t_send.at[i], t_recv.at[i], other)
        for i in range(shard_count)
    ]
    sums.append(remote(rows, rows_oth, t_send.at[shard_count], t_recv.at[shard_count], other))
    for copy in sums:
        copy.start()
    for copy in sums:
        copy.wait()
    for i in range(shard_count):
        shards[i, :, 0:width] = taps[:, columns(i, core)] + taps_oth[i]
        shards[i, :, width:] = rows[...] + rows_oth[...]

    def shard_copy(r):
        return remote(shards.at[dp_at(r)], arrived.at[r], d_send.at[r], d_recv.at[r], ctx, dp_at(r))

    for r in range(1, shard_count):
        shard_copy(r).start()

    @pl.when(ctx < devices - 1)
    def _():
        def landed(g, _):
            for copy in spill_copies(g):
                copy.wait_recv()
            return 0

        lax.fori_loop(0, GROUPS, landed, 0)
        last[8:16, :] += spill_in[...]

    ig_ref[ROWS - 16 :, :] = last[...].astype(BF16)

    summed = shards[dp]
    for r in range(1, shard_count):
        shard_copy(r).wait()
        summed = summed + arrived[r]
    flat[0:4, 0:half] = summed[0:4, 0:half]
    flat[4:8, 0:half] = summed[0:4, half:width]
    flat[8:9, 0:half] = summed[4:5, 0:half]
    flat[9:10, 0:half] = summed[4:5, half:width]
    flat[10:16, 0:half] = jnp.zeros((6, half), F32)
    flat[0:8, half:] = summed[:, width:]
    flat[8:16, half:] = jnp.zeros((8, 128), F32)
    packed[...] = flat[...].astype(BF16)

    def chip_copy(r):
        return remote(packed, packed_in.at[r], c_send.at[r], c_recv.at[r], chip_at(r) * 2 + core)

    def send(r, _):
        chip_copy(r).start()
        return 0

    lax.fori_loop(1, chips, send, 0)

    close_swap.wait_send()

    def cleared(i, _):
        for copy in swaps(i) + swap_back(i):
            copy.wait_send()

        def sent(r, _):
            @pl.when(i == 0)
            def _():
                close_copy(r).wait_send()

            sg_copy(i, r).wait_send()
            hl_copy(i, r).wait_send()
            return 0

        lax.fori_loop(1, chips, sent, 0)
        return 0

    lax.fori_loop(0, BATCHES, cleared, 0)

    @pl.when(ctx > 0)
    def _():
        def left_here(g, _):
            for copy in spill_copies(g):
                copy.wait_send()
            return 0

        lax.fori_loop(0, GROUPS, left_here, 0)

    def take(r, _):
        chip_copy(r).wait()
        flat[...] += packed_in[r].astype(F32)
        return 0

    lax.fori_loop(1, chips, take, 0)
    total[0:4, 0:half] = flat[0:4, 0:half]
    total[0:4, half:] = flat[4:8, 0:half]
    total[4:5, 0:half] = flat[8:9, 0:half]
    total[4:5, half:] = flat[9:10, 0:half]
    total[5:8, :] = jnp.zeros((3, width), F32)
    final = remote(total, total_oth, o_send.at[0], o_recv.at[0], other)
    final.start()
    head_ref[...] = pltpu.roll(flat[0:8, half:], lax.rem(HEADS - (HEADS // shard_count) * dp, HEADS), 1)
    conv_ref[:, pl.ds(pl.multiple_of(core * width, 128), width)] = total[...]
    final.wait()
    conv_ref[:, pl.ds(pl.multiple_of((1 - core) * width, 128), width)] = total_oth[...]


def mixer_grads(mixer, halo, weight, shift, raw, bias, decay, gain, dy):
    chips = lax.axis_size("ctx") // 2
    shards = lax.axis_size("dp")
    width = CONV // shards // 2
    V = pltpu.VMEM
    dma = pltpu.SemaphoreType.DMA
    blocks = PAIRS * STATE // BLOCK_ROWS
    plane = V((ROWS, HEADS), F32)
    row = V((8, HEADS), F32)
    tall = V((GROUP_PAIRS + 2, ROWS + 8, 128), F32)
    group16 = V((GROUPS, ROWS, STATE), BF16)
    group32 = V((GROUPS, ROWS, ROWS), F32)
    inner = V((ROWS, INNER), BF16)
    whole = V((blocks, BLOCK_ROWS, 128), BF16)
    part = V((blocks // 2, BLOCK_ROWS, 128), BF16)
    sent = V((BATCHES, chips, 2, BLOCK_ROWS, 128), BF16)
    edge = V((8, CONV), F32)
    memory = pl.BlockSpec(memory_space=pltpu.VMEM)
    return pl.pallas_call(
        mixer_kernel,
        out_shape=[
            jax.ShapeDtypeStruct((ROWS, CONV), BF16), jax.ShapeDtypeStruct((ROWS, HEADS), F32),
            jax.ShapeDtypeStruct((8, 2 * width), F32), jax.ShapeDtypeStruct((8, HEADS), F32),
        ],
        in_specs=[memory] * 9,
        out_specs=[memory] * 4,
        scratch_shapes=[
            plane, plane, plane, row, row, row, V((chips, 8, HEADS), F32),
            V((HALF, 128), F32), V((HALF, 128), F32), V((chips, 128), F32), tall, tall,
            inner, group16, group16, group32, inner, group32, plane, plane, whole, whole, part, part,
            sent, sent, sent, sent, whole, whole, part, part, plane, plane, plane, plane, row, plane, plane, row,
            V((16, CONV), F32), edge, edge, edge, row,
            V((shards, 8, width), F32), row, V((shards, 8, width + 128), F32), V((shards, 8, width + 128), F32),
            V((16, width // 2 + 128), F32), V((16, width // 2 + 128), BF16),
            V((chips, 16, width // 2 + 128), BF16), V((8, width), F32), V((8, width), F32),
            dma((1,)), dma((1,)), dma((chips,)), dma((chips,)),
        ]
        + [dma((BATCHES,))] * 4 + [dma((BATCHES, chips))] * 4 + [dma((BATCHES,))] * 4
        + [dma((GROUPS, 3))] * 2 + [dma((shards + 1,))] * 2 + [dma((shards,))] * 2 + [dma((chips,))] * 2 + [dma((1,))] * 2,
        compiler_params=pltpu.CompilerParams(
            collective_id=0, has_side_effects=True, vmem_limit_bytes=VMEM
        ),
        name="mixer_grads",
    )(mixer, halo, weight, shift, raw, bias, decay, gain, dy)


def finish_kernel(factor, ig_ref, step_ref, conv_ref, head_ref, ig_out, step_out, conv_out, head_out, gain_out):
    ig_out[...] = ig_ref[...]

    @pl.when(pl.program_id(0) == 0)
    def _():
        step_out[...] = step_ref[...]
        conv_out[...] = conv_ref[0 : KERNEL + 1, :] * factor
        head_out[...] = head_ref[0:2, 0 : head_out.shape[1]] * factor
        gain_out[...] = head_ref[2:3, 0 : gain_out.shape[1]] * factor


def finish(factor, input_grad, step_grad, conv, head):
    heads = HEADS // lax.axis_size("dp")
    parts = 4
    block = pl.BlockSpec((ROWS // parts, CONV), lambda i: (i, 0))

    def full(shape):
        return pl.BlockSpec(shape, lambda i: (0,) * len(shape))

    return pl.pallas_call(
        functools.partial(finish_kernel, factor),
        grid=(parts,),
        in_specs=[block, full(step_grad.shape), full(conv.shape), full(head.shape)],
        out_specs=[block, full(step_grad.shape), full((KERNEL + 1, conv.shape[1])), full((2, heads)), full((1, heads))],
        out_shape=[
            jax.ShapeDtypeStruct((ROWS, CONV), BF16), jax.ShapeDtypeStruct((ROWS, HEADS), F32),
            jax.ShapeDtypeStruct((KERNEL + 1, conv.shape[1]), F32),
            jax.ShapeDtypeStruct((2, heads), F32), jax.ShapeDtypeStruct((1, heads), F32),
        ],
        compiler_params=pltpu.CompilerParams(vmem_limit_bytes=VMEM),
        name="finish",
    )(input_grad, step_grad, conv, head)


def passed_along(value, axis, steps):
    count = lax.axis_size(axis)
    initial, last = (max(0, -steps), min(count, count - steps))
    return lax.ppermute(value, axis, [(source, source + steps) for source in range(initial, last)])


def local(mixer_input, step_raw, out_grad, conv_weight, conv_bias, step_bias, decay_log, skip_gain):
    mixer, raw, dy = mixer_input[0], step_raw[0], out_grad[0]
    halo = passed_along(mixer[ROWS - 8 :], "ctx", 1)
    input_grad, step_grad, conv, head = mixer_grads(
        mixer, halo, conv_weight, conv_bias[None], raw, step_bias[None], decay_log[None], skip_gain[None], dy
    )
    factor = 1.0 / math.sqrt(lax.axis_size("dp") * ROWS * lax.axis_size("ctx"))
    input_grad, step_grad, conv, head, gain = finish(factor, input_grad, step_grad, conv, head)
    return input_grad[None], step_grad[None], conv, head, gain[0]


def solution(mesh):
    spread = P("dp", "ctx", None)
    in_specs = (spread, spread, spread, P(), P(), P(), P(), P())
    out_specs = (spread, spread, P(None, "dp"), P(None, "dp"), P("dp"))
    return jax.shard_map(local, mesh=mesh, in_specs=in_specs, out_specs=out_specs, check_vma=False)
```

time: 924 us -> 113 us (0.12); the launches traced: 910 us -> 113 us
  local copies, waits for them, and re-layouts: 224 us -> 1.6 us
  matrix products: 219 us -> 0 us
  other arithmetic: 187 us -> 0 us
  blocking collectives: 123 us -> 0 us
  Pallas kernels: 0 us -> 104 us
  waiting for transfers between devices: 73.3 us -> 2.24 us
  starting transfers between devices: 58.4 us -> 4.59 us
  between operations: 14.9 us -> 0.65 us
  loops' own time: 10.5 us -> 0 us
    dot_general x53 -> x0, matrix products: 219 us -> none  [the longest x12 55.7 us: ssd_core(): jnp.einsum('ctgn,cgknp->ctgkp', c_parts, entering, precision=FULL_PRECISION)]
    psum x1 -> x0, blocking collectives: 123 us -> none  [local(): lax.psum(conv_part.astype(jnp.bfloat16), 'ctx').astype(jnp.float32)]
    pallas_call x0 -> x2, Pallas kernels: none -> 104 us  [the longest x1 100 us: mixer_grads(): pl.pallas_call(mixer_kernel, out_shape=[jax.ShapeDtypeStruct((ROWS, CONV)...]
    another operation x31 -> x0, other arithmetic: 56.2 us -> none  [the longest x8 41.9 us: ssd_core(): running = jnp.cumsum(step_parts * rates, axis=1)]
    unnamed x57 -> x2, local copies, waits for them, and re-layouts: 53.3 us -> 0.67 us
    all_to_all x7 -> x0, starting transfers between devices: 50.8 us -> none  [the longest x1 9.6 us: local(): lax.all_to_all(raw_send, 'ctx', split_axis=1, concat_axis=0, tiled=True)]
    all_to_all x7 -> x0, waiting for transfers between devices: 48.9 us -> none  [the longest x1 26.6 us: local(): lax.all_to_all(x_send, 'ctx', split_axis=1, concat_axis=0, tiled=True)]
    reduce_sum x15 -> x0, other arithmetic: 41.5 us -> none  [the longest x1 22.6 us: causal_conv(): conv_weight[offset][None, :] * padded[offset:offset + seq_len]]
  transfers between devices with their start and end apart: 11 -> 1, of which waited for: 7 -> 1; matrix products, arithmetic and copies ran while one was open for 15% -> 0% of each run, Pallas kernels for 0% -> 0%
where the time goes in v3:
time: 113 us
  Pallas kernels  104 us (92%)
  starting transfers between devices  4.59 us (4%)
  waiting for transfers between devices  2.24 us (2%)
  local copies, waits for them, and re-layouts  1.6 us (1%)
    pallas_call x1, Pallas kernels, mixer_grads(): pl.pallas_call(mixer_kernel, out_shape=[jax.ShapeDtypeStruct((ROWS, CONV)...  100 us
    ppermute x1, starting transfers between devices, passed_along(): lax.ppermute(value, axis, [(source, source + steps) for source in range(i...  4.59 us
    pallas_call x1, Pallas kernels, finish(): pl.pallas_call(functools.partial(finish_kernel, factor), grid=(parts,), i...  4.08 us
  transfers between devices with their start and end apart: 1, of which 1 were waited for; matrix products, arithmetic and copies ran while one was open for 0% of the time, Pallas kernels for 0%

profile of v3, /device:TPU:1, one launch (start us, length us, event | category | flops | bytes accessed | tf_op | source)
XLA Modules:
  0.0 113.1 jit_solution(8914945286502536035)
XLA Ops:
  0.6 0.9 slice_bitcast_fusion
  1.6 4.6 %collective-permute-start = (bf16[8,10240]{1,0:T(8,128)(2,1)S(1)}, bf16[8,10240]{1,0:T(8,128)(2,1)S(1)}, u32[]{:S(2)}, u32[]{:S(2)}) collective-permute-start(bf16[8,10240]{1,0:T(8,128)(2,1)S(1)} %slice_bitcast_fusion), channel_id=1, source_target_pairs={{0,1},{1,2},{2,3},{3,4},{4,5},{5,6},{6,7},{7,8},{8,9},{9,10},{10,1... | collective-permute-start | bytes 491528 | tf_op jit(solution)/shard_map/ppermute | solution.py:692
  6.2 2.2 %collective-permute-done.halo_ref = bf16[8,10240]{1,0:T(8,128)(2,1)S(1)} collective-permute-done((bf16[8,10240]{1,0:T(8,128)(2,1)S(1)}, bf16[8,10240]{1,0:T(8,128)(2,1)S(1)}, u32[]{:S(2)}, u32[]{:S(2)}) %collective-permute-start) | collective-permute-done | bytes 163872 | tf_op jit(solution)/shard_map/ppermute | solution.py:692
  8.4 0.0 copy-start
  8.4 0.7 copy-done
  9.1 100.0 %mixer_grads.1 = (bf16[128,10240]{1,0:T(8,128)(2,1)}, f32[128,128]{1,0:T(8,128)}, f32[8,2560]{1,0:T(8,128)}, f32[8,128]{1,0:T(8,128)}) custom-call(bf16[128,10240]{1,0:T(8,128)(2,1)} %bitcast.12, bf16[8,10240]{1,0:T(8,128)(2,1)} %copy-done, f32[4,10240]{1,0:T(4,128)} %weight_ref.1, f32[1,10240]{1,0:T(1,128)} %bitcast.14, bf16[128,128]{1,0:T(8,128)(2,1)} %bitcast.15, ...), custom_call_target="tpu_custom_call" | custom-call | tf_op jit(solution)/shard_map/mixer_grads/pallas_call | solution.py:627
  109.1 4.1 %finish.1 = (bf16[128,10240]{1,0:T(8,128)(2,1)}, f32[128,128]{1,0:T(8,128)}, f32[5,2560]{1,0:T(8,128)}, f32[2,32]{1,0:T(2,128)}, f32[1,32]{1,0:T(1,128)}) custom-call(bf16[128,10240]{1,0:T(8,128)(2,1)} %get-tuple-element.14.ig_ref, f32[128,128]{1,0:T(8,128)} %get-tuple-element.15.step_ref, f32[8,2560]{1,0:T(8,128)} %get-tuple-element.16.conv_ref, ...), custom_call_target="tpu_custom_call" | custom-call | tf_op jit(solution)/shard_map/finish/pallas_call | solution.py:674
Async XLA Ops:
  1.6 6.8 %collective-permute-start = (bf16[8,10240]{1,0:T(8,128)(2,1)S(1)}, bf16[8,10240]{1,0:T(8,128)(2,1)S(1)}, u32[]{:S(2)}, u32[]{:S(2)}) collective-permute-start(bf16[8,10240]{1,0:T(8,128)(2,1)S(1)} %slice_bitcast_fusion), channel_id=1, source_target_pairs={{0,1},{1,2},{2,3},{3,4},{4,5},{5,6},{6,7},{7,8},{8,9},{9,10},{10,1... | collective-permute-start | bytes 491528 | tf_op jit(solution)/shard_map/ppermute | solution.py:692
  8.4 0.7 copy-start

commit v4 on v3

--- a/solution.py
+++ b/solution.py
@@ -27,7 +27,8 @@
 VMEM = 60 << 20
 BATCHES = 4
 BLOCK_ROWS = 64
-FIRST, SLICE = 6, 14
+FIRST, SLICE = 2, 3
+FINISH_PARTS = 2
 EXACT = lax.Precision.HIGHEST
 
 
@@ -63,14 +64,15 @@
 
 
 def mixer_kernel(
-    mix_ref, halo_ref, weight_ref, shift_ref, raw_ref, bias_ref, decay_ref, gain_ref, dy_ref,
-    ig_ref, step_ref, conv_ref, head_ref,
-    run_ref, run_t_ref, sp_ref, close_own, close_oth, close_out, close_in, decay_own, decay_oth, decay_in, pad, dpad,
+    mix_hbm, halo_ref, weight_ref, shift_ref, raw_ref, bias_ref, decay_ref, gain_ref, dy_hbm,
+    ig_hbm, step_ref, conv_ref, head_ref,
+    mix_ref, dy_ref, ig_ref, run_ref, run_t_ref, sp_ref, close_own, close_oth, close_out, close_in, decay_own, decay_oth, decay_in, pad, dpad,
     xm, bm, cm, scores, dxi, dsc, sum_s, sum_r, s_own, g_own, s_oth, g_oth, sg_out, sg_in, hl_out, hl_in,
-    h_all, l_all, h_oth, l_oth, acc_b, acc_c, col_u, col_q, row_g, full_u, full_q, full_g,
+    h_all, l_all, h_oth, l_oth, acc_b, acc_c, col_s, xc, dyg, close, ones, ent, use, row_g, full_u, full_q, full_g,
     last, spill, spill_in, taps, rows, taps_oth, rows_oth, shards, arrived, flat, packed, packed_in, total, total_oth,
     e_send, e_recv, k_send, k_recv, x_send, x_recv, y_send, y_recv, sg_send, sg_recv, hl_send, hl_recv,
     p_send, p_recv, q_send, q_recv, sp_send, sp_recv, t_send, t_recv, d_send, d_recv, c_send, c_recv, o_send, o_recv,
+    in_sem, out_sem, last_sem,
 ):
     dp = lax.axis_index("dp")
     ctx = lax.axis_index("ctx")
@@ -101,6 +103,41 @@
     def dp_at(r):
         return lax.rem(dp + r, shard_count)
 
+    def tile(start):
+        return pl.ds(pl.multiple_of(start, 128), 128)
+
+    def group_lanes(g):
+        return (
+            pl.ds(pl.multiple_of(GROUP_LANES * g, 128), GROUP_LANES),
+            tile(INNER + STATE * g),
+            tile(INNER + GROUPS * STATE + STATE * g),
+        )
+
+    def loads(g):
+        lanes = group_lanes(g)
+        copies = [
+            pltpu.make_async_copy(mix_hbm.at[:, part], mix_ref.at[:, part], in_sem.at[g, n])
+            for n, part in enumerate(lanes)
+        ]
+        copies.append(pltpu.make_async_copy(dy_hbm.at[:, lanes[0]], dy_ref.at[:, lanes[0]], in_sem.at[g, 3]))
+        return copies
+
+    def stores(g):
+        top = pl.ds(0, ROWS - 16)
+        return [
+            pltpu.make_async_copy(ig_ref.at[top, part], ig_hbm.at[top, part], out_sem.at[g, n])
+            for n, part in enumerate(group_lanes(g))
+        ]
+
+    def group_of(u):
+        return jnp.where(lax.rem(u, 2) == 0, theirs_group, mine_group) + u // 2
+
+    def load(u, _):
+        for copy in loads(group_of(u)):
+            copy.start()
+        return 0
+
+    lax.fori_loop(0, GROUPS, load, 0)
     barrier = pltpu.get_barrier_semaphore()
     for device in (other, beyond):
         pl.semaphore_signal(barrier, inc=1, device_id=(dp, device), device_id_type=MESH)
@@ -118,9 +155,6 @@
             src_ref=src, dst_ref=dst, send_sem=send, recv_sem=recv,
             device_id=(dp if d is None else d, device), device_id_type=MESH,
         )
-
-    def tile(start):
-        return pl.ds(pl.multiple_of(start, 128), 128)
 
     rate = -jnp.exp(decay_ref[...])
     spread = softplus(raw_ref[...].astype(F32) + bias_ref[...])
@@ -131,6 +165,7 @@
     run_t_ref[...] = running.T
     close_own[...] = jnp.broadcast_to(running[ROWS - 1 : ROWS, :], (8, HEADS))
     sum_s[...] = jnp.zeros((ROWS, HEADS), F32)
+    col_s[...] = jnp.zeros((ROWS, HEADS), F32)
 
     def conv_pre(slot, lanes):
         here = pad.at[slot]
@@ -164,9 +199,15 @@
             lanes = tile(GROUP_LANES * g + 128 * j)
             x16 = mixed(j, lanes)
             xm[:, lanes] = x16
-            state = dot(b_t, (x16.astype(F32) * pair_of(to_close, j)).astype(BF16))
+            close_2 = pair_of(to_close, j)
+            close[:, lanes] = close_2
+            x_closed = (x16.astype(F32) * close_2).astype(BF16)
+            xc[:, lanes] = x_closed
+            state = dot(b_t, x_closed)
             s_own[at] = state.astype(BF16).reshape(2, BLOCK_ROWS, 128)
-            state = dot(c_t, (dy_ref[:, lanes].astype(F32) * pair_of(grown, j)).astype(BF16))
+            dy_grown = (dy_ref[:, lanes].astype(F32) * pair_of(grown, j)).astype(BF16)
+            dyg[:, lanes] = dy_grown
+            state = dot(c_t, dy_grown)
             g_own[at] = state.astype(BF16).reshape(2, BLOCK_ROWS, 128)
 
     def batch(i):
@@ -223,7 +264,9 @@
     def build(u, _):
         i = u // 2
         theirs = lax.rem(u, 2) == 0
-        group_states(jnp.where(theirs, theirs_group, mine_group) + i)
+        for copy in loads(group_of(u)):
+            copy.wait()
+        group_states(group_of(u))
 
         @pl.when(u == 0)
         def _():
@@ -276,35 +319,34 @@
 
     lax.fori_loop(0, 2 * BATCHES, build, 0)
 
-    def inside(jj, _):
-        g = jj // GROUP_PAIRS
-        lanes = tile(128 * jj)
-        x16 = xm[:, lanes]
-        dy = dy_ref[:, lanes].astype(F32)
-        split = jnp.concatenate([jnp.where(low, dy, 0.0), jnp.where(low, 0.0, dy)], axis=0).astype(BF16)
-        d_weights = dot_nt(x16, split)
-        back = lax.rem(HEADS - 2 * jj, HEADS)
+    def inside(n, _):
+        g = n // 2
+        back = lax.rem(HEADS - 8 * n, HEADS)
         run = pltpu.roll(run_ref[...], back, 1)
         steps = pltpu.roll(sp_ref[...], back, 1)
-        score = scores[g]
-        weights = []
-        gathered = dsc[g]
-        sums = sum_s[...]
-        lane = iota(shape, 1)
-        for i in range(2):
-            at = 2 * jj + i
-            step = steps[:, i : i + 1]
-            d_weight = d_weights[:, 128 * i : 128 * i + 128]
-            decay = jnp.exp(jnp.minimum(run_t_ref[pl.ds(at, 1), :] - run[:, i : i + 1], 0.0))
-            plain = decay * score
-            weights.append((plain * step).astype(BF16))
-            product = d_weight * plain
-            sums = jnp.where(lane == at, jnp.sum(product, axis=1, keepdims=True), sums)
-            sum_r[pl.ds(at, 1), :] = jnp.sum(product * step, axis=0, keepdims=True)
-            gathered = gathered + d_weight * decay * step
-        sum_s[...] = sums
-        dsc[g] = gathered
-        dxi[:, lanes] = dot(jnp.concatenate(weights, axis=1), split).astype(BF16)
+        for j in range(4):
+            lanes = tile(512 * n + 128 * j)
+            dy = dy_ref[:, lanes].astype(F32)
+            split = jnp.concatenate([jnp.where(low, dy, 0.0), jnp.where(low, 0.0, dy)], axis=0).astype(BF16)
+            d_weights = dot_nt(xm[:, lanes], split)
+            weights = []
+            gathered = jnp.zeros(shape, F32)
+            for i in range(2):
+                head = 2 * j + i
+                at = pl.ds(8 * n + head, 1)
+                step = steps[:, head : head + 1]
+                d_weight = d_weights[:, 128 * i : 128 * i + 128]
+                decay = jnp.exp(jnp.minimum(run_t_ref[at, :] - run[:, head : head + 1], 0.0))
+                plain = decay * scores[g]
+                weights.append((plain * step).astype(BF16))
+                product = d_weight * plain
+                col_s[:, head : head + 1] = jnp.sum(product, axis=1, keepdims=True)
+                sum_r[at, :] = jnp.sum(product * step, axis=0, keepdims=True)
+                gathered = gathered + d_weight * decay * step
+            dsc[g] += gathered
+            dxi[:, lanes] = dot(jnp.concatenate(weights, axis=1), split).astype(BF16)
+        kept = jnp.where(iota(shape, 1) < 8, col_s[...], 0.0)
+        sum_s[...] += pltpu.roll(kept, lax.rem(8 * n, HEADS), 1)
         return 0
 
     def scan(i):
@@ -344,11 +386,12 @@
         return 0
 
     lax.fori_loop(0, BATCHES, middle, 0)
-    lax.fori_loop(SLICE * (BATCHES - 1) + FIRST, PAIRS, inside, 0)
-
+    lax.fori_loop(SLICE * (BATCHES - 1) + FIRST, PAIRS // 4, inside, 0)
+
+    ones[...] = jnp.where(iota(ones.shape, 0) // HEAD_DIM == iota(ones.shape, 1), 1.0, 0.0).astype(BF16)
     dpad[:, ROWS:, :] = jnp.zeros((GROUP_PAIRS + 2, 8, 128), F32)
     taps[...] = jnp.zeros(taps.shape, F32)
-    for ref in (full_u, full_q, full_g, col_u, col_q, row_g):
+    for ref in (full_u, full_q, full_g, row_g):
         ref[...] = jnp.zeros(ref.shape, F32)
 
     def conv_back(slot, grad, pre, gate, lanes):
@@ -374,28 +417,20 @@
     before = lax.rem(ctx + devices - 1, devices)
 
     def spill_copies(g):
-        parts = (
-            pl.ds(pl.multiple_of(GROUP_LANES * g, 128), GROUP_LANES),
-            tile(INNER + STATE * g),
-            tile(INNER + GROUPS * STATE + STATE * g),
-        )
         return [
             remote(spill.at[:, lanes], spill_in.at[:, lanes], sp_send.at[g, n], sp_recv.at[g, n], before)
-            for n, lanes in enumerate(parts)
+            for n, lanes in enumerate(group_lanes(g))
         ]
 
     def group_grads(g):
         back = lax.rem(HEADS - GROUP_HEADS * g, HEADS)
         b16, c16 = bm[g], cm[g]
-        run = pltpu.roll(run_ref[...], back, 1)
-        step = pltpu.roll(sp_ref[...], back, 1)
         gain = pltpu.roll(jnp.broadcast_to(gain_ref[...], (8, HEADS)), back, 1)
-        grown = jnp.exp(run)
-        to_close = jnp.exp(run[ROWS - 1 : ROWS, :] - run) * step
         acc_b[...] = jnp.zeros(shape, F32)
         acc_c[...] = jnp.zeros(shape, F32)
         for j in range(GROUP_PAIRS):
             lanes = tile(GROUP_LANES * g + 128 * j)
+            here = pl.ds(128 * j, 128)
             at = pl.ds(2 * (GROUP_PAIRS * g + j), 2)
             pre = conv_pre(j, lanes)
             gate = sigmoid(pre)
@@ -403,23 +438,14 @@
             dy = dy_ref[:, lanes].astype(F32)
             h16 = h_all[at].reshape(STATE, 128)
             l16 = l_all[at].reshape(STATE, 128)
-            close_2 = pair_of(to_close, j)
-            entered = dy * dot(c16, h16)
             left = dot(b16, l16)
-            used = x * left
-            crossed = jnp.sum(h16.astype(F32) * l16.astype(F32), axis=0, keepdims=True)
-            gained = jnp.sum(dy * x, axis=0, keepdims=True)
-            for i in range(2):
-                head = 2 * j + i
-                mask = low if i == 0 else jnp.logical_not(low)
-                mask_row = low_row if i == 0 else jnp.logical_not(low_row)
-                col_u[:, head : head + 1] = jnp.sum(jnp.where(mask, entered, 0.0), axis=1, keepdims=True)
-                col_q[:, head : head + 1] = jnp.sum(jnp.where(mask, used, 0.0), axis=1, keepdims=True)
-                row_g[0:1, head : head + 1] = jnp.sum(jnp.where(mask_row, crossed, 0.0), axis=1, keepdims=True)
-                row_g[1:2, head : head + 1] = jnp.sum(jnp.where(mask_row, gained, 0.0), axis=1, keepdims=True)
-            acc_c[...] += dot_nt((dy * pair_of(grown, j)).astype(BF16), h16)
-            acc_b[...] += dot_nt((x * close_2).astype(BF16), l16)
-            grad_x = dxi[:, lanes].astype(F32) + close_2 * left + pair_of(gain, j)[0:1, :] * dy
+            ent[:, here] = (dy * dot(c16, h16)).astype(BF16)
+            use[:, here] = (x * left).astype(BF16)
+            row_g[0:1, here] = jnp.sum(h16.astype(F32) * l16.astype(F32), axis=0, keepdims=True)
+            row_g[1:2, here] = jnp.sum(dy * x, axis=0, keepdims=True)
+            acc_c[...] += dot_nt(dyg[:, lanes], h16)
+            acc_b[...] += dot_nt(xc[:, lanes], l16)
+            grad_x = dxi[:, lanes].astype(F32) + close[:, lanes] * left + pair_of(gain, j)[0:1, :] * dy
             conv_back(j, grad_x, pre, gate, lanes)
         d_scores = jnp.where(iota(shape, 1) >= iota(shape, 0), dsc[g], 0.0)
         grad_b = acc_b[...] + dot(d_scores.astype(BF16), c16)
@@ -429,9 +455,19 @@
             pre = conv_pre(GROUP_PAIRS + i, lanes)
             conv_back(GROUP_PAIRS + i, grad, pre, sigmoid(pre), lanes)
         forward = lax.rem(GROUP_HEADS * g, HEADS)
-        for whole_ref, part_ref in ((full_u, col_u), (full_q, col_q), (full_g, row_g)):
-            lane = iota(part_ref.shape, 1)
-            whole_ref[...] += pltpu.roll(jnp.where(lane < GROUP_HEADS, part_ref[...], 0.0), forward, 1)
+        full_u[...] += pltpu.roll(dot(ent[...], ones[...]), forward, 1)
+        full_q[...] += pltpu.roll(dot(use[...], ones[...]), forward, 1)
+        rest = row_g[...]
+        thirds = []
+        for _ in range(3):
+            part = rest.astype(BF16)
+            thirds.append(part.astype(F32))
+            rest = rest - thirds[-1]
+        sums = dot(jnp.concatenate(thirds, axis=0).astype(BF16), ones[...])
+        full_g[...] += pltpu.roll(sums[0:8] + sums[8:16] + sums[16:24], forward, 1)
+
+        for copy in stores(g):
+            copy.start()
 
         @pl.when(ctx > 0)
         def _():
@@ -535,6 +571,9 @@
         last[8:16, :] += spill_in[...]
 
     ig_ref[ROWS - 16 :, :] = last[...].astype(BF16)
+    bottom = pl.ds(ROWS - 16, 16)
+    last_store = pltpu.make_async_copy(ig_ref.at[bottom], ig_hbm.at[bottom], last_sem.at[0])
+    last_store.start()
 
     summed = shards[dp]
     for r in range(1, shard_count):
@@ -559,6 +598,14 @@
     lax.fori_loop(1, chips, send, 0)
 
     close_swap.wait_send()
+    last_store.wait()
+
+    def stored(g, _):
+        for copy in stores(g):
+            copy.wait()
+        return 0
+
+    lax.fori_loop(0, GROUPS, stored, 0)
 
     def cleared(i, _):
         for copy in swaps(i) + swap_back(i):
@@ -624,19 +671,22 @@
     sent = V((BATCHES, chips, 2, BLOCK_ROWS, 128), BF16)
     edge = V((8, CONV), F32)
     memory = pl.BlockSpec(memory_space=pltpu.VMEM)
+    remote_memory = pl.BlockSpec(memory_space=pl.ANY)
     return pl.pallas_call(
         mixer_kernel,
         out_shape=[
             jax.ShapeDtypeStruct((ROWS, CONV), BF16), jax.ShapeDtypeStruct((ROWS, HEADS), F32),
             jax.ShapeDtypeStruct((8, 2 * width), F32), jax.ShapeDtypeStruct((8, HEADS), F32),
         ],
-        in_specs=[memory] * 9,
-        out_specs=[memory] * 4,
+        in_specs=[remote_memory] + [memory] * 7 + [remote_memory],
+        out_specs=[remote_memory] + [memory] * 3,
         scratch_shapes=[
-            plane, plane, plane, row, row, row, V((chips, 8, HEADS), F32),
+            V((ROWS, CONV), BF16), inner, V((ROWS, CONV), BF16), plane, plane, plane, row, row, row, V((chips, 8, HEADS), F32),
             V((HALF, 128), F32), V((HALF, 128), F32), V((chips, 128), F32), tall, tall,
             inner, group16, group16, group32, inner, group32, plane, plane, whole, whole, part, part,
-            sent, sent, sent, sent, whole, whole, part, part, plane, plane, plane, plane, row, plane, plane, row,
+            sent, sent, sent, sent, whole, whole, part, part, plane, plane, plane,
+            inner, inner, V((ROWS, INNER), F32), V((GROUP_LANES, 128), BF16),
+            V((ROWS, GROUP_LANES), BF16), V((ROWS, GROUP_LANES), BF16), V((8, GROUP_LANES), F32), plane, plane, row,
             V((16, CONV), F32), edge, edge, edge, row,
             V((shards, 8, width), F32), row, V((shards, 8, width + 128), F32), V((shards, 8, width + 128), F32),
             V((16, width // 2 + 128), F32), V((16, width // 2 + 128), BF16),
@@ -644,7 +694,8 @@
             dma((1,)), dma((1,)), dma((chips,)), dma((chips,)),
         ]
         + [dma((BATCHES,))] * 4 + [dma((BATCHES, chips))] * 4 + [dma((BATCHES,))] * 4
-        + [dma((GROUPS, 3))] * 2 + [dma((shards + 1,))] * 2 + [dma((shards,))] * 2 + [dma((chips,))] * 2 + [dma((1,))] * 2,
+        + [dma((GROUPS, 3))] * 2 + [dma((shards + 1,))] * 2 + [dma((shards,))] * 2 + [dma((chips,))] * 2 + [dma((1,))] * 2
+        + [dma((GROUPS, 4)), dma((GROUPS, 3)), dma((1,))],
         compiler_params=pltpu.CompilerParams(
             collective_id=0, has_side_effects=True, vmem_limit_bytes=VMEM
         ),
@@ -665,15 +716,14 @@
 
 def finish(factor, input_grad, step_grad, conv, head):
     heads = HEADS // lax.axis_size("dp")
-    parts = 4
-    block = pl.BlockSpec((ROWS // parts, CONV), lambda i: (i, 0))
+    block = pl.BlockSpec((ROWS // FINISH_PARTS, CONV), lambda i: (i, 0))
 
     def full(shape):
         return pl.BlockSpec(shape, lambda i: (0,) * len(shape))
 
     return pl.pallas_call(
         functools.partial(finish_kernel, factor),
-        grid=(parts,),
+        grid=(FINISH_PARTS,),
         in_specs=[block, full(step_grad.shape), full(conv.shape), full(head.shape)],
         out_specs=[block, full(step_grad.shape), full((KERNEL + 1, conv.shape[1])), full((2, heads)), full((1, heads))],
         out_shape=[

time: 113 us -> 97.7 us (0.86)
  Pallas kernels: 104 us -> 88.4 us
    pallas_call x1, Pallas kernels: 100 us -> 85.5 us  [mixer_grads(): pl.pallas_call(mixer_kernel, out_shape=[jax.ShapeDtypeStruct((ROWS, CONV)...]
where the time goes in v4:
time: 97.7 us; the launch traced here: 97.5 us
  Pallas kernels  88.4 us (90%)
  starting transfers between devices  4.59 us (5%)
  waiting for transfers between devices  2.24 us (2%)
  local copies, waits for them, and re-layouts  1.6 us (2%)
    pallas_call x1, Pallas kernels, mixer_grads(): pl.pallas_call(mixer_kernel, out_shape=[jax.ShapeDtypeStruct((ROWS, CONV)...  85.5 us
    ppermute x1, starting transfers between devices, passed_along(): lax.ppermute(value, axis, [(source, source + steps) for source in range(i...  4.59 us
    pallas_call x1, Pallas kernels, finish(): pl.pallas_call(functools.partial(finish_kernel, factor), grid=(FINISH_PAR...  2.97 us
    ppermute x1, waiting for transfers between devices, passed_along(): lax.ppermute(value, axis, [(source, source + steps) for source in range(i...  2.24 us
  transfers between devices with their start and end apart: 1, of which 1 were waited for; matrix products, arithmetic and copies ran while one was open for 0% of the time, Pallas kernels for 0%

profile of v4, /device:TPU:1, one launch (start us, length us, event | category | flops | bytes accessed | tf_op | source)
XLA Modules:
  0.0 97.5 jit_solution(14369335286823692762)
XLA Ops:
  0.6 0.9 slice_bitcast_fusion
  1.6 4.6 %collective-permute-start = (bf16[8,10240]{1,0:T(8,128)(2,1)S(1)}, bf16[8,10240]{1,0:T(8,128)(2,1)S(1)}, u32[]{:S(2)}, u32[]{:S(2)}) collective-permute-start(bf16[8,10240]{1,0:T(8,128)(2,1)S(1)} %slice_bitcast_fusion), channel_id=1, source_target_pairs={{0,1},{1,2},{2,3},{3,4},{4,5},{5,6},{6,7},{7,8},{8,9},{9,10},{10,1... | collective-permute-start | bytes 491528 | tf_op jit(solution)/shard_map/ppermute | solution.py:742
  6.2 2.2 %collective-permute-done.halo_ref = bf16[8,10240]{1,0:T(8,128)(2,1)S(1)} collective-permute-done((bf16[8,10240]{1,0:T(8,128)(2,1)S(1)}, bf16[8,10240]{1,0:T(8,128)(2,1)S(1)}, u32[]{:S(2)}, u32[]{:S(2)}) %collective-permute-start) | collective-permute-done | bytes 163872 | tf_op jit(solution)/shard_map/ppermute | solution.py:742
  8.4 0.0 copy-start
  8.4 0.7 copy-done
  9.1 85.5 %mixer_grads.1 = (bf16[128,10240]{1,0:T(8,128)(2,1)}, f32[128,128]{1,0:T(8,128)}, f32[8,2560]{1,0:T(8,128)}, f32[8,128]{1,0:T(8,128)}) custom-call(bf16[128,10240]{1,0:T(8,128)(2,1)} %bitcast.12, bf16[8,10240]{1,0:T(8,128)(2,1)} %copy-done, f32[4,10240]{1,0:T(4,128)} %weight_ref.1, f32[1,10240]{1,0:T(1,128)} %bitcast.14, bf16[128,128]{1,0:T(8,128)(2,1)} %bitcast.15, ...), custom_call_target="tpu_custom_call" | custom-call | tf_op jit(solution)/shard_map/mixer_grads/pallas_call | solution.py:675
  94.5 3.0 %finish.1 = (bf16[128,10240]{1,0:T(8,128)(2,1)}, f32[128,128]{1,0:T(8,128)}, f32[5,2560]{1,0:T(8,128)}, f32[2,32]{1,0:T(2,128)}, f32[1,32]{1,0:T(1,128)}) custom-call(bf16[128,10240]{1,0:T(8,128)(2,1)} %get-tuple-element.14.ig_ref, f32[128,128]{1,0:T(8,128)} %get-tuple-element.15.step_ref, f32[8,2560]{1,0:T(8,128)} %get-tuple-element.16.conv_ref, ...), custom_call_target="tpu_custom_call" | custom-call | tf_op jit(solution)/shard_map/finish/pallas_call | solution.py:724
Async XLA Ops:
  1.6 6.8 %collective-permute-start = (bf16[8,10240]{1,0:T(8,128)(2,1)S(1)}, bf16[8,10240]{1,0:T(8,128)(2,1)S(1)}, u32[]{:S(2)}, u32[]{:S(2)}) collective-permute-start(bf16[8,10240]{1,0:T(8,128)(2,1)S(1)} %slice_bitcast_fusion), channel_id=1, source_target_pairs={{0,1},{1,2},{2,3},{3,4},{4,5},{5,6},{6,7},{7,8},{8,9},{9,10},{10,1... | collective-permute-start | bytes 491528 | tf_op jit(solution)/shard_map/ppermute | solution.py:742
  8.4 0.7 copy-start

commit v5 on v4

--- a/solution.py
+++ b/solution.py
@@ -27,7 +27,7 @@
 VMEM = 60 << 20
 BATCHES = 4
 BLOCK_ROWS = 64
-FIRST, SLICE = 2, 3
+FIRST, SLICE = 2, 4
 FINISH_PARTS = 2
 EXACT = lax.Precision.HIGHEST
 
@@ -66,11 +66,11 @@
 def mixer_kernel(
     mix_hbm, halo_ref, weight_ref, shift_ref, raw_ref, bias_ref, decay_ref, gain_ref, dy_hbm,
     ig_hbm, step_ref, conv_ref, head_ref,
-    mix_ref, dy_ref, ig_ref, run_ref, run_t_ref, sp_ref, close_own, close_oth, close_out, close_in, decay_own, decay_oth, decay_in, pad, dpad,
-    xm, bm, cm, scores, dxi, dsc, sum_s, sum_r, s_own, g_own, s_oth, g_oth, sg_out, sg_in, hl_out, hl_in,
+    mix_ref, dy_ref, ig_ref, slope, run_ref, run_t_ref, sp_ref, close_own, close_oth, close_out, close_in, decay_own, decay_oth, decay_in, decay_row, pad, dpad,
+    xm, bm, cm, scores, dxi, dsc, sum_s, sum_r, s_own, g_own, s_oth, g_oth, sg_out, sg_in, hl_out, hl_in, row_out, row_in,
     h_all, l_all, h_oth, l_oth, acc_b, acc_c, col_s, xc, dyg, close, ones, ent, use, row_g, full_u, full_q, full_g,
     last, spill, spill_in, taps, rows, taps_oth, rows_oth, shards, arrived, flat, packed, packed_in, total, total_oth,
-    e_send, e_recv, k_send, k_recv, x_send, x_recv, y_send, y_recv, sg_send, sg_recv, hl_send, hl_recv,
+    e_send, e_recv, k_send, k_recv, x_send, x_recv, y_send, y_recv, sg_send, sg_recv, hl_send, hl_recv, r_send, r_recv,
     p_send, p_recv, q_send, q_recv, sp_send, sp_recv, t_send, t_recv, d_send, d_recv, c_send, c_recv, o_send, o_recv,
     in_sem, out_sem, last_sem,
 ):
@@ -97,9 +97,6 @@
     def chip_at(r):
         return lax.rem(z + r // 4, 4) * 4 + lax.rem(y + r, 4)
 
-    def chip_before(r):
-        return lax.rem(z + 4 - r // 4, 4) * 4 + lax.rem(y + 4 - lax.rem(r, 4), 4)
-
     def dp_at(r):
         return lax.rem(dp + r, shard_count)
 
@@ -167,10 +164,14 @@
     sum_s[...] = jnp.zeros((ROWS, HEADS), F32)
     col_s[...] = jnp.zeros((ROWS, HEADS), F32)
 
-    def conv_pre(slot, lanes):
+    def padded(slot, lanes):
         here = pad.at[slot]
         here[0:8, :] = halo_ref[:, lanes].astype(F32)
         here[8:, :] = mix_ref[:, lanes].astype(F32)
+        return here
+
+    def conv_pre(slot, lanes):
+        here = padded(slot, lanes)
         pre = jnp.broadcast_to(shift_ref[:, lanes], (ROWS, 128))
         for k in range(KERNEL):
             pre = pre + weight_ref[k : k + 1, lanes] * here[5 + k : 5 + k + ROWS, :]
@@ -178,7 +179,9 @@
 
     def mixed(slot, lanes):
         pre = conv_pre(slot, lanes)
-        return (pre * sigmoid(pre)).astype(BF16)
+        gate = sigmoid(pre)
+        slope[:, lanes] = gate * (1.0 + pre * (1.0 - gate))
+        return (pre * gate).astype(BF16)
 
     def group_states(g):
         b16 = mixed(GROUP_PAIRS, tile(INNER + STATE * g))
@@ -232,13 +235,20 @@
     def close_copy(r):
         return remote(close_out, close_in.at[chip], k_send.at[r], k_recv.at[r], chip_at(r) * 2 + core)
 
+    def beside(r):
+        return lax.rem(y + r, 4)
+
     def sg_copy(i, r):
-        q = chip_at(r)
-        return remote(sg_out.at[i, q], sg_in.at[i, chip], sg_send.at[i, r], sg_recv.at[i, r], q * 2 + core)
+        q = beside(r)
+        return remote(sg_out.at[i, q], sg_in.at[i, y], sg_send.at[i, r], sg_recv.at[i, r], (z * 4 + q) * 2 + core)
+
+    def row_copy(i, r):
+        q = lax.rem(z + r, 4)
+        return remote(row_out.at[i], row_in.at[i, z], r_send.at[i, r], r_recv.at[i, r], (q * 4 + y) * 2 + core)
 
     def hl_copy(i, r):
-        q = chip_at(r)
-        return remote(hl_out.at[i, q], hl_in.at[i, chip], hl_send.at[i, r], hl_recv.at[i, r], q * 2 + core)
+        q = beside(r)
+        return remote(hl_out.at[i, q], hl_in.at[i, y], hl_send.at[i, r], hl_recv.at[i, r], (z * 4 + q) * 2 + core)
 
     def ordered(held, sent):
         return jnp.where(first, held, sent), jnp.where(first, sent, held)
@@ -298,13 +308,14 @@
                 copy.wait_recv()
 
             def combine(r, _):
-                q = chip_at(r)
-                b = chips * i + q
-                a0, a1 = both_decays(b)
-                s0, s1 = values(s_own, s_oth, b)
-                g0, g1 = values(g_own, g_oth, b)
-                sg_out[i, q, 0] = (a1 * s0 + s1).astype(BF16)
-                sg_out[i, q, 1] = (a0 * g1 + g0).astype(BF16)
+                q = beside(r)
+                for k in range(4):
+                    b = chips * i + 4 * q + k
+                    a0, a1 = both_decays(b)
+                    s0, s1 = values(s_own, s_oth, b)
+                    g0, g1 = values(g_own, g_oth, b)
+                    sg_out[i, q, k, 0] = (a1 * s0 + s1).astype(BF16)
+                    sg_out[i, q, k, 1] = (a0 * g1 + g0).astype(BF16)
 
                 @pl.when(r > 0)
                 def _():
@@ -312,8 +323,8 @@
 
                 return 0
 
-            lax.fori_loop(0, chips, combine, 0)
-            sg_in[i, chip] = sg_out[i, chip]
+            lax.fori_loop(0, 4, combine, 0)
+            sg_in[i, y] = sg_out[i, y]
 
         return 0
 
@@ -349,40 +360,70 @@
         sum_s[...] += pltpu.roll(kept, lax.rem(8 * n, HEADS), 1)
         return 0
 
+    def row_totals(i):
+        @pl.when(i == 0)
+        def _():
+            def known(r, _):
+                close_copy(r).wait_recv()
+                return 0
+
+            lax.fori_loop(1, chips, known, 0)
+
+        closing = close_in[:, 0, :]
+        by_row = [jnp.sum(closing[4 * q : 4 * q + 4], axis=0, keepdims=True) for q in range(4)]
+        by_row = jnp.concatenate(by_row + [jnp.zeros((4, HEADS), F32)], axis=0)
+        for p in range(2):
+            pair = (mine + chips * i + 4 * y) // 2 + p
+            decay_in[i, p] = spread_pairs(closing, pair)
+            decay_row[i, p] = spread_pairs(by_row, pair)
+        for r in range(1, 4):
+            sg_copy(i, r).wait_recv()
+        for k in range(4):
+            forth = jnp.zeros((BLOCK_ROWS, 128), F32)
+            back = forth
+            for c in range(4):
+                d = 3 - c
+                forth = decay_in[i, k // 2, pl.ds(4 * z + c, 1), :] * forth + sg_in[i, c, k, 0].astype(F32)
+                back = decay_in[i, k // 2, pl.ds(4 * z + d, 1), :] * back + sg_in[i, d, k, 1].astype(F32)
+            row_out[i, k, 0] = forth.astype(BF16)
+            row_out[i, k, 1] = back.astype(BF16)
+        for r in range(1, 4):
+            row_copy(i, r).start()
+        row_in[i, z] = row_out[i]
+
     def scan(i):
-        def arrive(r, _):
-            @pl.when(i == 0)
-            def _():
-                close_copy(r).wait_recv()
-
-            sg_copy(i, r).wait_recv()
-            return 0
-
-        lax.fori_loop(1, chips, arrive, 0)
-        decay_in[...] = spread_pairs(close_in[:, 0, :], (mine + chips * i + chip) // 2)
-
-        def both(c, states):
-            forth, back = states
-            d = chips - 1 - c
-            hl_out[i, c, 0] = forth.astype(BF16)
-            hl_out[i, d, 1] = back.astype(BF16)
-            forth = decay_in[pl.ds(c, 1), :] * forth + sg_in[i, c, 0].astype(F32)
-            back = decay_in[pl.ds(d, 1), :] * back + sg_in[i, d, 1].astype(F32)
-            return forth, back
-
-        zero = jnp.zeros((BLOCK_ROWS, 128), F32)
-        lax.fori_loop(0, chips, both, (zero, zero), unroll=4)
-
-        def send(r, _):
+        for r in range(1, 4):
+            row_copy(i, r).wait_recv()
+        for k in range(4):
+            forth = jnp.zeros((BLOCK_ROWS, 128), F32)
+            back = forth
+            for q in range(4):
+                d = 3 - q
+                step = decay_row[i, k // 2, q : q + 1, :] * forth + row_in[i, q, k, 0].astype(F32)
+                forth = jnp.where(q < z, step, forth)
+                step = decay_row[i, k // 2, d : d + 1, :] * back + row_in[i, d, k, 1].astype(F32)
+                back = jnp.where(d > z, step, back)
+            for c in range(4):
+                d = 3 - c
+                hl_out[i, c, k, 0] = forth.astype(BF16)
+                hl_out[i, d, k, 1] = back.astype(BF16)
+                forth = decay_in[i, k // 2, pl.ds(4 * z + c, 1), :] * forth + sg_in[i, c, k, 0].astype(F32)
+                back = decay_in[i, k // 2, pl.ds(4 * z + d, 1), :] * back + sg_in[i, d, k, 1].astype(F32)
+        for r in range(1, 4):
             hl_copy(i, r).start()
-            return 0
-
-        lax.fori_loop(1, chips, send, 0)
-        hl_in[i, chip] = hl_out[i, chip]
+        hl_in[i, y] = hl_out[i, y]
 
     def middle(i, _):
         lax.fori_loop(jnp.maximum(SLICE * (i - 1) + FIRST, 0), SLICE * i + FIRST, inside, 0)
-        scan(i)
+
+        @pl.when(i < BATCHES)
+        def _():
+            row_totals(i)
+
+        @pl.when(i > 0)
+        def _():
+            scan(i - 1)
+
         return 0
 
     lax.fori_loop(0, BATCHES, middle, 0)
@@ -394,10 +435,10 @@
     for ref in (full_u, full_q, full_g, row_g):
         ref[...] = jnp.zeros(ref.shape, F32)
 
-    def conv_back(slot, grad, pre, gate, lanes):
-        here = pad.at[slot]
+    def conv_back(slot, grad, lanes):
+        here = padded(slot, lanes)
         there = dpad.at[slot]
-        dpre = grad * (gate * (1.0 + pre * (1.0 - gate)))
+        dpre = grad * slope[:, lanes]
         there[0:ROWS, :] = dpre
         whole = jnp.zeros(shape, F32)
         for k in range(KERNEL):
@@ -432,8 +473,6 @@
             lanes = tile(GROUP_LANES * g + 128 * j)
             here = pl.ds(128 * j, 128)
             at = pl.ds(2 * (GROUP_PAIRS * g + j), 2)
-            pre = conv_pre(j, lanes)
-            gate = sigmoid(pre)
             x = xm[:, lanes].astype(F32)
             dy = dy_ref[:, lanes].astype(F32)
             h16 = h_all[at].reshape(STATE, 128)
@@ -446,14 +485,13 @@
             acc_c[...] += dot_nt(dyg[:, lanes], h16)
             acc_b[...] += dot_nt(xc[:, lanes], l16)
             grad_x = dxi[:, lanes].astype(F32) + close[:, lanes] * left + pair_of(gain, j)[0:1, :] * dy
-            conv_back(j, grad_x, pre, gate, lanes)
+            conv_back(j, grad_x, lanes)
         d_scores = jnp.where(iota(shape, 1) >= iota(shape, 0), dsc[g], 0.0)
         grad_b = acc_b[...] + dot(d_scores.astype(BF16), c16)
         grad_c = acc_c[...] + dot(d_scores.T.astype(BF16), b16)
         for i, grad in enumerate((grad_b, grad_c)):
             lanes = tile(INNER + GROUPS * STATE * i + STATE * g)
-            pre = conv_pre(GROUP_PAIRS + i, lanes)
-            conv_back(GROUP_PAIRS + i, grad, pre, sigmoid(pre), lanes)
+            conv_back(GROUP_PAIRS + i, grad, lanes)
         forward = lax.rem(GROUP_HEADS * g, HEADS)
         full_u[...] += pltpu.roll(dot(ent[...], ones[...]), forward, 1)
         full_q[...] += pltpu.roll(dot(use[...], ones[...]), forward, 1)
@@ -476,27 +514,28 @@
 
     def gather(i):
         def finish(r, _):
-            q = chip_before(r)
+            q = lax.rem(y + 4 - r, 4)
 
             @pl.when(r > 0)
             def _():
                 hl_copy(i, r).wait_recv()
 
-            b = chips * i + q
-            a0, a1 = both_decays(b)
-            s0, _ = values(s_own, s_oth, b)
-            _, g1 = values(g_own, g_oth, b)
-            h0 = hl_in[i, q, 0]
-            h1 = (a0 * h0.astype(F32) + s0).astype(BF16)
-            l1 = hl_in[i, q, 1]
-            l0 = (a1 * l1.astype(F32) + g1).astype(BF16)
-            h_all[mine + b] = jnp.where(first, h0, h1)
-            h_oth[b] = jnp.where(first, h1, h0)
-            l_all[mine + b] = jnp.where(first, l0, l1)
-            l_oth[b] = jnp.where(first, l1, l0)
+            for k in range(4):
+                b = chips * i + 4 * q + k
+                a0, a1 = both_decays(b)
+                s0, _ = values(s_own, s_oth, b)
+                _, g1 = values(g_own, g_oth, b)
+                h0 = hl_in[i, q, k, 0]
+                h1 = (a0 * h0.astype(F32) + s0).astype(BF16)
+                l1 = hl_in[i, q, k, 1]
+                l0 = (a1 * l1.astype(F32) + g1).astype(BF16)
+                h_all[mine + b] = jnp.where(first, h0, h1)
+                h_oth[b] = jnp.where(first, h1, h0)
+                l_all[mine + b] = jnp.where(first, l0, l1)
+                l_oth[b] = jnp.where(first, l1, l0)
             return 0
 
-        lax.fori_loop(0, chips, finish, 0)
+        lax.fori_loop(0, 4, finish, 0)
         for copy in swap_back(i):
             copy.start()
 
@@ -504,6 +543,10 @@
         i = u // 2
         held = lax.rem(u, 2) == 0
 
+        @pl.when(u == 1)
+        def _():
+            scan(BATCHES - 1)
+
         @pl.when(held)
         def _():
             gather(i)
@@ -517,6 +560,19 @@
         return 0
 
     lax.fori_loop(0, 2 * BATCHES, outer, 0)
+
+    width = total.shape[1]
+    half = width // 2
+
+    def columns(shard, part):
+        return pl.ds(pl.multiple_of(shard * (2 * width) + part * width, 128), width)
+
+    sums = [
+        remote(taps.at[:, columns(i, 1 - core)], taps_oth.at[i], t_send.at[i], t_recv.at[i], other)
+        for i in range(shard_count)
+    ]
+    for copy in sums:
+        copy.start()
 
     closing = run_ref[ROWS - 1 : ROWS, :]
     running = run_ref[...]
@@ -535,20 +591,9 @@
     rows[1:2, :] = jnp.sum(step_grad, axis=0, keepdims=True)
     rows[2:3, :] = full_g[1:2, :]
 
-    width = total.shape[1]
-    half = width // 2
-
-    def columns(shard, part):
-        return pl.ds(pl.multiple_of(shard * (2 * width) + part * width, 128), width)
-
-    sums = [
-        remote(taps.at[:, columns(i, 1 - core)], taps_oth.at[i], t_send.at[i], t_recv.at[i], other)
-        for i in range(shard_count)
-    ]
-    sums.append(remote(rows, rows_oth, t_send.at[shard_count], t_recv.at[shard_count], other))
-    for copy in sums:
-        copy.start()
-    for copy in sums:
+    rows_sum = remote(rows, rows_oth, t_send.at[shard_count], t_recv.at[shard_count], other)
+    rows_sum.start()
+    for copy in sums + [rows_sum]:
         copy.wait()
     for i in range(shard_count):
         shards[i, :, 0:width] = taps[:, columns(i, core)] + taps_oth[i]
@@ -616,8 +661,12 @@
             def _():
                 close_copy(r).wait_send()
 
-            sg_copy(i, r).wait_send()
-            hl_copy(i, r).wait_send()
+            @pl.when(r < 4)
+            def _():
+                sg_copy(i, r).wait_send()
+                row_copy(i, r).wait_send()
+                hl_copy(i, r).wait_send()
+
             return 0
 
         lax.fori_loop(1, chips, sent, 0)
@@ -668,7 +717,7 @@
     inner = V((ROWS, INNER), BF16)
     whole = V((blocks, BLOCK_ROWS, 128), BF16)
     part = V((blocks // 2, BLOCK_ROWS, 128), BF16)
-    sent = V((BATCHES, chips, 2, BLOCK_ROWS, 128), BF16)
+    sent = V((BATCHES, 4, 4, 2, BLOCK_ROWS, 128), BF16)
     edge = V((8, CONV), F32)
     memory = pl.BlockSpec(memory_space=pltpu.VMEM)
     remote_memory = pl.BlockSpec(memory_space=pl.ANY)
@@ -681,10 +730,11 @@
         in_specs=[remote_memory] + [memory] * 7 + [remote_memory],
         out_specs=[remote_memory] + [memory] * 3,
         scratch_shapes=[
-            V((ROWS, CONV), BF16), inner, V((ROWS, CONV), BF16), plane, plane, plane, row, row, row, V((chips, 8, HEADS), F32),
-            V((HALF, 128), F32), V((HALF, 128), F32), V((chips, 128), F32), tall, tall,
+            V((ROWS, CONV), BF16), inner, V((ROWS, CONV), BF16), V((ROWS, CONV), F32), plane, plane, plane, row, row, row, V((chips, 8, HEADS), F32),
+            V((HALF, 128), F32), V((HALF, 128), F32),
+            V((BATCHES, 2, chips, 128), F32), V((BATCHES, 2, 8, 128), F32), tall, tall,
             inner, group16, group16, group32, inner, group32, plane, plane, whole, whole, part, part,
-            sent, sent, sent, sent, whole, whole, part, part, plane, plane, plane,
+            sent, sent, sent, sent, V((BATCHES, 4, 2, BLOCK_ROWS, 128), BF16), sent, whole, whole, part, part, plane, plane, plane,
             inner, inner, V((ROWS, INNER), F32), V((GROUP_LANES, 128), BF16),
             V((ROWS, GROUP_LANES), BF16), V((ROWS, GROUP_LANES), BF16), V((8, GROUP_LANES), F32), plane, plane, row,
             V((16, CONV), F32), edge, edge, edge, row,
@@ -693,7 +743,7 @@
             V((chips, 16, width // 2 + 128), BF16), V((8, width), F32), V((8, width), F32),
             dma((1,)), dma((1,)), dma((chips,)), dma((chips,)),
         ]
-        + [dma((BATCHES,))] * 4 + [dma((BATCHES, chips))] * 4 + [dma((BATCHES,))] * 4
+        + [dma((BATCHES,))] * 4 + [dma((BATCHES, 4))] * 6 + [dma((BATCHES,))] * 4
         + [dma((GROUPS, 3))] * 2 + [dma((shards + 1,))] * 2 + [dma((shards,))] * 2 + [dma((chips,))] * 2 + [dma((1,))] * 2
         + [dma((GROUPS, 4)), dma((GROUPS, 3)), dma((1,))],
         compiler_params=pltpu.CompilerParams(

time: 97.7 us -> 94.9 us (0.971)
  Pallas kernels: 88.4 us -> 85.6 us
    pallas_call x1, Pallas kernels: 85.5 us -> 82.6 us  [mixer_grads(): pl.pallas_call(mixer_kernel, out_shape=[jax.ShapeDtypeStruct((ROWS, CONV)...]
where the time goes in v5:
time: 94.9 us; the launch traced here: 94.7 us
  Pallas kernels  85.6 us (90%)
  starting transfers between devices  4.59 us (5%)
  waiting for transfers between devices  2.24 us (2%)
  local copies, waits for them, and re-layouts  1.6 us (2%)
    pallas_call x1, Pallas kernels, mixer_grads(): pl.pallas_call(mixer_kernel, out_shape=[jax.ShapeDtypeStruct((ROWS, CONV)...  82.6 us
    ppermute x1, starting transfers between devices, passed_along(): lax.ppermute(value, axis, [(source, source + steps) for source in range(i...  4.59 us
    pallas_call x1, Pallas kernels, finish(): pl.pallas_call(functools.partial(finish_kernel, factor), grid=(FINISH_PAR...  2.97 us
    ppermute x1, waiting for transfers between devices, passed_along(): lax.ppermute(value, axis, [(source, source + steps) for source in range(i...  2.24 us
  transfers between devices with their start and end apart: 1, of which 1 were waited for; matrix products, arithmetic and copies ran while one was open for 0% of the time, Pallas kernels for 0%

profile of v5, /device:TPU:1, one launch (start us, length us, event | category | flops | bytes accessed | tf_op | source)
XLA Modules:
  0.0 94.7 jit_solution(7220076928811009516)
XLA Ops:
  0.6 0.9 slice_bitcast_fusion
  1.6 4.6 %collective-permute-start = (bf16[8,10240]{1,0:T(8,128)(2,1)S(1)}, bf16[8,10240]{1,0:T(8,128)(2,1)S(1)}, u32[]{:S(2)}, u32[]{:S(2)}) collective-permute-start(bf16[8,10240]{1,0:T(8,128)(2,1)S(1)} %slice_bitcast_fusion), channel_id=1, source_target_pairs={{0,1},{1,2},{2,3},{3,4},{4,5},{5,6},{6,7},{7,8},{8,9},{9,10},{10,1... | collective-permute-start | bytes 491528 | tf_op jit(solution)/shard_map/ppermute | solution.py:792
  6.2 2.2 %collective-permute-done.halo_ref = bf16[8,10240]{1,0:T(8,128)(2,1)S(1)} collective-permute-done((bf16[8,10240]{1,0:T(8,128)(2,1)S(1)}, bf16[8,10240]{1,0:T(8,128)(2,1)S(1)}, u32[]{:S(2)}, u32[]{:S(2)}) %collective-permute-start) | collective-permute-done | bytes 163872 | tf_op jit(solution)/shard_map/ppermute | solution.py:792
  8.4 0.0 copy-start
  8.4 0.7 copy-done
  9.1 82.6 %mixer_grads.1 = (bf16[128,10240]{1,0:T(8,128)(2,1)}, f32[128,128]{1,0:T(8,128)}, f32[8,2560]{1,0:T(8,128)}, f32[8,128]{1,0:T(8,128)}) custom-call(bf16[128,10240]{1,0:T(8,128)(2,1)} %bitcast.12, bf16[8,10240]{1,0:T(8,128)(2,1)} %copy-done, f32[4,10240]{1,0:T(4,128)} %weight_ref.1, f32[1,10240]{1,0:T(1,128)} %bitcast.14, bf16[128,128]{1,0:T(8,128)(2,1)} %bitcast.15, ...), custom_call_target="tpu_custom_call" | custom-call | tf_op jit(solution)/shard_map/mixer_grads/pallas_call | solution.py:724
  91.7 3.0 %finish.1 = (bf16[128,10240]{1,0:T(8,128)(2,1)}, f32[128,128]{1,0:T(8,128)}, f32[5,2560]{1,0:T(8,128)}, f32[2,32]{1,0:T(2,128)}, f32[1,32]{1,0:T(1,128)}) custom-call(bf16[128,10240]{1,0:T(8,128)(2,1)} %get-tuple-element.14.ig_ref, f32[128,128]{1,0:T(8,128)} %get-tuple-element.15.step_ref, f32[8,2560]{1,0:T(8,128)} %get-tuple-element.16.conv_ref, ...), custom_call_target="tpu_custom_call" | custom-call | tf_op jit(solution)/shard_map/finish/pallas_call | solution.py:774
Async XLA Ops:
  1.6 6.8 %collective-permute-start = (bf16[8,10240]{1,0:T(8,128)(2,1)S(1)}, bf16[8,10240]{1,0:T(8,128)(2,1)S(1)}, u32[]{:S(2)}, u32[]{:S(2)}) collective-permute-start(bf16[8,10240]{1,0:T(8,128)(2,1)S(1)} %slice_bitcast_fusion), channel_id=1, source_target_pairs={{0,1},{1,2},{2,3},{3,4},{4,5},{5,6},{6,7},{7,8},{8,9},{9,10},{10,1... | collective-permute-start | bytes 491528 | tf_op jit(solution)/shard_map/ppermute | solution.py:792
  8.4 0.7 copy-start

commit v6 on v5

--- a/solution.py
+++ b/solution.py
@@ -68,7 +68,7 @@
     ig_hbm, step_ref, conv_ref, head_ref,
     mix_ref, dy_ref, ig_ref, slope, run_ref, run_t_ref, sp_ref, close_own, close_oth, close_out, close_in, decay_own, decay_oth, decay_in, decay_row, pad, dpad,
     xm, bm, cm, scores, dxi, dsc, sum_s, sum_r, s_own, g_own, s_oth, g_oth, sg_out, sg_in, hl_out, hl_in, row_out, row_in,
-    h_all, l_all, h_oth, l_oth, acc_b, acc_c, col_s, xc, dyg, close, ones, ent, use, row_g, full_u, full_q, full_g,
+    h_all, l_all, h_oth, l_oth, col_s, xc, dyg, close, ones, ent, use, row_g, full_u, full_q, full_g,
     last, spill, spill_in, taps, rows, taps_oth, rows_oth, shards, arrived, flat, packed, packed_in, total, total_oth,
     e_send, e_recv, k_send, k_recv, x_send, x_recv, y_send, y_recv, sg_send, sg_recv, hl_send, hl_recv, r_send, r_recv,
     p_send, p_recv, q_send, q_recv, sp_send, sp_recv, t_send, t_recv, d_send, d_recv, c_send, c_recv, o_send, o_recv,
@@ -467,8 +467,6 @@
         back = lax.rem(HEADS - GROUP_HEADS * g, HEADS)
         b16, c16 = bm[g], cm[g]
         gain = pltpu.roll(jnp.broadcast_to(gain_ref[...], (8, HEADS)), back, 1)
-        acc_b[...] = jnp.zeros(shape, F32)
-        acc_c[...] = jnp.zeros(shape, F32)
         for j in range(GROUP_PAIRS):
             lanes = tile(GROUP_LANES * g + 128 * j)
             here = pl.ds(128 * j, 128)
@@ -482,13 +480,17 @@
             use[:, here] = (x * left).astype(BF16)
             row_g[0:1, here] = jnp.sum(h16.astype(F32) * l16.astype(F32), axis=0, keepdims=True)
             row_g[1:2, here] = jnp.sum(dy * x, axis=0, keepdims=True)
-            acc_c[...] += dot_nt(dyg[:, lanes], h16)
-            acc_b[...] += dot_nt(xc[:, lanes], l16)
             grad_x = dxi[:, lanes].astype(F32) + close[:, lanes] * left + pair_of(gain, j)[0:1, :] * dy
             conv_back(j, grad_x, lanes)
         d_scores = jnp.where(iota(shape, 1) >= iota(shape, 0), dsc[g], 0.0)
-        grad_b = acc_b[...] + dot(d_scores.astype(BF16), c16)
-        grad_c = acc_c[...] + dot(d_scores.T.astype(BF16), b16)
+        channels = group_lanes(g)[0]
+
+        def side_by_side(ref):
+            ats = [pl.ds(2 * (GROUP_PAIRS * g + j), 2) for j in range(GROUP_PAIRS)]
+            return jnp.concatenate([ref[at].reshape(STATE, 128) for at in ats], axis=1)
+
+        grad_b = dot_nt(xc[:, channels], side_by_side(l_all)) + dot(d_scores.astype(BF16), c16)
+        grad_c = dot_nt(dyg[:, channels], side_by_side(h_all)) + dot(d_scores.T.astype(BF16), b16)
         for i, grad in enumerate((grad_b, grad_c)):
             lanes = tile(INNER + GROUPS * STATE * i + STATE * g)
             conv_back(GROUP_PAIRS + i, grad, lanes)
@@ -734,7 +736,7 @@
             V((HALF, 128), F32), V((HALF, 128), F32),
             V((BATCHES, 2, chips, 128), F32), V((BATCHES, 2, 8, 128), F32), tall, tall,
             inner, group16, group16, group32, inner, group32, plane, plane, whole, whole, part, part,
-            sent, sent, sent, sent, V((BATCHES, 4, 2, BLOCK_ROWS, 128), BF16), sent, whole, whole, part, part, plane, plane, plane,
+            sent, sent, sent, sent, V((BATCHES, 4, 2, BLOCK_ROWS, 128), BF16), sent, whole, whole, part, part, plane,
             inner, inner, V((ROWS, INNER), F32), V((GROUP_LANES, 128), BF16),
             V((ROWS, GROUP_LANES), BF16), V((ROWS, GROUP_LANES), BF16), V((8, GROUP_LANES), F32), plane, plane, row,
             V((16, CONV), F32), edge, edge, edge, row,

time: 94.9 us -> 94.2 us (level)
  no operation moved by 1% of the time
where the time goes in v6:
time: 94.2 us; the launch traced here: 94 us
  Pallas kernels  84.9 us (90%)
  starting transfers between devices  4.59 us (5%)
  waiting for transfers between devices  2.24 us (2%)
  local copies, waits for them, and re-layouts  1.6 us (2%)
    pallas_call x1, Pallas kernels, mixer_grads(): pl.pallas_call(mixer_kernel, out_shape=[jax.ShapeDtypeStruct((ROWS, CONV)...  82 us
    ppermute x1, starting transfers between devices, passed_along(): lax.ppermute(value, axis, [(source, source + steps) for source in range(i...  4.59 us
    pallas_call x1, Pallas kernels, finish(): pl.pallas_call(functools.partial(finish_kernel, factor), grid=(FINISH_PAR...  2.97 us
    ppermute x1, waiting for transfers between devices, passed_along(): lax.ppermute(value, axis, [(source, source + steps) for source in range(i...  2.24 us
  transfers between devices with their start and end apart: 1, of which 1 were waited for; matrix products, arithmetic and copies ran while one was open for 0% of the time, Pallas kernels for 0%

profile of v6, /device:TPU:1, one launch (start us, length us, event | category | flops | bytes accessed | tf_op | source)
XLA Modules:
  0.0 94.0 jit_solution(5526401349499062673)
XLA Ops:
  0.6 0.9 slice_bitcast_fusion
  1.6 4.6 %collective-permute-start = (bf16[8,10240]{1,0:T(8,128)(2,1)S(1)}, bf16[8,10240]{1,0:T(8,128)(2,1)S(1)}, u32[]{:S(2)}, u32[]{:S(2)}) collective-permute-start(bf16[8,10240]{1,0:T(8,128)(2,1)S(1)} %slice_bitcast_fusion), channel_id=1, source_target_pairs={{0,1},{1,2},{2,3},{3,4},{4,5},{5,6},{6,7},{7,8},{8,9},{9,10},{10,1... | collective-permute-start | bytes 491528 | tf_op jit(solution)/shard_map/ppermute | solution.py:794
  6.2 2.2 %collective-permute-done.halo_ref = bf16[8,10240]{1,0:T(8,128)(2,1)S(1)} collective-permute-done((bf16[8,10240]{1,0:T(8,128)(2,1)S(1)}, bf16[8,10240]{1,0:T(8,128)(2,1)S(1)}, u32[]{:S(2)}, u32[]{:S(2)}) %collective-permute-start) | collective-permute-done | bytes 163872 | tf_op jit(solution)/shard_map/ppermute | solution.py:794
  8.4 0.0 copy-start
  8.4 0.7 copy-done
  9.1 82.0 %mixer_grads.1 = (bf16[128,10240]{1,0:T(8,128)(2,1)}, f32[128,128]{1,0:T(8,128)}, f32[8,2560]{1,0:T(8,128)}, f32[8,128]{1,0:T(8,128)}) custom-call(bf16[128,10240]{1,0:T(8,128)(2,1)} %bitcast.12, bf16[8,10240]{1,0:T(8,128)(2,1)} %copy-done, f32[4,10240]{1,0:T(4,128)} %weight_ref.1, f32[1,10240]{1,0:T(1,128)} %bitcast.14, bf16[128,128]{1,0:T(8,128)(2,1)} %bitcast.15, ...), custom_call_target="tpu_custom_call" | custom-call | tf_op jit(solution)/shard_map/mixer_grads/pallas_call | solution.py:726
  91.0 3.0 %finish.1 = (bf16[128,10240]{1,0:T(8,128)(2,1)}, f32[128,128]{1,0:T(8,128)}, f32[5,2560]{1,0:T(8,128)}, f32[2,32]{1,0:T(2,128)}, f32[1,32]{1,0:T(1,128)}) custom-call(bf16[128,10240]{1,0:T(8,128)(2,1)} %get-tuple-element.14.ig_ref, f32[128,128]{1,0:T(8,128)} %get-tuple-element.15.step_ref, f32[8,2560]{1,0:T(8,128)} %get-tuple-element.16.conv_ref, ...), custom_call_target="tpu_custom_call" | custom-call | tf_op jit(solution)/shard_map/finish/pallas_call | solution.py:776
Async XLA Ops:
  1.6 6.8 %collective-permute-start = (bf16[8,10240]{1,0:T(8,128)(2,1)S(1)}, bf16[8,10240]{1,0:T(8,128)(2,1)S(1)}, u32[]{:S(2)}, u32[]{:S(2)}) collective-permute-start(bf16[8,10240]{1,0:T(8,128)(2,1)S(1)} %slice_bitcast_fusion), channel_id=1, source_target_pairs={{0,1},{1,2},{2,3},{3,4},{4,5},{5,6},{6,7},{7,8},{8,9},{9,10},{10,1... | collective-permute-start | bytes 491528 | tf_op jit(solution)/shard_map/ppermute | solution.py:794
  8.4 0.7 copy-start
